TPU v7x, 32 devices: a whole 2x2x4 slice. The times are simulated.
32 devices in a mesh: tm: 2 (over y), lat: 16 (over z, x, core).
Axes of the slice: x: 2, y: 2, z: 4, core: 2. Of those that a mesh axis runs over, the one named last changes fastest.
Arguments:
- background: bfloat16 [4, 2, 256, 2048], P('tm', None, 'lat'), may hold values from -12 to 12
- conv_weight: bfloat16 [32, 90], replicated, may hold values from -0.625 to 0.625
- conv_bias: float32 [32], replicated, may hold values from -3 to 3
- mix_weight: bfloat16 [32, 32], replicated, may hold values from -1 to 1
- mix_bias: float32 [32], replicated, may hold values from -3 to 3
- out_weight: bfloat16 [2, 32], replicated, may hold values from -0.1875 to 0.1875
- out_bias: float32 [2], replicated, may hold values from -0.3 to 0.3
- drift_east: float32 [256, 2048], P('lat', 'tm'), may hold values from -0.2 to 0.2
- drift_north: float32 [256, 2048], P('lat', 'tm'), may hold values from -0.2 to 0.2
- diffusivity: float32 [256, 2048], P('lat', 'tm'), may hold values from 0.1 to 0.24
- sensors: int32 [4, 16, 2, 128], P(None, 'lat', 'tm'), may hold values from 0 to 16383, as said below
- observations: float32 [4, 16, 2, 2, 128], P(None, 'lat', 'tm'), may hold values from -6 to 6
Outputs:
- total_score: float32 [4, 2, 256, 2048], P('tm', None, 'lat')
Inputs may be any that keep to these rules, and one draw needn't show every extreme that they name: `sensors`: each entry is a cell of its tile counted row by row over 16 rows of 1024 cells; cells may repeat.
All inputs are finite; a program needn't handle non-finite values.
Results may differ from a plain program's by a relative error of at most 0.0039.
Values may be sent and summed in bfloat16 or wider, within the bound.
No kernel may reach another device: no remote copies, remote signals or barrier semaphores. Data moves between devices by JAX's collectives and lax.ppermute only.
A program may use at most 128 MiB of HBM per device.

v0:
```python
import functools

import jax
import jax.numpy as jnp
import numpy as np
from jax import lax
from jax.experimental import pallas as pl
from jax.experimental.pallas import tpu as pltpu
from jax.sharding import PartitionSpec as P

KT = 5
SUB = 3
K_MID = 0.17
HALO = 2 * SUB
CROWS = 2 * SUB - 1
BF = jnp.bfloat16
F32 = jnp.float32
VMEM_BYTES = 48 * 1024 * 1024
GELU_1 = 2.0 * float(np.sqrt(2.0 / np.pi))
GELU_2 = 8.0 * 0.044715 * float(np.sqrt(2.0 / np.pi))


def dot(a, b):
    return jnp.dot(a, b, preferred_element_type=F32)


def dot_t(a, b):
    return lax.dot_general(a, b, (((1,), (1,)), ((), ())), preferred_element_type=F32)


def split2(x):
    high = x.astype(BF)
    return high, (x - high.astype(F32)).astype(BF)


def pack_table(rows, fields):
    table = np.zeros((2, 2, 96, 128), np.float32)
    coef_row = fields * rows
    for parity in range(2):
        for side in range(2):
            for message in range(4):
                far, diagonal = message % 2, message // 2
                bottom = (far == 0) == (parity == 0)
                base = 64 + 16 * far if diagonal else 32 * far
                height = 16 if diagonal else 32
                out = table[parity, side]
                if diagonal:
                    for field in range(fields):
                        out[base + field, field * rows + (rows - 1 if bottom else 0)] = 1
                else:
                    for field in range(fields):
                        for e in range(HALO):
                            row = rows - HALO + e if bottom else e
                            out[base + field * HALO + e, field * rows + row] = 1
                for slot in range(8):
                    j = side * 8 + slot
                    target = base + height - 8 + slot
                    if j < 3 * CROWS:
                        c, e = divmod(j, CROWS)
                        row = rows - CROWS + e if bottom else e
                        out[target, coef_row + c * rows + row] = 1
                    else:
                        out[target, coef_row + 3 * rows + (15 if diagonal else 14)] = 1
    return table


def near_far(case):
    parity = case in (1, 3)
    top_ok = case != 2
    bottom_ok = case not in (3, 4)
    top_slot = 0 if parity else 1
    return top_slot, 1 - top_slot, top_ok, bottom_ok


def model_tables(rows, frames, variables, quarters):
    lanes = quarters * variables
    own = np.zeros((rows * lanes, quarters * variables * rows), np.float32)
    coef = np.zeros((rows * lanes, quarters * rows), np.float32)
    out = np.zeros((lanes * rows, rows * lanes), np.float32)
    for r in range(rows):
        for q in range(quarters):
            for v in range(variables):
                own[r * lanes + q * variables + v, (q * variables + v) * rows + r] = 1
                coef[r * lanes + q * variables + v, q * rows + r] = 1
                out[(q * variables + v) * rows + r, r * lanes + q * variables + v] = 1
    halo = np.zeros((5, frames, 2 * HALO * lanes, quarters * 64), np.float32)
    chalo = np.zeros((5, 3 * 2 * CROWS * lanes, quarters * 64), np.float32)
    for case in range(5):
        top_slot, bottom_slot, top_ok, bottom_ok = near_far(case)
        for q in range(quarters):
            for v in range(variables):
                lane = q * variables + v
                for half, slot, ok in ((0, top_slot, top_ok), (1, bottom_slot, bottom_ok)):
                    if not ok:
                        continue
                    for t in range(frames):
                        for e in range(HALO):
                            local = (t * variables + v) * HALO + e
                            halo[case, t, (half * HALO + e) * lanes + lane, q * 64 + slot * 32 + local] = 1
                    for c in range(3):
                        for e in range(CROWS):
                            j = c * CROWS + e
                            column = q * 64 + slot * 32 + (j // 8) * 16 + 8 + j % 8
                            row = ((c * 2 + half) * CROWS + e) * lanes + lane
                            chalo[case, row, column] = 1.0 if c == 2 else 0.5
    return own, coef, out, halo, chalo


def conv_table(rows, frames, others, variables, group):
    channels = (frames + others) * variables
    tall = group + 2
    own_rows = frames * variables * rows
    oth_rows = others * variables * rows
    table = np.zeros((5, rows // group * tall * channels, own_rows + oth_rows + 96), np.float32)
    for case in range(5):
        top_slot, bottom_slot, top_ok, bottom_ok = near_far(case)
        for g in range(rows // group):
            for yy in range(tall):
                y = g * group + yy - 1
                for f in range(frames + others):
                    for v in range(variables):
                        target = (g * tall + yy) * channels + f * variables + v
                        own = f < frames
                        field = (f if own else f - frames) * variables + v
                        if 0 <= y < rows:
                            table[case, target, (0 if own else own_rows) + field * rows + y] = 1
                            continue
                        slot, ok = (top_slot, top_ok) if y < 0 else (bottom_slot, bottom_ok)
                        if not ok:
                            continue
                        if own:
                            column = own_rows + oth_rows + slot * 32
                            column += field * HALO + (HALO - 1 if y < 0 else 0)
                        else:
                            column = own_rows + oth_rows + 64 + slot * 16 + field
                        table[case, target, column] = 1
    return table


def tap_table(offsets, frames, variables, group, depth):
    channels = len(offsets) * variables
    tall = group + 2
    table = np.full((frames * group, depth), -1, np.int32)
    for t in range(frames):
        for y in range(group):
            for s in range(3):
                for yy in range(tall):
                    for f, offset in enumerate(offsets):
                        for v in range(variables):
                            lag, i = offset - t + KT // 2, yy - y
                            if 0 <= lag < KT and 0 <= i < 3:
                                k = s * tall * channels + yy * channels + f * variables + v
                                table[t * group + y, k] = ((v * KT + lag) * 3 + i) * 3 + s
            for part in range(3):
                table[t * group + y, 3 * tall * channels + part] = 3 * 3 * KT * variables + part
    return table


def case_of(parity, index, count):
    return jnp.where(index == 0, 2, jnp.where(index == count - 1, jnp.where(parity == 1, 3, 4), parity))


def pack_kernel(bg, east, north, diff, sensors, obs, table, p0, near, far, dnear, dfar, *, frames):
    me_t = lax.axis_index("tm")
    parity = lax.axis_index("lat") % 2
    fields = bg.shape[0] * bg.shape[1]
    rows, lon = bg.shape[2], bg.shape[3]
    half = lon // 2
    fields_2d = bg[...].reshape(fields * rows, lon)
    a, b = east[...].astype(BF), north[...].astype(BF)
    k = (diff[...] - K_MID).astype(BF)

    def described(first, low):
        pieces = []
        for t in range(frames):
            cells = sensors[first + t, 0]
            if not low:
                pieces += [(cells >> 8).astype(F32), (cells & 255).astype(F32)]
            for v in range(obs.shape[3]):
                value = obs[first + t, 0, 0, v : v + 1]
                high = value.astype(BF).astype(F32)
                pieces.append(value - high if low else high)
        row = jnp.concatenate(pieces, axis=1)
        if row.shape[1] < half:
            row = jnp.concatenate([row, jnp.zeros((1, half - row.shape[1]), F32)], axis=1)
        return row

    mine, theirs = me_t * frames, (1 - me_t) * frames
    extra = jnp.concatenate(
        [
            jnp.zeros((12, half), F32),
            described(mine, True),
            described(theirs, True),
            described(mine, False),
            described(theirs, False),
        ],
        axis=0,
    ).astype(BF)
    split = fields * rows
    p0[0:split, :] = fields_2d
    p0[split : split + rows, 0:half] = a
    p0[split + rows : split + 2 * rows, 0:half] = b
    p0[split : split + rows, half:lon] = k
    p0[split + rows : split + 2 * rows, half:lon] = extra
    for side in range(2):
        cut = slice(side * half, (side + 1) * half)
        source = jnp.concatenate([fields_2d[:, cut], a, b, k, extra], axis=0)
        message = dot(table[parity, side], source).astype(BF)
        near[:, cut] = message[0:32]
        far[:, cut] = message[32:64]
        dnear[:, cut] = message[64:80]
        dfar[:, cut] = message[80:96]


def prep_kernel(conv_w, conv_b, mix_w, mix_b, out_w, out_b, taps, w1, w2, w3, b2, b3, *, group, i_of):
    hid = mix_w.shape[0]
    table = taps[i_of()]

    def column(row):
        n = row.shape[1]
        here = lax.broadcasted_iota(jnp.int32, (n, n), 0) == lax.broadcasted_iota(jnp.int32, (n, n), 1)
        return jnp.sum(jnp.where(here, jnp.broadcast_to(row, (n, n)), 0.0), axis=1, keepdims=True)

    bias = 0.5 * column(conv_b[...])
    pieces = []
    for _ in range(3):
        piece = bias.astype(BF)
        bias = bias - piece.astype(F32)
        pieces.append(piece.astype(F32))
    ntap = conv_w.shape[1]
    padded = 128
    weights = jnp.concatenate(
        [0.5 * conv_w[...].astype(F32)] + pieces + [jnp.zeros((hid, padded - ntap - 3), F32)], axis=1
    ).astype(BF)
    tap_id = lax.broadcasted_iota(jnp.int32, (padded, table.shape[1]), 0)
    for ty in range(table.shape[0]):
        chosen = jnp.where(tap_id == table[ty : ty + 1, :], 1.0, 0.0).astype(BF)
        w1[ty * hid : (ty + 1) * hid, :] = dot(weights, chosen).astype(BF)
    tall = group * hid
    row = lax.broadcasted_iota(jnp.int32, (tall, hid), 0) & (hid - 1)
    up = jnp.where(row == lax.broadcasted_iota(jnp.int32, (tall, hid), 1), 1.0, 0.0).astype(BF)
    mixed = dot_t(dot(up, (0.5 * mix_w[...].astype(F32)).astype(BF)).astype(BF), up)
    shift = hid.bit_length() - 1
    rows2 = lax.broadcasted_iota(jnp.int32, (tall, tall), 0) >> shift
    cols2 = lax.broadcasted_iota(jnp.int32, (tall, tall), 1) >> shift
    w2[...] = jnp.where(rows2 == cols2, mixed, 0.0).astype(BF)
    variables = out_w.shape[0]
    spread = dot_t(out_w[...], up)
    parts, parts_b = [], []
    for v in range(variables):
        here = lax.broadcasted_iota(jnp.int32, (group, tall), 0) == (
            lax.broadcasted_iota(jnp.int32, (group, tall), 1) >> shift
        )
        parts.append(jnp.where(here, jnp.broadcast_to(spread[v : v + 1], (group, tall)), 0.0))
        parts_b.append(jnp.broadcast_to(out_b[:, v : v + 1], (group, 128)))
    w3[...] = jnp.concatenate(parts, axis=0).astype(BF)
    b3[...] = jnp.concatenate(parts_b, axis=0)
    mixed_bias = jnp.broadcast_to(0.5 * column(mix_b[...]), (hid, 128))
    b2[...] = jnp.concatenate([mixed_bias] * group, axis=0)


def model_kernel(
    p0, r0, near, far, dnear, dfar, *rest,
    rows, frames, variables, own_bg, oth_bg, tile_cols, n_sens, paired, i_of, parity_of,
):
    sens = None if paired else rest[0]
    p_own, p_coef, p_out, p_halo, p_chalo, out, field_a, field_b, coefs = rest[-9:]
    lon = p0.shape[1]
    half = lon // 2
    quarters = 8 // variables
    width = half // quarters
    me_l, count = lax.axis_index("lat"), lax.axis_size("lat")
    parity = parity_of()
    me_t = i_of()
    case = case_of(parity, me_l, count)
    top_ok, bottom_ok = me_l > 0, me_l < count - 1
    tall = rows + 2 * HALO

    for t in range(frames):
        for h in range(2):
            g = t * 2 + h
            body, rim = [], []
            for q in range(quarters):
                cut = slice(h * half + q * width, h * half + (q + 1) * width)
                body.append(p0[t * variables * rows : (t + 1) * variables * rows, cut])
                rim += [near[:, cut], far[:, cut]]
            field_a[g, HALO : HALO + rows] = dot(p_own[...], jnp.concatenate(body, axis=0)).reshape(rows, 8, width)
            edges = dot(p_halo[case, t], jnp.concatenate(rim, axis=0)).reshape(2 * HALO, 8, width)
            field_a[g, 0:HALO] = edges[0:HALO]
            field_a[g, HALO + rows : tall] = edges[HALO:]

    ctall = rows + 2 * CROWS
    for source in range(2):
        big, at = (p0, own_bg) if source == 0 else (r0, oth_bg)
        spot = me_t if source == 0 else 1 - me_t
        m_near, m_far = (near, far) if source == 0 else (dnear, dfar)
        last = m_near.shape[0]
        pieces = []
        for side in range(2):
            for c_row in range(2):
                stack = []
                for q in range(quarters):
                    cut = slice(side * half + q * width, side * half + (q + 1) * width)
                    stack.append(big[at + c_row * rows : at + (c_row + 1) * rows, cut])
                pieces.append(jnp.concatenate(stack, axis=0))
        scaled = p_coef[...]
        ha = (0.5 * dot(scaled, pieces[0])).reshape(rows, 8, width)
        hb = (0.5 * dot(scaled, pieces[1])).reshape(rows, 8, width)
        kk = dot(scaled, pieces[2]).reshape(rows, 8, width) + K_MID
        rim = []
        for q in range(quarters):
            for message in (m_near, m_far):
                for side in range(2):
                    cut = slice(side * half + q * width, side * half + (q + 1) * width)
                    rim.append(message[last - 16 : last, cut])
        edges = dot(p_chalo[case], jnp.concatenate(rim, axis=0)).reshape(3, 2, CROWS, 8, width)
        k_top = edges[2, 0] + jnp.where(top_ok, K_MID, 0.0)
        k_bottom = edges[2, 1] + jnp.where(bottom_ok, K_MID, 0.0)
        for start, size, xa, xb, xk in (
            (0, CROWS, edges[0, 0], edges[1, 0], k_top),
            (CROWS, rows, ha, hb, kk),
            (CROWS + rows, CROWS, edges[0, 1], edges[1, 1], k_bottom),
        ):
            span = slice(start, start + size)
            coefs[spot, 0, span] = xk - xa
            coefs[spot, 1, span] = xk + xa
            coefs[spot, 2, span] = xk - xb
            coefs[spot, 3, span] = xk + xb
            coefs[spot, 4, span] = 1.0 - 4.0 * xk

    lane = lax.broadcasted_iota(jnp.int32, (8, 128), 1)
    sub_q = lax.broadcasted_iota(jnp.int32, (8, 128), 0) >> (variables.bit_length() - 1)
    first_lane, last_lane = lane == 0, lane == 127
    first_q, last_q = sub_q == 0, sub_q == quarters - 1
    tiles = width // 128

    def cut_tiles(x):
        return [x[:, n * 128 : (n + 1) * 128] for n in range(tiles)]

    def from_west(x0, x1):
        both = [[pltpu.roll(part, 1, 1) for part in cut_tiles(x)] for x in (x0, x1)]
        result = []
        for h in range(2):
            wrapped = jnp.where(last_q, both[1 - h][-1], both[h][-1])
            carry = pltpu.roll(wrapped, variables, 0)
            parts = []
            for n in range(tiles):
                parts.append(jnp.where(first_lane, carry if n == 0 else both[h][n - 1], both[h][n]))
            result.append(jnp.concatenate(parts, axis=1))
        return result

    def from_east(x0, x1):
        both = [[pltpu.roll(part, 127, 1) for part in cut_tiles(x)] for x in (x0, x1)]
        result = []
        for h in range(2):
            wrapped = jnp.where(first_q, both[1 - h][0], both[h][0])
            carry = pltpu.roll(wrapped, 8 - variables, 0)
            parts = []
            for n in range(tiles):
                parts.append(
                    jnp.where(last_lane, carry if n == tiles - 1 else both[h][n + 1], both[h][n])
                )
            result.append(jnp.concatenate(parts, axis=1))
        return result

    def forward(source, target, low, high):
        def row_step(r, _):
            cr = r - (HALO - CROWS)
            for t in range(frames):
                center = [source[t * 2 + h, r] for h in range(2)]
                west, east = from_west(*center), from_east(*center)
                for h in range(2):
                    g = t * 2 + h
                    target[g, r] = (
                        (coefs[h, 4, cr] * center[h] + coefs[h, 0, cr] * east[h])
                        + (coefs[h, 1, cr] * west[h] + coefs[h, 2, cr] * source[g, r + 1])
                        + coefs[h, 3, cr] * source[g, r - 1]
                    )
            return 0

        lax.fori_loop(low, high, row_step, 0, unroll=2)

    def backward(source, target, low, high):
        def row_step(r, _):
            cr = r - (HALO - CROWS)
            for t in range(frames):
                center = [source[t * 2 + h, r] for h in range(2)]
                west = from_west(*[coefs[h, 0, cr] * center[h] for h in range(2)])
                east = from_east(*[coefs[h, 1, cr] * center[h] for h in range(2)])
                for h in range(2):
                    g = t * 2 + h
                    target[g, r] = (
                        (coefs[h, 4, cr] * center[h] + west[h])
                        + (east[h] + coefs[h, 2, cr - 1] * source[g, r - 1])
                        + coefs[h, 3, cr + 1] * source[g, r + 1]
                    )
            return 0

        lax.fori_loop(low, high, row_step, 0, unroll=2)

    buffers = [field_a, field_b]
    for step in range(SUB):
        forward(buffers[step % 2], buffers[(step + 1) % 2], step + 1, tall - step - 1)
    forecast, spread = buffers[SUB % 2], buffers[(SUB + 1) % 2]

    def kinds(row, t):
        base = t * (2 + variables) * n_sens
        return [row[:, base + n * n_sens : base + (n + 1) * n_sens] for n in range(2 + variables)]

    def sensor_rows(h, band):
        if not paired:
            count = sens.shape[0] // 8
            first = (h * 4 + band) * count
            return [sens[...].astype(F32)[first + n : first + n + 1] for n in range(count)]
        if band in (1, 3):
            at = slice(own_bg + rows, own_bg + rows + 16)
            mine, other = p0[at, half:lon].astype(F32), r0[at, half:lon].astype(F32)
            n = 14 if band == 1 else 12
            return [jnp.where(me_t == h, mine[n : n + 1], other[n + 1 : n + 2])]
        from_far = parity == (0 if band == 0 else 1)
        found = []
        for x, y in ((near, far), (dnear, dfar)):
            last = x.shape[0]
            pair = [m[last - 16 : last, half:lon].astype(F32)[15:16] for m in (x, y)]
            found.append(jnp.where(from_far, pair[1], pair[0]))
        return [jnp.where(me_t == h, found[0], found[1])]

    row_bits = tile_cols.bit_length() - 1
    width_bits = width.bit_length() - 1

    def located(h, band, t):
        found = []
        for n, row in enumerate(sensor_rows(h, band)):
            high, low, *values = kinds(row, t)
            cell = (high * 256.0 + low).astype(jnp.int32)
            column = (cell & (tile_cols - 1)) + n * tile_cols
            found.append([cell >> row_bits, column >> width_bits, column & (width - 1)] + list(values))
        if band == 1:
            for n, row in enumerate(sensor_rows(h, 3)):
                for v in range(variables):
                    found[n][3 + v] = found[n][3 + v] + row[:, (t * variables + v) * n_sens : (t * variables + v + 1) * n_sens]
        return [jnp.concatenate([f[n] for f in found], axis=1) for n in range(3 + variables)]

    def assimilate(g, row_list, where_row, quarter, lane_of, values):
        total = where_row.shape[1]
        onehot = jnp.where(
            lax.broadcasted_iota(jnp.int32, (width, total), 0) == lane_of, 1.0, 0.0
        ).astype(BF)
        stack = jnp.concatenate([forecast[g, HALO + r] for r in row_list], axis=0)
        high, low = split2(stack)
        picked = dot(high, onehot) + dot(low, onehot)
        shape = (8, total)
        here_q = (lax.broadcasted_iota(jnp.int32, shape, 0) >> (variables.bit_length() - 1)) == quarter
        variable = lax.broadcasted_iota(jnp.int32, shape, 0) & (variables - 1)
        misfit = jnp.zeros(shape, F32)
        for n, r in enumerate(row_list):
            misfit = misfit + jnp.where(where_row == r, picked[n * 8 : (n + 1) * 8], 0.0)
        target = jnp.broadcast_to(values[0], shape)
        for v in range(1, variables):
            target = jnp.where(variable == v, values[v], target)
        misfit = jnp.where(here_q, misfit - target, 0.0)
        weighted = jnp.concatenate([jnp.where(where_row == r, misfit, 0.0) for r in row_list], axis=0)
        high, low = split2(weighted)
        return (dot_t(high, onehot) + dot_t(low, onehot)).reshape(len(row_list), 8, width)

    far_away = -(1 << 20)
    for t in range(frames):
        for h in range(2):
            g = t * 2 + h
            row, quarter, lane_of, *values = located(h, 1, t)
            spread[g, HALO : HALO + rows] = assimilate(g, list(range(rows)), row, quarter, lane_of, values)
            above, below = located(h, 0, t), located(h, 2, t)
            above[0] = jnp.where(top_ok, above[0] - rows, far_away)
            below[0] = jnp.where(bottom_ok, below[0] + rows, far_away)
            merged = [jnp.concatenate([x, y], axis=1) for x, y in zip(above, below)]
            rim_rows = list(range(-SUB, 0)) + list(range(rows, rows + SUB))
            rim = assimilate(g, rim_rows, merged[0], merged[1], merged[2], merged[3:])
            spread[g, HALO - SUB : HALO] = rim[0:SUB]
            spread[g, HALO + rows : HALO + rows + SUB] = rim[SUB:]

    buffers = [spread, forecast]
    for step in range(SUB):
        low = HALO - SUB + step + 1
        backward(buffers[step % 2], buffers[(step + 1) % 2], low, tall - low)
    result = buffers[SUB % 2]

    for t in range(frames):
        for h in range(2):
            high, low = split2(result[t * 2 + h, HALO : HALO + rows].reshape(rows * 8, width))
            back = dot(p_out[...], high) + dot(p_out[...], low)
            for q in range(quarters):
                cut = slice(h * half + q * width, h * half + (q + 1) * width)
                for v in range(variables):
                    base = (q * variables + v) * rows
                    out[t, v, :, cut] = back[base : base + rows]


def conv_kernel(
    p0, r0, near, far, dnear, dfar, adjoint, table, w1, w2, w3, b2, b3, out, window,
    *, rows, frames, variables, own_bg, oth_bg, group, chunk, parity_of,
):
    lon = p0.shape[1]
    me_l, count = lax.axis_index("lat"), lax.axis_size("lat")
    case = case_of(parity_of(), me_l, count)
    groups = rows // group
    tall = table.shape[1] // groups
    depth = window.shape[1]
    stack = jnp.concatenate(
        [p0[0:own_bg], r0[0:oth_bg], near[...], far[...], dnear[...], dfar[...]], axis=0
    )
    chosen = dot(table[case], stack)
    for g in range(groups):
        center = chosen[g * tall : (g + 1) * tall]
        window[g, 0:tall] = pltpu.roll(center, 1, 1).astype(BF)
        window[g, tall : 2 * tall] = center.astype(BF)
        window[g, 2 * tall : 3 * tall] = pltpu.roll(center, lon - 1, 1).astype(BF)
        left = depth - 3 * tall
        ones = lax.broadcasted_iota(jnp.int32, (left, lon), 0) < 3
        window[g, 3 * tall : depth] = jnp.where(ones, 1.0, 0.0).astype(BF)

    def gelu(y):
        inner = y * (GELU_1 + GELU_2 * (y * y))
        return (y + y * jnp.tanh(inner)).astype(BF)

    hidden = w2.shape[0]
    bias2 = jnp.concatenate([b2[...]] * (chunk // 128), axis=1)
    bias3 = jnp.concatenate([b3[...]] * (chunk // 128), axis=1)

    def columns(n, _):
        cut = pl.ds(pl.multiple_of(n * chunk, chunk), chunk)
        for g in range(groups):
            taps = window[g, :, cut]
            for t in range(frames):
                one = gelu(dot(w1[t * hidden : (t + 1) * hidden], taps))
                two = gelu(dot(w2[...], one) + bias2)
                score = dot(w3[...], two) + bias3
                for v in range(variables):
                    span = slice(g * group, (g + 1) * group)
                    out[t, v, span, cut] = score[v * group : (v + 1) * group] - adjoint[t, v, span, cut]
        return 0

    lax.fori_loop(0, lon // chunk, columns, 0)


def call(body, out_shape, scratch, *args):
    whole = pl.BlockSpec(memory_space=pltpu.VMEM)
    several = isinstance(out_shape, (list, tuple))
    return pl.pallas_call(
        body,
        out_shape=out_shape,
        in_specs=[whole] * len(args),
        out_specs=[whole] * len(out_shape) if several else whole,
        scratch_shapes=scratch,
        compiler_params=pltpu.CompilerParams(vmem_limit_bytes=VMEM_BYTES),
    )(*args)


def struct(shape, dtype):
    return jax.ShapeDtypeStruct(shape, dtype)


def swap_pairs(tiles, bands):
    def at(t, j):
        return t * bands + j

    def far(j):
        return j + 1 if j % 2 else j - 1

    cells = [(t, j) for t in range(tiles) for j in range(bands)]
    inner = lambda j: 0 <= far(j) < bands
    return (
        [(at(t, j), at(1 - t, j)) for t, j in cells],
        [(at(t, j), at(t, j ^ 1)) for t, j in cells],
        [(at(t, j), at(t, far(j)) if inner(j) else at(1 - t, j)) for t, j in cells],
        [(at(t, j), at(1 - t, j ^ 1)) for t, j in cells],
        [(at(t, j), at(1 - t, far(j)) if inner(j) else at(1 - t, j)) for t, j in cells],
    )


def exchange_pairs(background, east, north, diff, sensors, observations):
    frames, variables, rows, lon = background.shape
    fields = frames * variables
    bands = lax.axis_size("lat")
    table = jnp.asarray(pack_table(rows, fields), BF)
    big = struct((fields * rows + 2 * rows, lon), BF)
    lat_message, diagonal = struct((32, lon), BF), struct((16, lon), BF)
    with jax.named_scope("pack"):
        p0, near, far, dnear, dfar = call(
            functools.partial(pack_kernel, frames=frames),
            [big, lat_message, lat_message, diagonal, diagonal],
            [],
            background, east, north, diff, sensors, observations, table,
        )
    axes = ("tm", "lat")
    across, on_chip, next_chip, diag_near, diag_far = swap_pairs(lax.axis_size("tm"), bands)
    r0 = lax.ppermute(p0, axes, across)
    r_dfar = lax.ppermute(dfar, axes, diag_far)
    r_far = lax.ppermute(far, axes, next_chip)
    r_dnear = lax.ppermute(dnear, axes, diag_near)
    r_near = lax.ppermute(near, axes, on_chip)
    return p0, r0, r_near, r_far, r_dnear, r_dfar


def exchange_gathered(background, east, north, diff, sensors, observations):
    frames, variables, rows, lon = background.shape
    fields = frames * variables
    half = lon // 2
    tiles, bands = lax.axis_size("tm"), lax.axis_size("lat")
    down = [(j, j + 1) for j in range(bands - 1)]
    up = [(j + 1, j) for j in range(bands - 1)]
    later = [(t, t + 1) for t in range(tiles - 1)]
    earlier = [(t + 1, t) for t in range(tiles - 1)]
    coefs = jnp.stack([east, north, diff - K_MID]).astype(BF)
    coefs = lax.all_gather(coefs, "tm", axis=2, tiled=True)
    around = jnp.concatenate(
        [lax.ppermute(background, "tm", later), lax.ppermute(background, "tm", earlier)], axis=0
    )
    cells = lax.all_to_all(sensors, "tm", split_axis=0, concat_axis=2, tiled=True)[:, 0]
    obs = lax.all_to_all(observations, "tm", split_axis=0, concat_axis=2, tiled=True)[:, 0]
    cells = jnp.moveaxis(cells, 1, 0)
    obs = jnp.transpose(obs, (1, 0, 2, 3))
    obs_high = obs.astype(BF).astype(F32)
    digits = jnp.stack([(cells >> 8).astype(F32), (cells & 255).astype(F32)], axis=2)
    described = jnp.concatenate([digits, obs_high], axis=2).reshape(tiles, -1).astype(BF)
    low = (obs - obs_high).astype(BF).reshape(tiles, -1)
    low = jnp.pad(low, ((0, 0), (0, described.shape[1] - low.shape[1])))
    bands_of = [
        lax.ppermute(described, "lat", down), described, lax.ppermute(described, "lat", up), low
    ]
    sens = jnp.stack([x.reshape(2, tiles // 2, -1) for x in bands_of], axis=1)
    sens = sens.reshape(-1, described.shape[1])

    def block(fields_3d, h):
        part = coefs[:, :, h * half : (h + 1) * half]
        blank = jnp.zeros_like(part[0])
        return jnp.concatenate(
            [
                fields_3d.reshape(-1, lon),
                jnp.concatenate([part[0], part[2]], axis=1),
                jnp.concatenate([part[1], blank], axis=1),
            ],
            axis=0,
        )

    def message(fields_4d, depth, h, bottom, height):
        height_rows = fields_4d.shape[2]
        edge = fields_4d[:, :, height_rows - depth :] if bottom else fields_4d[:, :, :depth]
        edge = edge.reshape(-1, lon)
        part = coefs[:, :, h * half : (h + 1) * half]
        part = part[:, rows - CROWS :] if bottom else part[:, :CROWS]
        part = jnp.pad(part.reshape(3 * CROWS, half), ((0, 16 - 3 * CROWS), (0, 0)))
        part = jnp.concatenate([part[:8], part[8:]], axis=1)
        blank = jnp.zeros((height - 8 - edge.shape[0], lon), BF)
        return jnp.concatenate([edge, blank, part], axis=0)

    p0, r0 = block(background, 0), block(around, 1)
    near = lax.ppermute(message(background, HALO, 0, False, 32), "lat", up)
    far = lax.ppermute(message(background, HALO, 0, True, 32), "lat", down)
    dnear = lax.ppermute(message(around, 1, 1, False, 16), "lat", up)
    dfar = lax.ppermute(message(around, 1, 1, True, 16), "lat", down)
    return p0, r0, near, far, dnear, dfar, sens


def shards(
    background, conv_weight, conv_bias, mix_weight, mix_bias, out_weight, out_bias,
    drift_east, drift_north, diffusivity, sensors, observations,
):
    frames, variables, rows, lon = background.shape
    tiles, bands = lax.axis_size("tm"), lax.axis_size("lat")
    paired = tiles == 2 and bands % 2 == 0
    group = 8
    hid = mix_weight.shape[0]
    fields = frames * variables
    arrays = (background, drift_east, drift_north, diffusivity, sensors, observations)
    if paired:
        received, sens = exchange_pairs(*arrays), ()
        offsets = [[*range(2 * frames)], [*range(frames), *range(-frames, 0)]]
        i_of = lambda: lax.axis_index("tm")
        parity_of = lambda: lax.axis_index("lat") % 2
    else:
        *received, sens = exchange_gathered(*arrays)
        sens = (sens,)
        offsets = [[*range(frames), *range(-frames, 0), *range(frames, 2 * frames)]]
        i_of = lambda: 0
        parity_of = lambda: 0
    others = len(offsets[0]) - frames
    own_bg, oth_bg = fields * rows, others * variables * rows

    need = 3 * (group + 2) * (frames + others) * variables + 3
    depth = -(-need // 128) * 128
    taps = jnp.asarray(np.stack([tap_table(o, frames, variables, group, depth) for o in offsets]))
    with jax.named_scope("weights"):
        weights = call(
            functools.partial(prep_kernel, group=group, i_of=i_of),
            [
                struct((frames * group * hid, depth), BF),
                struct((group * hid, group * hid), BF),
                struct((variables * group, group * hid), BF),
                struct((group * hid, 128), F32),
                struct((variables * group, 128), F32),
            ],
            [],
            conv_weight, conv_bias.reshape(1, -1), mix_weight, mix_bias.reshape(1, -1),
            out_weight, out_bias.reshape(1, -1), taps,
        )
    quarters = 8 // variables
    width = lon // 8
    tables = [jnp.asarray(x, BF) for x in model_tables(rows, frames, variables, quarters)]
    tall, ctall = rows + 2 * HALO, rows + 2 * CROWS
    with jax.named_scope("model"):
        adjoint = call(
            functools.partial(
                model_kernel, rows=rows, frames=frames, variables=variables, own_bg=own_bg,
                oth_bg=oth_bg, tile_cols=drift_east.shape[1], n_sens=sensors.shape[3],
                paired=paired, i_of=i_of, parity_of=parity_of,
            ),
            struct(background.shape, F32),
            [
                pltpu.VMEM((2 * frames, tall, 8, width), F32),
                pltpu.VMEM((2 * frames, tall, 8, width), F32),
                pltpu.VMEM((2, 5, ctall, 8, width), F32),
            ],
            *received, *sens, *tables,
        )
    table = jnp.asarray(conv_table(rows, frames, others, variables, group), BF)
    with jax.named_scope("prior"):
        return call(
            functools.partial(
                conv_kernel, rows=rows, frames=frames, variables=variables, own_bg=own_bg,
                oth_bg=oth_bg, group=group, chunk=256, parity_of=parity_of,
            ),
            struct(background.shape, F32),
            [pltpu.VMEM((rows // group, depth, lon), BF)],
            *received, adjoint, table, *weights,
        )


def solution(mesh):
    placed = (
        P("tm", None, "lat", None),
        P(),
        P(),
        P(),
        P(),
        P(),
        P(),
        P("lat", "tm"),
        P("lat", "tm"),
        P("lat", "tm"),
        P(None, "lat", "tm", None),
        P(None, "lat", "tm", None, None),
    )
    return jax.shard_map(
        shards, mesh=mesh, in_specs=placed, out_specs=P("tm", None, "lat", None), check_vma=False
    )
```

profile of v0, /device:TPU:0, one launch (start us, length us, event | category | flops | bytes accessed | tf_op | source)
XLA Modules:
  0.0 47.1 jit_solution(4448758514619128877)
XLA Ops:
  0.0 1.0 %copy-done.3 = bf16[2,2,16,2048]{3,2,1,0:T(8,128)(2,1)S(1)} copy-done((bf16[2,2,16,2048]{3,2,1,0:T(8,128)(2,1)S(1)}, bf16[2,2,16,2048]{3,2,1,0:T(8,128)(2,1)}, u32[]{:S(2)}) %copy-start.3) | copy-done | bytes 262168
  1.0 0.9 %copy-done.4 = bf16[2,2,96,128]{3,2,1,0:T(8,128)(2,1)S(1)} copy-done((bf16[2,2,96,128]{3,2,1,0:T(8,128)(2,1)S(1)}, bf16[2,2,96,128]{3,2,1,0:T(8,128)(2,1)}, u32[]{:S(2)}) %copy-start.4) | copy-done | bytes 98328
  1.9 0.8 %copy-done.5 = f32[16,1024]{1,0:T(8,128)S(1)} copy-done((f32[16,1024]{1,0:T(8,128)S(1)}, f32[16,1024]{1,0:T(8,128)}, u32[]{:S(2)}) %copy-start.5) | copy-done | bytes 65560
  2.8 0.8 %copy-done.6 = f32[16,1024]{1,0:T(8,128)S(1)} copy-done((f32[16,1024]{1,0:T(8,128)S(1)}, f32[16,1024]{1,0:T(8,128)}, u32[]{:S(2)}) %copy-start.6) | copy-done | bytes 65560
  3.6 0.8 %copy-done.7 = f32[16,1024]{1,0:T(8,128)S(1)} copy-done((f32[16,1024]{1,0:T(8,128)S(1)}, f32[16,1024]{1,0:T(8,128)}, u32[]{:S(2)}) %copy-start.7) | copy-done | bytes 65560
  4.4 0.7 %copy-done.14 = f32[4,1,1,2,128]{4,3,2,1,0:T(2,128)S(1)} copy-done((f32[4,1,1,2,128]{4,3,2,1,0:T(2,128)S(1)}, f32[4,1,1,2,128]{4,3,2,1,0:T(2,128)}, u32[]{:S(2)}) %copy-start.14) | copy-done | bytes 4120
  5.1 0.7 %copy-done.15 = s32[4,1,1,128]{3,2,1,0:T(1,128)S(1)} copy-done((s32[4,1,1,128]{3,2,1,0:T(1,128)S(1)}, s32[4,1,1,128]{3,2,1,0:T(1,128)}, u32[]{:S(2)}) %copy-start.15) | copy-done | bytes 2072
  5.8 0.3 pack.1
  6.1 3.0 %collective-permute-start = (bf16[96,2048]{1,0:T(8,128)(2,1)S(1)}, bf16[96,2048]{1,0:T(8,128)(2,1)S(1)}, u32[]{:S(2)}, u32[]{:S(2)}) collective-permute-start(bf16[96,2048]{1,0:T(8,128)(2,1)S(1)} %get-tuple-element.15.p0), channel_id=1, source_target_pairs={{0,16},{1,17},{2,18},{3,19},{4,20},{5,21},{6,22},{7,23},{8,24},{9,... | collective-permute-start | bytes 1179656 | tf_op jit(solution)/shard_map/ppermute | solution.py:596
  9.1 0.2 collective-permute-start.2
  9.3 1.6 %collective-permute-start.3 = (bf16[16,2048]{1,0:T(8,128)(2,1)S(1)}, bf16[16,2048]{1,0:T(8,128)(2,1)S(1)}, u32[]{:S(2)}, u32[]{:S(2)}) collective-permute-start(bf16[16,2048]{1,0:T(8,128)(2,1)S(1)} %get-tuple-element.18), channel_id=1, source_target_pairs={{0,17},{1,16},{2,19},{3,18},{4,21},{5,20},{6,23},{7,22},{8,25},{9,... | collective-permute-start | bytes 196616 | tf_op jit(solution)/shard_map/ppermute | solution.py:599
  10.8 1.5 %collective-permute-start.4 = (bf16[16,2048]{1,0:T(8,128)(2,1)S(1)}, bf16[16,2048]{1,0:T(8,128)(2,1)S(1)}, u32[]{:S(2)}, u32[]{:S(2)}) collective-permute-start(bf16[16,2048]{1,0:T(8,128)(2,1)S(1)} %get-tuple-element.19), channel_id=1, source_target_pairs={{0,16},{1,18},{2,17},{3,20},{4,19},{5,22},{6,21},{7,24},{8,23},{9,... | collective-permute-start | bytes 196616 | tf_op jit(solution)/shard_map/ppermute | solution.py:597
  12.4 0.8 %copy-done.11 = s32[2,16,256]{2,1,0:T(8,128)S(1)} copy-done((s32[2,16,256]{2,1,0:T(8,128)S(1)}, s32[2,16,256]{2,1,0:T(8,128)}, u32[]{:S(2)}) %copy-start.11) | copy-done | bytes 32792
  13.1 0.7 %copy-done.12 = bf16[32,90]{1,0:T(8,128)(2,1)S(1)} copy-done((bf16[32,90]{1,0:T(8,128)(2,1)S(1)}, bf16[32,90]{1,0:T(8,128)(2,1)}, u32[]{:S(2)}) %copy-start.12) | copy-done | bytes 5784
  13.8 0.7 %copy-done.13 = bf16[32,32]{1,0:T(8,128)(2,1)S(1)} copy-done((bf16[32,32]{1,0:T(8,128)(2,1)S(1)}, bf16[32,32]{1,0:T(8,128)(2,1)}, u32[]{:S(2)}) %copy-start.13) | copy-done | bytes 2072
  14.5 0.7 %copy-done.16 = f32[32]{0:T(128)S(1)} copy-done((f32[32]{0:T(128)S(1)}, f32[32]{0:T(128)}, u32[]{:S(2)}) %copy-start.16) | copy-done | bytes 152
  15.2 0.7 %copy-done.17 = f32[32]{0:T(128)S(1)} copy-done((f32[32]{0:T(128)S(1)}, f32[32]{0:T(128)}, u32[]{:S(2)}) %copy-start.17) | copy-done | bytes 152
  15.8 0.7 %copy-done.18 = bf16[2,32]{1,0:T(2,128)(2,1)S(1)} copy-done((bf16[2,32]{1,0:T(2,128)(2,1)S(1)}, bf16[2,32]{1,0:T(2,128)(2,1)}, u32[]{:S(2)}) %copy-start.18) | copy-done | bytes 152
  16.5 0.7 %copy-done.19 = f32[2]{0:T(128)S(1)} copy-done((f32[2]{0:T(128)S(1)}, f32[2]{0:T(128)}, u32[]{:S(2)}) %copy-start.19) | copy-done | bytes 32
  17.1 0.5 %weights.1 = (bf16[512,256]{1,0:T(8,128)(2,1)S(1)}, bf16[256,256]{1,0:T(8,128)(2,1)S(1)}, bf16[16,256]{1,0:T(8,128)(2,1)S(1)}, f32[256,128]{1,0:T(8,128)S(1)}, f32[16,128]{1,0:T(8,128)S(1)}) custom-call(bf16[32,90]{1,0:T(8,128)(2,1)S(1)} %copy-done.12, f32[1,32]{1,0:T(1,128)S(1)} %bitcast.3, bf16[32,32]{1,0:T(8,128)(2,1)S(1)} %copy-done.13, ...), custom_call_target="tpu_custom_call" | custom-call | tf_op jit(solution)/shard_map/weights/pallas_call | solution.py:548
  17.7 3.3 %collective-permute-done.3.dnear = bf16[16,2048]{1,0:T(8,128)(2,1)S(1)} collective-permute-done((bf16[16,2048]{1,0:T(8,128)(2,1)S(1)}, bf16[16,2048]{1,0:T(8,128)(2,1)S(1)}, u32[]{:S(2)}, u32[]{:S(2)}) %collective-permute-start.3) | collective-permute-done | bytes 65568 | tf_op jit(solution)/shard_map/ppermute | solution.py:599
  21.0 1.4 %collective-permute-done.4.dfar = bf16[16,2048]{1,0:T(8,128)(2,1)S(1)} collective-permute-done((bf16[16,2048]{1,0:T(8,128)(2,1)S(1)}, bf16[16,2048]{1,0:T(8,128)(2,1)S(1)}, u32[]{:S(2)}, u32[]{:S(2)}) %collective-permute-start.4) | collective-permute-done | bytes 65568 | tf_op jit(solution)/shard_map/ppermute | solution.py:597
  22.4 0.0 collective-permute-done.1.near
  22.4 0.0 collective-permute-done.2.far
  22.4 0.0 collective-permute-done.r0
  22.5 0.0 copy-start.1
  22.5 1.0 %copy-done.1 = bf16[5,2,96,256]{3,2,1,0:T(8,128)(2,1)S(1)} copy-done((bf16[5,2,96,256]{3,2,1,0:T(8,128)(2,1)S(1)}, bf16[5,2,96,256]{3,2,1,0:T(8,128)(2,1)}, u32[]{:S(2)}) %copy-start.1) | copy-done | bytes 491544
  23.5 0.8 %copy-done.8 = bf16[128,128]{1,0:T(8,128)(2,1)S(1)} copy-done((bf16[128,128]{1,0:T(8,128)(2,1)S(1)}, bf16[128,128]{1,0:T(8,128)(2,1)}, u32[]{:S(2)}) %copy-start.8) | copy-done | bytes 32792
  24.3 0.8 %copy-done.9 = bf16[128,64]{1,0:T(8,128)(2,1)S(1)} copy-done((bf16[128,64]{1,0:T(8,128)(2,1)S(1)}, bf16[128,64]{1,0:T(8,128)(2,1)}, u32[]{:S(2)}) %copy-start.9) | copy-done | bytes 16408
  25.0 0.8 %copy-done.10 = bf16[128,128]{1,0:T(8,128)(2,1)S(1)} copy-done((bf16[128,128]{1,0:T(8,128)(2,1)S(1)}, bf16[128,128]{1,0:T(8,128)(2,1)}, u32[]{:S(2)}) %copy-start.10) | copy-done | bytes 32792
  25.8 9.2 %model.1.adjoint = f32[2,2,16,2048]{3,2,1,0:T(8,128)S(1)} custom-call(bf16[96,2048]{1,0:T(8,128)(2,1)S(1)} %get-tuple-element.15.p0, bf16[96,2048]{1,0:T(8,128)(2,1)S(1)} %collective-permute-done.r0, bf16[32,2048]{1,0:T(8,128)(2,1)S(1)} %collective-permute-done.1.near, bf16[32,2048]{1,0:T(8,128)(2,1)S(1)} %collective-permute-done.2.far, ...), custom_call_target="tpu_custom_call" | custom-call | tf_op jit(solution)/shard_map/model/pallas_call | solution.py:548
  35.0 12.2 %prior.1 = f32[2,2,16,2048]{3,2,1,0:T(8,128)} custom-call(bf16[96,2048]{1,0:T(8,128)(2,1)S(1)} %get-tuple-element.15.p0, bf16[96,2048]{1,0:T(8,128)(2,1)S(1)} %collective-permute-done.r0, bf16[32,2048]{1,0:T(8,128)(2,1)S(1)} %collective-permute-done.1.near, bf16[32,2048]{1,0:T(8,128)(2,1)S(1)} %collective-permute-done.2.far, ...), custom_call_target="tpu_custom_call" | custom-call | tf_op jit(solution)/shard_map/prior/pallas_call | solution.py:548
  (22 shorter events, 0.0 us)
Async XLA Ops:
  0.0 22.5 %copy-start = (bf16[5,240,256]{2,1,0:T(8,128)(2,1)S(1)}, bf16[5,240,256]{2,1,0:T(8,128)(2,1)}, u32[]{:S(2)}) copy-start(bf16[5,240,256]{2,1,0:T(8,128)(2,1)} %constant.22.clone.rest_4_) | copy-start | bytes 1843204
  0.0 1.0 %copy-start.3 = (bf16[2,2,16,2048]{3,2,1,0:T(8,128)(2,1)S(1)}, bf16[2,2,16,2048]{3,2,1,0:T(8,128)(2,1)}, u32[]{:S(2)}) copy-start(bf16[2,2,16,2048]{3,2,1,0:T(8,128)(2,1)} %bg.1) | copy-start | bytes 786436
  1.0 0.9 %copy-start.4 = (bf16[2,2,96,128]{3,2,1,0:T(8,128)(2,1)S(1)}, bf16[2,2,96,128]{3,2,1,0:T(8,128)(2,1)}, u32[]{:S(2)}) copy-start(bf16[2,2,96,128]{3,2,1,0:T(8,128)(2,1)} %constant.16.clone.table) | copy-start | bytes 294916
  1.9 0.8 %copy-start.5 = (f32[16,1024]{1,0:T(8,128)S(1)}, f32[16,1024]{1,0:T(8,128)}, u32[]{:S(2)}) copy-start(f32[16,1024]{1,0:T(8,128)} %east.1) | copy-start | bytes 196612
  2.8 0.8 %copy-start.6 = (f32[16,1024]{1,0:T(8,128)S(1)}, f32[16,1024]{1,0:T(8,128)}, u32[]{:S(2)}) copy-start(f32[16,1024]{1,0:T(8,128)} %north.1) | copy-start | bytes 196612
  3.6 0.8 %copy-start.7 = (f32[16,1024]{1,0:T(8,128)S(1)}, f32[16,1024]{1,0:T(8,128)}, u32[]{:S(2)}) copy-start(f32[16,1024]{1,0:T(8,128)} %diff.1) | copy-start | bytes 196612
  4.4 0.7 %copy-start.14 = (f32[4,1,1,2,128]{4,3,2,1,0:T(2,128)S(1)}, f32[4,1,1,2,128]{4,3,2,1,0:T(2,128)}, u32[]{:S(2)}) copy-start(f32[4,1,1,2,128]{4,3,2,1,0:T(2,128)} %obs.1) | copy-start | bytes 12292
  5.1 0.7 %copy-start.15 = (s32[4,1,1,128]{3,2,1,0:T(1,128)S(1)}, s32[4,1,1,128]{3,2,1,0:T(1,128)}, u32[]{:S(2)}) copy-start(s32[4,1,1,128]{3,2,1,0:T(1,128)} %sensors.1) | copy-start | bytes 6148
  6.1 16.4 %collective-permute-start = (bf16[96,2048]{1,0:T(8,128)(2,1)S(1)}, bf16[96,2048]{1,0:T(8,128)(2,1)S(1)}, u32[]{:S(2)}, u32[]{:S(2)}) collective-permute-start(bf16[96,2048]{1,0:T(8,128)(2,1)S(1)} %get-tuple-element.15.p0), channel_id=1, source_target_pairs={{0,16},{1,17},{2,18},{3,19},{4,20},{5,21},{6,22},{7,23},{8,24},{9,... | collective-permute-start | bytes 1179656 | tf_op jit(solution)/shard_map/ppermute | solution.py:596
  9.1 13.3 %collective-permute-start.1 = (bf16[32,2048]{1,0:T(8,128)(2,1)S(1)}, bf16[32,2048]{1,0:T(8,128)(2,1)S(1)}, u32[]{:S(2)}, u32[]{:S(2)}) collective-permute-start(bf16[32,2048]{1,0:T(8,128)(2,1)S(1)} %get-tuple-element.16), channel_id=1, source_target_pairs={{0,1},{1,0},{2,3},{3,2},{4,5},{5,4},{6,7},{7,6},{8,9},{9,8},{10,11... | collective-permute-start | bytes 393224 | tf_op jit(solution)/shard_map/ppermute | solution.py:600
  9.1 13.3 %collective-permute-start.2 = (bf16[32,2048]{1,0:T(8,128)(2,1)S(1)}, bf16[32,2048]{1,0:T(8,128)(2,1)S(1)}, u32[]{:S(2)}, u32[]{:S(2)}) collective-permute-start(bf16[32,2048]{1,0:T(8,128)(2,1)S(1)} %get-tuple-element.17), channel_id=1, source_target_pairs={{0,16},{1,2},{2,1},{3,4},{4,3},{5,6},{6,5},{7,8},{8,7},{9,10},{10,... | collective-permute-start | bytes 393224 | tf_op jit(solution)/shard_map/ppermute | solution.py:598
  9.3 11.7 %collective-permute-start.3 = (bf16[16,2048]{1,0:T(8,128)(2,1)S(1)}, bf16[16,2048]{1,0:T(8,128)(2,1)S(1)}, u32[]{:S(2)}, u32[]{:S(2)}) collective-permute-start(bf16[16,2048]{1,0:T(8,128)(2,1)S(1)} %get-tuple-element.18), channel_id=1, source_target_pairs={{0,17},{1,16},{2,19},{3,18},{4,21},{5,20},{6,23},{7,22},{8,25},{9,... | collective-permute-start | bytes 196616 | tf_op jit(solution)/shard_map/ppermute | solution.py:599
  10.8 11.6 %collective-permute-start.4 = (bf16[16,2048]{1,0:T(8,128)(2,1)S(1)}, bf16[16,2048]{1,0:T(8,128)(2,1)S(1)}, u32[]{:S(2)}, u32[]{:S(2)}) collective-permute-start(bf16[16,2048]{1,0:T(8,128)(2,1)S(1)} %get-tuple-element.19), channel_id=1, source_target_pairs={{0,16},{1,18},{2,17},{3,20},{4,19},{5,22},{6,21},{7,24},{8,23},{9,... | collective-permute-start | bytes 196616 | tf_op jit(solution)/shard_map/ppermute | solution.py:597
  12.4 0.8 %copy-start.11 = (s32[2,16,256]{2,1,0:T(8,128)S(1)}, s32[2,16,256]{2,1,0:T(8,128)}, u32[]{:S(2)}) copy-start(s32[2,16,256]{2,1,0:T(8,128)} %constant.17.clone.taps) | copy-start | bytes 98308
  13.1 0.7 %copy-start.12 = (bf16[32,90]{1,0:T(8,128)(2,1)S(1)}, bf16[32,90]{1,0:T(8,128)(2,1)}, u32[]{:S(2)}) copy-start(bf16[32,90]{1,0:T(8,128)(2,1)} %conv_w.1) | copy-start | bytes 17284
  13.8 0.7 %copy-start.13 = (bf16[32,32]{1,0:T(8,128)(2,1)S(1)}, bf16[32,32]{1,0:T(8,128)(2,1)}, u32[]{:S(2)}) copy-start(bf16[32,32]{1,0:T(8,128)(2,1)} %mix_w.1) | copy-start | bytes 6148
  14.5 0.7 %copy-start.16 = (f32[32]{0:T(128)S(1)}, f32[32]{0:T(128)}, u32[]{:S(2)}) copy-start(f32[32]{0:T(128)} %param.22) | copy-start | bytes 388
  15.2 0.7 %copy-start.17 = (f32[32]{0:T(128)S(1)}, f32[32]{0:T(128)}, u32[]{:S(2)}) copy-start(f32[32]{0:T(128)} %param.24) | copy-start | bytes 388
  15.8 0.7 %copy-start.18 = (bf16[2,32]{1,0:T(2,128)(2,1)S(1)}, bf16[2,32]{1,0:T(2,128)(2,1)}, u32[]{:S(2)}) copy-start(bf16[2,32]{1,0:T(2,128)(2,1)} %out_w.1) | copy-start | bytes 388
  16.5 0.7 %copy-start.19 = (f32[2]{0:T(128)S(1)}, f32[2]{0:T(128)}, u32[]{:S(2)}) copy-start(f32[2]{0:T(128)} %param.26) | copy-start | bytes 28
  22.5 1.0 %copy-start.1 = (bf16[5,2,96,256]{3,2,1,0:T(8,128)(2,1)S(1)}, bf16[5,2,96,256]{3,2,1,0:T(8,128)(2,1)}, u32[]{:S(2)}) copy-start(bf16[5,2,96,256]{3,2,1,0:T(8,128)(2,1)} %constant.21.clone.rest_3_) | copy-start | bytes 1474564
  23.5 0.8 %copy-start.8 = (bf16[128,128]{1,0:T(8,128)(2,1)S(1)}, bf16[128,128]{1,0:T(8,128)(2,1)}, u32[]{:S(2)}) copy-start(bf16[128,128]{1,0:T(8,128)(2,1)} %constant.20.clone.rest_2_) | copy-start | bytes 98308
  24.3 0.8 %copy-start.9 = (bf16[128,64]{1,0:T(8,128)(2,1)S(1)}, bf16[128,64]{1,0:T(8,128)(2,1)}, u32[]{:S(2)}) copy-start(bf16[128,64]{1,0:T(8,128)(2,1)} %constant.19.clone.rest_1_) | copy-start | bytes 49156
  25.0 0.8 %copy-start.10 = (bf16[128,128]{1,0:T(8,128)(2,1)S(1)}, bf16[128,128]{1,0:T(8,128)(2,1)}, u32[]{:S(2)}) copy-start(bf16[128,128]{1,0:T(8,128)(2,1)} %constant.18.clone.rest_0_) | copy-start | bytes 98308
  25.8 9.2 %copy-start.2 = (bf16[5,160,224]{2,1,0:T(8,128)(2,1)S(1)}, bf16[5,160,224]{2,1,0:T(8,128)(2,1)}, u32[]{:S(2)}) copy-start(bf16[5,160,224]{2,1,0:T(8,128)(2,1)} %constant.23.clone.table) | copy-start | bytes 1075204
where the time goes:
time: 47.9 us; the launch traced here: 47.1 us
  Pallas kernels  22.2 us (46%)
  local copies, waits for them, and re-layouts  13.9 us (29%)
  starting transfers between devices  6.27 us (13%)
  waiting for transfers between devices  4.78 us (10%)
    pallas_call x4, Pallas kernels, call(): pl.pallas_call(body, out_shape=out_shape, in_specs=[whole] * len(args), o...  22.2 us
    unnamed x40, local copies, waits for them, and re-layouts  13.9 us
    ppermute x1, waiting for transfers between devices, exchange_pairs(): r_dnear = lax.ppermute(dnear, axes, diag_near)  3.33 us
    ppermute x1, starting transfers between devices, exchange_pairs(): r0 = lax.ppermute(p0, axes, across)  3.03 us
    ppermute x1, starting transfers between devices, exchange_pairs(): r_dnear = lax.ppermute(dnear, axes, diag_near)  1.56 us
    ppermute x1, starting transfers between devices, exchange_pairs(): r_dfar = lax.ppermute(dfar, axes, diag_far)  1.52 us
    ppermute x1, waiting for transfers between devices, exchange_pairs(): r_dfar = lax.ppermute(dfar, axes, diag_far)  1.44 us
  transfers between devices with their start and end apart: 5, of which 2 were waited for; matrix products, arithmetic and copies ran while one was open for 0% of the time, Pallas kernels for 1%

commit v1 on v0

--- a/solution.py
+++ b/solution.py
@@ -16,6 +16,8 @@
 BF = jnp.bfloat16
 F32 = jnp.float32
 VMEM_BYTES = 48 * 1024 * 1024
+COST = 60 * 10**6
+PACK_BYTES = 64 * 1024 * 1024 - 1024 * 1024
 GELU_1 = 2.0 * float(np.sqrt(2.0 / np.pi))
 GELU_2 = 8.0 * 0.044715 * float(np.sqrt(2.0 / np.pi))
 
@@ -33,34 +35,44 @@
     return high, (x - high.astype(F32)).astype(BF)
 
 
+def fetch(pairs, sems):
+    copies = [pltpu.make_async_copy(source, target, sems.at[n]) for n, (source, target) in enumerate(pairs)]
+    for copy in copies:
+        copy.start()
+    for copy in copies:
+        copy.wait()
+
+
 def pack_table(rows, fields):
-    table = np.zeros((2, 2, 96, 128), np.float32)
+    table = np.zeros((2, 2, 80, 128), np.float32)
     coef_row = fields * rows
     for parity in range(2):
         for side in range(2):
             for message in range(4):
                 far, diagonal = message % 2, message // 2
                 bottom = (far == 0) == (parity == 0)
-                base = 64 + 16 * far if diagonal else 32 * far
-                height = 16 if diagonal else 32
                 out = table[parity, side]
                 if diagonal:
+                    base = 64 + 8 * far
                     for field in range(fields):
                         out[base + field, field * rows + (rows - 1 if bottom else 0)] = 1
-                else:
-                    for field in range(fields):
-                        for e in range(HALO):
-                            row = rows - HALO + e if bottom else e
-                            out[base + field * HALO + e, field * rows + row] = 1
+                    if side == 0:
+                        out[base + fields, coef_row + 3 * rows + 15] = 1
+                    continue
+                base = 32 * far
+                for field in range(fields):
+                    for e in range(HALO):
+                        row = rows - HALO + e if bottom else e
+                        out[base + field * HALO + e, field * rows + row] = 1
                 for slot in range(8):
                     j = side * 8 + slot
-                    target = base + height - 8 + slot
+                    target = base + 24 + slot
                     if j < 3 * CROWS:
                         c, e = divmod(j, CROWS)
                         row = rows - CROWS + e if bottom else e
                         out[target, coef_row + c * rows + row] = 1
                     else:
-                        out[target, coef_row + 3 * rows + (15 if diagonal else 14)] = 1
+                        out[target, coef_row + 3 * rows + 14] = 1
     return table
 
 
@@ -85,6 +97,7 @@
                 out[(q * variables + v) * rows + r, r * lanes + q * variables + v] = 1
     halo = np.zeros((5, frames, 2 * HALO * lanes, quarters * 64), np.float32)
     chalo = np.zeros((5, 3 * 2 * CROWS * lanes, quarters * 64), np.float32)
+    ohalo = np.zeros((5, 3 * 2 * CROWS * lanes, quarters * 32), np.float32)
     for case in range(5):
         top_slot, bottom_slot, top_ok, bottom_ok = near_far(case)
         for q in range(quarters):
@@ -102,24 +115,30 @@
                             j = c * CROWS + e
                             column = q * 64 + slot * 32 + (j // 8) * 16 + 8 + j % 8
                             row = ((c * 2 + half) * CROWS + e) * lanes + lane
-                            chalo[case, row, column] = 1.0 if c == 2 else 0.5
-    return own, coef, out, halo, chalo
+                            chalo[case, row, column] = 1
+                            column = q * 32 + (j // 8) * 16 + slot * 8 + j % 8
+                            ohalo[case, row, column] = 1
+    return own, coef, out, halo, chalo, ohalo
+
+
+def round16(n):
+    return -(-n // 16) * 16
 
 
 def conv_table(rows, frames, others, variables, group):
     channels = (frames + others) * variables
-    tall = group + 2
+    tall = round16((group + 2) * channels)
     own_rows = frames * variables * rows
     oth_rows = others * variables * rows
-    table = np.zeros((5, rows // group * tall * channels, own_rows + oth_rows + 96), np.float32)
+    table = np.zeros((5, rows // group * tall, own_rows + oth_rows + 80), np.float32)
     for case in range(5):
         top_slot, bottom_slot, top_ok, bottom_ok = near_far(case)
         for g in range(rows // group):
-            for yy in range(tall):
+            for yy in range(group + 2):
                 y = g * group + yy - 1
                 for f in range(frames + others):
                     for v in range(variables):
-                        target = (g * tall + yy) * channels + f * variables + v
+                        target = g * tall + yy * channels + f * variables + v
                         own = f < frames
                         field = (f if own else f - frames) * variables + v
                         if 0 <= y < rows:
@@ -128,41 +147,56 @@
                         slot, ok = (top_slot, top_ok) if y < 0 else (bottom_slot, bottom_ok)
                         if not ok:
                             continue
+                        column = own_rows + oth_rows
                         if own:
-                            column = own_rows + oth_rows + slot * 32
-                            column += field * HALO + (HALO - 1 if y < 0 else 0)
+                            column += slot * 32 + field * HALO + (HALO - 1 if y < 0 else 0)
                         else:
-                            column = own_rows + oth_rows + 64 + slot * 16 + field
+                            column += 64 + slot * 8 + field
                         table[case, target, column] = 1
     return table
 
 
 def tap_table(offsets, frames, variables, group, depth):
     channels = len(offsets) * variables
-    tall = group + 2
-    table = np.full((frames * group, depth), -1, np.int32)
+    tall = round16((group + 2) * channels)
+    table = np.full((8, depth), -1, np.int32)
     for t in range(frames):
-        for y in range(group):
-            for s in range(3):
-                for yy in range(tall):
-                    for f, offset in enumerate(offsets):
-                        for v in range(variables):
-                            lag, i = offset - t + KT // 2, yy - y
-                            if 0 <= lag < KT and 0 <= i < 3:
-                                k = s * tall * channels + yy * channels + f * variables + v
-                                table[t * group + y, k] = ((v * KT + lag) * 3 + i) * 3 + s
-            for part in range(3):
-                table[t * group + y, 3 * tall * channels + part] = 3 * 3 * KT * variables + part
+        for s in range(3):
+            for i in range(3):
+                for f, offset in enumerate(offsets):
+                    lag = offset - t + KT // 2
+                    for v in range(variables):
+                        if 0 <= lag < KT:
+                            k = s * tall + i * channels + f * variables + v
+                            table[t, k] = ((v * KT + lag) * 3 + i) * 3 + s
+    table[frames, 3 * tall : 3 * tall + 3] = 3 * 3 * KT * variables + np.arange(3)
     return table
+
+
+def index_rows(tables, lanes):
+    out = np.full((8, lanes), -1, np.int32)
+    for n, table in enumerate(tables):
+        out[n, : table.shape[0]] = np.where(table.any(1), table.argmax(1), -1)
+    return out
 
 
 def case_of(parity, index, count):
     return jnp.where(index == 0, 2, jnp.where(index == count - 1, jnp.where(parity == 1, 3, 4), parity))
 
 
-def pack_kernel(bg, east, north, diff, sensors, obs, table, p0, near, far, dnear, dfar, *, frames):
+def pack_kernel(
+    bg_in, east_in, north_in, diff_in, sensors_in, obs_in, table_in, p_c, near, far, dnear, dfar,
+    bg, east, north, diff, sensors, obs, table, sems, *, frames,
+):
     me_t = lax.axis_index("tm")
     parity = lax.axis_index("lat") % 2
+    fetch(
+        [
+            (bg_in, bg), (east_in, east), (north_in, north), (diff_in, diff),
+            (sensors_in, sensors), (obs_in, obs), (table_in.at[parity], table),
+        ],
+        sems,
+    )
     fields = bg.shape[0] * bg.shape[1]
     rows, lon = bg.shape[2], bg.shape[3]
     half = lon // 2
@@ -196,25 +230,52 @@
         ],
         axis=0,
     ).astype(BF)
-    split = fields * rows
-    p0[0:split, :] = fields_2d
-    p0[split : split + rows, 0:half] = a
-    p0[split + rows : split + 2 * rows, 0:half] = b
-    p0[split : split + rows, half:lon] = k
-    p0[split + rows : split + 2 * rows, half:lon] = extra
+    p_c[0:rows, 0:half] = a
+    p_c[rows : 2 * rows, 0:half] = b
+    p_c[0:rows, half:lon] = k
+    p_c[rows : 2 * rows, half:lon] = extra
     for side in range(2):
         cut = slice(side * half, (side + 1) * half)
         source = jnp.concatenate([fields_2d[:, cut], a, b, k, extra], axis=0)
-        message = dot(table[parity, side], source).astype(BF)
+        message = dot(table[side], source).astype(BF)
         near[:, cut] = message[0:32]
         far[:, cut] = message[32:64]
-        dnear[:, cut] = message[64:80]
-        dfar[:, cut] = message[80:96]
-
-
-def prep_kernel(conv_w, conv_b, mix_w, mix_b, out_w, out_b, taps, w1, w2, w3, b2, b3, *, group, i_of):
+        dnear[:, cut] = message[64:72]
+        dfar[:, cut] = message[72:80]
+
+
+def prep_kernel(*refs, group, channels, relay, i_of, parity_of):
+    sources, rest = refs[:8], refs[8:]
+    if relay:
+        p_c, near, far, q_c, *rest = rest
+    w1, w2, w3, b2, b3, p_conv, p_own, p_coef, p_out, p_halo, p_chalo, p_ohalo = rest[:12]
+    conv_w, conv_b, mix_w, mix_b, out_w, out_b, taps, index, sems = rest[12:]
     hid = mix_w.shape[0]
-    table = taps[i_of()]
+    case = case_of(parity_of(), lax.axis_index("lat"), lax.axis_size("lat"))
+    moves = [*zip(sources[:6], (conv_w, conv_b, mix_w, mix_b, out_w, out_b))]
+    moves += [(sources[6].at[i_of()], taps), (sources[7].at[case], index)]
+    if relay:
+        moves.append((p_c, q_c.at[0:32]))
+        q_c[32:40, :] = near[24:32, :]
+        q_c[40:48, :] = far[24:32, :]
+    fetch(moves, sems)
+    columns = index[...].astype(F32).T
+
+    def select(n, shape):
+        lanes = lax.broadcasted_iota(jnp.int32, shape, 1).astype(F32)
+        return jnp.where(lanes == columns[0 : shape[0], n : n + 1], 1.0, 0.0)
+
+    frames = p_halo.shape[0]
+    p_conv[...] = select(0, p_conv.shape).astype(BF)
+    for t in range(frames):
+        p_halo[t] = select(1 + t, p_halo.shape[1:]).astype(BF)
+    for n, target in ((1 + frames, p_chalo), (5 + frames, p_ohalo)):
+        halved = lax.broadcasted_iota(jnp.int32, target.shape, 0) < target.shape[0] // 3 * 2
+        target[...] = (select(n, target.shape) * jnp.where(halved, 0.5, 1.0)).astype(BF)
+    p_own[...] = select(2 + frames, p_own.shape).astype(BF)
+    p_coef[...] = select(3 + frames, p_coef.shape).astype(BF)
+    p_out[...] = select(4 + frames, p_out.shape).astype(BF)
+    table = taps[...]
 
     def column(row):
         n = row.shape[1]
@@ -233,9 +294,17 @@
         [0.5 * conv_w[...].astype(F32)] + pieces + [jnp.zeros((hid, padded - ntap - 3), F32)], axis=1
     ).astype(BF)
     tap_id = lax.broadcasted_iota(jnp.int32, (padded, table.shape[1]), 0)
-    for ty in range(table.shape[0]):
-        chosen = jnp.where(tap_id == table[ty : ty + 1, :], 1.0, 0.0).astype(BF)
-        w1[ty * hid : (ty + 1) * hid, :] = dot(weights, chosen).astype(BF)
+
+    def chosen(n):
+        return dot(weights, jnp.where(tap_id == table[n : n + 1, :], 1.0, 0.0).astype(BF))
+
+    biased = chosen(frames)
+    for t in range(frames):
+        first = chosen(t)
+        for y in range(group):
+            start = (t * group + y) * hid
+            moved = pltpu.roll(first, y * channels, 1) if y else first
+            w1[start : start + hid, :] = (moved + biased).astype(BF)
     tall = group * hid
     row = lax.broadcasted_iota(jnp.int32, (tall, hid), 0) & (hid - 1)
     up = jnp.where(row == lax.broadcasted_iota(jnp.int32, (tall, hid), 1), 1.0, 0.0).astype(BF)
@@ -245,34 +314,35 @@
     cols2 = lax.broadcasted_iota(jnp.int32, (tall, tall), 1) >> shift
     w2[...] = jnp.where(rows2 == cols2, mixed, 0.0).astype(BF)
     variables = out_w.shape[0]
-    spread = dot_t(out_w[...], up)
-    parts, parts_b = [], []
-    for v in range(variables):
-        here = lax.broadcasted_iota(jnp.int32, (group, tall), 0) == (
-            lax.broadcasted_iota(jnp.int32, (group, tall), 1) >> shift
-        )
-        parts.append(jnp.where(here, jnp.broadcast_to(spread[v : v + 1], (group, tall)), 0.0))
-        parts_b.append(jnp.broadcast_to(out_b[:, v : v + 1], (group, 128)))
-    w3[...] = jnp.concatenate(parts, axis=0).astype(BF)
-    b3[...] = jnp.concatenate(parts_b, axis=0)
+    wide = dot_t(out_w[...], up)
+    y = lax.broadcasted_iota(jnp.int32, (group, tall), 0)
+    here = y == lax.broadcasted_iota(jnp.int32, (group, tall), 1) >> shift
+    w3[...] = jnp.concatenate(
+        [jnp.where(here, jnp.broadcast_to(wide[v : v + 1], (group, tall)), 0.0) for v in range(variables)],
+        axis=0,
+    ).astype(BF)
+    b3[...] = jnp.concatenate(
+        [jnp.broadcast_to(out_b[:, v : v + 1], (group, 128)) for v in range(variables)], axis=0
+    )
     mixed_bias = jnp.broadcast_to(0.5 * column(mix_b[...]), (hid, 128))
     b2[...] = jnp.concatenate([mixed_bias] * group, axis=0)
 
 
 def model_kernel(
-    p0, r0, near, far, dnear, dfar, *rest,
-    rows, frames, variables, own_bg, oth_bg, tile_cols, n_sens, paired, i_of, parity_of,
+    p_bg, q_c, r_c, near, far, dnear, dfar, *rest,
+    rows, frames, variables, tile_cols, n_sens, paired, i_of, parity_of,
 ):
     sens = None if paired else rest[0]
-    p_own, p_coef, p_out, p_halo, p_chalo, out, field_a, field_b, coefs = rest[-9:]
-    lon = p0.shape[1]
+    first = 0 if paired else 1
+    prior, p_own, p_coef, p_out, p_halo, p_chalo, p_ohalo = rest[first : first + 7]
+    out, field_a, field_b, coefs = rest[first + 7 :]
+    lon = p_bg.shape[1]
     half = lon // 2
     quarters = 8 // variables
     width = half // quarters
     me_l, count = lax.axis_index("lat"), lax.axis_size("lat")
     parity = parity_of()
     me_t = i_of()
-    case = case_of(parity, me_l, count)
     top_ok, bottom_ok = me_l > 0, me_l < count - 1
     tall = rows + 2 * HALO
 
@@ -282,26 +352,24 @@
             body, rim = [], []
             for q in range(quarters):
                 cut = slice(h * half + q * width, h * half + (q + 1) * width)
-                body.append(p0[t * variables * rows : (t + 1) * variables * rows, cut])
+                body.append(p_bg[t * variables * rows : (t + 1) * variables * rows, cut])
                 rim += [near[:, cut], far[:, cut]]
             field_a[g, HALO : HALO + rows] = dot(p_own[...], jnp.concatenate(body, axis=0)).reshape(rows, 8, width)
-            edges = dot(p_halo[case, t], jnp.concatenate(rim, axis=0)).reshape(2 * HALO, 8, width)
+            edges = dot(p_halo[t], jnp.concatenate(rim, axis=0)).reshape(2 * HALO, 8, width)
             field_a[g, 0:HALO] = edges[0:HALO]
             field_a[g, HALO + rows : tall] = edges[HALO:]
 
     ctall = rows + 2 * CROWS
     for source in range(2):
-        big, at = (p0, own_bg) if source == 0 else (r0, oth_bg)
+        big = q_c if source == 0 else r_c
         spot = me_t if source == 0 else 1 - me_t
-        m_near, m_far = (near, far) if source == 0 else (dnear, dfar)
-        last = m_near.shape[0]
         pieces = []
         for side in range(2):
             for c_row in range(2):
                 stack = []
                 for q in range(quarters):
                     cut = slice(side * half + q * width, side * half + (q + 1) * width)
-                    stack.append(big[at + c_row * rows : at + (c_row + 1) * rows, cut])
+                    stack.append(big[c_row * rows : (c_row + 1) * rows, cut])
                 pieces.append(jnp.concatenate(stack, axis=0))
         scaled = p_coef[...]
         ha = (0.5 * dot(scaled, pieces[0])).reshape(rows, 8, width)
@@ -309,11 +377,12 @@
         kk = dot(scaled, pieces[2]).reshape(rows, 8, width) + K_MID
         rim = []
         for q in range(quarters):
-            for message in (m_near, m_far):
+            for message in (near[16:32], far[16:32]) if source == 0 else (r_c[32:48],):
                 for side in range(2):
                     cut = slice(side * half + q * width, side * half + (q + 1) * width)
-                    rim.append(message[last - 16 : last, cut])
-        edges = dot(p_chalo[case], jnp.concatenate(rim, axis=0)).reshape(3, 2, CROWS, 8, width)
+                    rim.append(message[:, cut])
+        edges = dot((p_ohalo if source else p_chalo)[...], jnp.concatenate(rim, axis=0))
+        edges = edges.reshape(3, 2, CROWS, 8, width)
         k_top = edges[2, 0] + jnp.where(top_ok, K_MID, 0.0)
         k_bottom = edges[2, 1] + jnp.where(bottom_ok, K_MID, 0.0)
         for start, size, xa, xb, xk in (
@@ -364,7 +433,7 @@
         return result
 
     def forward(source, target, low, high):
-        def row_step(r, _):
+        for r in range(low, high):
             cr = r - (HALO - CROWS)
             for t in range(frames):
                 center = [source[t * 2 + h, r] for h in range(2)]
@@ -376,12 +445,9 @@
                         + (coefs[h, 1, cr] * west[h] + coefs[h, 2, cr] * source[g, r + 1])
                         + coefs[h, 3, cr] * source[g, r - 1]
                     )
-            return 0
-
-        lax.fori_loop(low, high, row_step, 0, unroll=2)
 
     def backward(source, target, low, high):
-        def row_step(r, _):
+        for r in range(low, high):
             cr = r - (HALO - CROWS)
             for t in range(frames):
                 center = [source[t * 2 + h, r] for h in range(2)]
@@ -394,9 +460,6 @@
                         + (east[h] + coefs[h, 2, cr - 1] * source[g, r - 1])
                         + coefs[h, 3, cr + 1] * source[g, r + 1]
                     )
-            return 0
-
-        lax.fori_loop(low, high, row_step, 0, unroll=2)
 
     buffers = [field_a, field_b]
     for step in range(SUB):
@@ -413,16 +476,15 @@
             first = (h * 4 + band) * count
             return [sens[...].astype(F32)[first + n : first + n + 1] for n in range(count)]
         if band in (1, 3):
-            at = slice(own_bg + rows, own_bg + rows + 16)
-            mine, other = p0[at, half:lon].astype(F32), r0[at, half:lon].astype(F32)
+            at = slice(rows, rows + 16)
+            mine, other = q_c[at, half:lon].astype(F32), r_c[at, half:lon].astype(F32)
             n = 14 if band == 1 else 12
             return [jnp.where(me_t == h, mine[n : n + 1], other[n + 1 : n + 2])]
         from_far = parity == (0 if band == 0 else 1)
-        found = []
-        for x, y in ((near, far), (dnear, dfar)):
-            last = x.shape[0]
-            pair = [m[last - 16 : last, half:lon].astype(F32)[15:16] for m in (x, y)]
-            found.append(jnp.where(from_far, pair[1], pair[0]))
+        pair = [m[16:32, half:lon].astype(F32)[15:16] for m in (near, far)]
+        row = frames * variables
+        pair += [m[:, 0:half].astype(F32)[row : row + 1] for m in (dnear, dfar)]
+        found = [jnp.where(from_far, pair[n + 1], pair[n]) for n in (0, 2)]
         return [jnp.where(me_t == h, found[0], found[1])]
 
     row_bits = tile_cols.bit_length() - 1
@@ -443,9 +505,8 @@
 
     def assimilate(g, row_list, where_row, quarter, lane_of, values):
         total = where_row.shape[1]
-        onehot = jnp.where(
-            lax.broadcasted_iota(jnp.int32, (width, total), 0) == lane_of, 1.0, 0.0
-        ).astype(BF)
+        lanes_bf = lax.broadcasted_iota(jnp.int32, (width, total), 0).astype(F32).astype(BF)
+        onehot = jnp.where(lanes_bf == lane_of.astype(F32).astype(BF), BF(1), BF(0))
         stack = jnp.concatenate([forecast[g, HALO + r] for r in row_list], axis=0)
         high, low = split2(stack)
         picked = dot(high, onehot) + dot(low, onehot)
@@ -459,7 +520,8 @@
         for v in range(1, variables):
             target = jnp.where(variable == v, values[v], target)
         misfit = jnp.where(here_q, misfit - target, 0.0)
-        weighted = jnp.concatenate([jnp.where(where_row == r, misfit, 0.0) for r in row_list], axis=0)
+        row_f = where_row.astype(F32)
+        weighted = jnp.concatenate([jnp.where(row_f == float(r), misfit, 0.0) for r in row_list], axis=0)
         high, low = split2(weighted)
         return (dot_t(high, onehot) + dot_t(low, onehot)).reshape(len(row_list), 8, width)
 
@@ -492,66 +554,67 @@
                 cut = slice(h * half + q * width, h * half + (q + 1) * width)
                 for v in range(variables):
                     base = (q * variables + v) * rows
-                    out[t, v, :, cut] = back[base : base + rows]
+                    out[t, v, :, cut] = prior[t, v, :, cut] - back[base : base + rows]
+
+
+def gelu(y):
+    inner = y * (GELU_1 + GELU_2 * (y * y))
+    return (y + y * jnp.tanh(inner)).astype(BF)
+
+
+def shifted(chosen, window, depth):
+    tall, lon = chosen.shape
+    window[0:tall] = pltpu.roll(chosen, 1, 1).astype(BF)
+    window[tall : 2 * tall] = chosen.astype(BF)
+    window[2 * tall : 3 * tall] = pltpu.roll(chosen, lon - 1, 1).astype(BF)
+    ones = lax.broadcasted_iota(jnp.int32, (depth - 3 * tall, lon), 0) < 3
+    window[3 * tall : depth] = jnp.where(ones, 1.0, 0.0).astype(BF)
+
+
+def widen(column, chunk):
+    return jnp.concatenate([column] * (chunk // 128), axis=1)
 
 
 def conv_kernel(
-    p0, r0, near, far, dnear, dfar, adjoint, table, w1, w2, w3, b2, b3, out, window,
-    *, rows, frames, variables, own_bg, oth_bg, group, chunk, parity_of,
+    p_bg, r_bg, near, far, dnear, dfar, w1, w2, w3, b2, b3, select, out, window,
+    *, frames, variables, group, chunk,
 ):
-    lon = p0.shape[1]
-    me_l, count = lax.axis_index("lat"), lax.axis_size("lat")
-    case = case_of(parity_of(), me_l, count)
-    groups = rows // group
-    tall = table.shape[1] // groups
-    depth = window.shape[1]
-    stack = jnp.concatenate(
-        [p0[0:own_bg], r0[0:oth_bg], near[...], far[...], dnear[...], dfar[...]], axis=0
-    )
-    chosen = dot(table[case], stack)
+    groups, depth, lon = window.shape
+    fields = jnp.concatenate([x[...] for x in (p_bg, r_bg, near, far, dnear, dfar)], axis=0)
+    chosen = dot(select[...], fields)
+    tall = chosen.shape[0] // groups
     for g in range(groups):
-        center = chosen[g * tall : (g + 1) * tall]
-        window[g, 0:tall] = pltpu.roll(center, 1, 1).astype(BF)
-        window[g, tall : 2 * tall] = center.astype(BF)
-        window[g, 2 * tall : 3 * tall] = pltpu.roll(center, lon - 1, 1).astype(BF)
-        left = depth - 3 * tall
-        ones = lax.broadcasted_iota(jnp.int32, (left, lon), 0) < 3
-        window[g, 3 * tall : depth] = jnp.where(ones, 1.0, 0.0).astype(BF)
-
-    def gelu(y):
-        inner = y * (GELU_1 + GELU_2 * (y * y))
-        return (y + y * jnp.tanh(inner)).astype(BF)
-
+        shifted(chosen[g * tall : (g + 1) * tall], window.at[g], depth)
     hidden = w2.shape[0]
-    bias2 = jnp.concatenate([b2[...]] * (chunk // 128), axis=1)
-    bias3 = jnp.concatenate([b3[...]] * (chunk // 128), axis=1)
-
-    def columns(n, _):
-        cut = pl.ds(pl.multiple_of(n * chunk, chunk), chunk)
+    bias2, bias3 = widen(b2[...], chunk), widen(b3[...], chunk)
+    pending = []
+    for n in range(lon // chunk):
+        cut = slice(n * chunk, (n + 1) * chunk)
         for g in range(groups):
-            taps = window[g, :, cut]
+            first = dot(w1[...], window[g, :, cut])
             for t in range(frames):
-                one = gelu(dot(w1[t * hidden : (t + 1) * hidden], taps))
-                two = gelu(dot(w2[...], one) + bias2)
-                score = dot(w3[...], two) + bias3
-                for v in range(variables):
-                    span = slice(g * group, (g + 1) * group)
-                    out[t, v, span, cut] = score[v * group : (v + 1) * group] - adjoint[t, v, span, cut]
-        return 0
-
-    lax.fori_loop(0, lon // chunk, columns, 0)
-
-
-def call(body, out_shape, scratch, *args):
+                one = gelu(first[t * hidden : (t + 1) * hidden])
+                pending.append((t, g, cut, gelu(dot(w2[...], one) + bias2)))
+    for t, g, cut, two in pending:
+        score = dot(w3[...], two) + bias3
+        for v in range(variables):
+            out[t, v, g * group : (g + 1) * group, cut] = score[v * group : (v + 1) * group]
+
+
+def call(body, out_shape, scratch, *args, fetched=(), limit=VMEM_BYTES, cost=None):
     whole = pl.BlockSpec(memory_space=pltpu.VMEM)
+    given = pl.BlockSpec(memory_space=pltpu.HBM)
     several = isinstance(out_shape, (list, tuple))
+    if cost is not None:
+        cost = pl.CostEstimate(flops=10**8, bytes_accessed=cost, transcendentals=0)
     return pl.pallas_call(
         body,
         out_shape=out_shape,
-        in_specs=[whole] * len(args),
+        in_specs=[given if n in fetched else whole for n in range(len(args))],
         out_specs=[whole] * len(out_shape) if several else whole,
         scratch_shapes=scratch,
-        compiler_params=pltpu.CompilerParams(vmem_limit_bytes=VMEM_BYTES),
+        compiler_params=pltpu.CompilerParams(vmem_limit_bytes=limit),
+        cost_estimate=cost,
     )(*args)
 
 
@@ -582,23 +645,25 @@
     fields = frames * variables
     bands = lax.axis_size("lat")
     table = jnp.asarray(pack_table(rows, fields), BF)
-    big = struct((fields * rows + 2 * rows, lon), BF)
-    lat_message, diagonal = struct((32, lon), BF), struct((16, lon), BF)
+    arrays = (background, east, north, diff, sensors, observations)
+    lat_message, diagonal = struct((32, lon), BF), struct((8, lon), BF)
     with jax.named_scope("pack"):
-        p0, near, far, dnear, dfar = call(
+        p_c, near, far, dnear, dfar = call(
             functools.partial(pack_kernel, frames=frames),
-            [big, lat_message, lat_message, diagonal, diagonal],
-            [],
-            background, east, north, diff, sensors, observations, table,
+            [struct((2 * rows, lon), BF), lat_message, lat_message, diagonal, diagonal],
+            [pltpu.VMEM(x.shape, x.dtype) for x in arrays]
+            + [pltpu.VMEM(table.shape[1:], BF), pltpu.SemaphoreType.DMA((7,))],
+            *arrays, table, fetched=range(7), limit=PACK_BYTES,
         )
     axes = ("tm", "lat")
     across, on_chip, next_chip, diag_near, diag_far = swap_pairs(lax.axis_size("tm"), bands)
-    r0 = lax.ppermute(p0, axes, across)
+    p_bg = background.reshape(fields * rows, lon)
+    r_bg = lax.ppermute(p_bg, axes, across)
     r_dfar = lax.ppermute(dfar, axes, diag_far)
     r_far = lax.ppermute(far, axes, next_chip)
     r_dnear = lax.ppermute(dnear, axes, diag_near)
     r_near = lax.ppermute(near, axes, on_chip)
-    return p0, r0, r_near, r_far, r_dnear, r_dfar
+    return p_bg, r_bg, p_c, r_near, r_far, r_dnear, r_dfar
 
 
 def exchange_gathered(background, east, north, diff, sensors, observations):
@@ -630,35 +695,34 @@
     sens = jnp.stack([x.reshape(2, tiles // 2, -1) for x in bands_of], axis=1)
     sens = sens.reshape(-1, described.shape[1])
 
-    def block(fields_3d, h):
+    def block(h):
         part = coefs[:, :, h * half : (h + 1) * half]
         blank = jnp.zeros_like(part[0])
         return jnp.concatenate(
-            [
-                fields_3d.reshape(-1, lon),
-                jnp.concatenate([part[0], part[2]], axis=1),
-                jnp.concatenate([part[1], blank], axis=1),
-            ],
+            [jnp.concatenate([part[0], part[2]], axis=1), jnp.concatenate([part[1], blank], axis=1)],
             axis=0,
         )
 
-    def message(fields_4d, depth, h, bottom, height):
-        height_rows = fields_4d.shape[2]
-        edge = fields_4d[:, :, height_rows - depth :] if bottom else fields_4d[:, :, :depth]
-        edge = edge.reshape(-1, lon)
-        part = coefs[:, :, h * half : (h + 1) * half]
-        part = part[:, rows - CROWS :] if bottom else part[:, :CROWS]
+    def edge_fields(fields_4d, depth, bottom):
+        first = rows - depth if bottom else 0
+        return fields_4d[:, :, first : first + depth].reshape(-1, lon)
+
+    def edge_coefs(h, bottom):
+        first = rows - CROWS if bottom else 0
+        part = coefs[:, first : first + CROWS, h * half : (h + 1) * half]
         part = jnp.pad(part.reshape(3 * CROWS, half), ((0, 16 - 3 * CROWS), (0, 0)))
-        part = jnp.concatenate([part[:8], part[8:]], axis=1)
-        blank = jnp.zeros((height - 8 - edge.shape[0], lon), BF)
-        return jnp.concatenate([edge, blank, part], axis=0)
-
-    p0, r0 = block(background, 0), block(around, 1)
-    near = lax.ppermute(message(background, HALO, 0, False, 32), "lat", up)
-    far = lax.ppermute(message(background, HALO, 0, True, 32), "lat", down)
-    dnear = lax.ppermute(message(around, 1, 1, False, 16), "lat", up)
-    dfar = lax.ppermute(message(around, 1, 1, True, 16), "lat", down)
-    return p0, r0, near, far, dnear, dfar, sens
+        return jnp.concatenate([part[:8], part[8:]], axis=1)
+
+    received = []
+    for bottom, pairs in ((False, up), (True, down)):
+        message = [edge_fields(background, HALO, bottom), edge_coefs(0, bottom)]
+        message = lax.ppermute(jnp.concatenate(message, axis=0), "lat", pairs)
+        diagonal = lax.ppermute(edge_fields(around, 1, bottom), "lat", pairs)
+        received.append((message, diagonal, lax.ppermute(edge_coefs(1, bottom), "lat", pairs)))
+    (near, dnear, c_near), (far, dfar, c_far) = received
+    r_c = jnp.concatenate([block(1), c_near, c_far], axis=0)
+    p_bg, r_bg = background.reshape(-1, lon), around.reshape(-1, lon)
+    return p_bg, r_bg, block(0), r_c, near, far, dnear, dfar, sens
 
 
 def shards(
@@ -668,50 +732,81 @@
     frames, variables, rows, lon = background.shape
     tiles, bands = lax.axis_size("tm"), lax.axis_size("lat")
     paired = tiles == 2 and bands % 2 == 0
-    group = 8
+    group = rows // 2
     hid = mix_weight.shape[0]
     fields = frames * variables
     arrays = (background, drift_east, drift_north, diffusivity, sensors, observations)
     if paired:
-        received, sens = exchange_pairs(*arrays), ()
+        p_bg, r_bg, p_c, near, far, dnear, dfar = exchange_pairs(*arrays)
         offsets = [[*range(2 * frames)], [*range(frames), *range(-frames, 0)]]
         i_of = lambda: lax.axis_index("tm")
         parity_of = lambda: lax.axis_index("lat") % 2
+        near, far, r_bg = lax.optimization_barrier((near, far, r_bg))
+        relayed, sens = (p_c, near, far), ()
     else:
-        *received, sens = exchange_gathered(*arrays)
-        sens = (sens,)
+        p_bg, r_bg, q_c, r_c, near, far, dnear, dfar, sens = exchange_gathered(*arrays)
         offsets = [[*range(frames), *range(-frames, 0), *range(frames, 2 * frames)]]
         i_of = lambda: 0
         parity_of = lambda: 0
+        relayed, sens = (), (sens,)
     others = len(offsets[0]) - frames
-    own_bg, oth_bg = fields * rows, others * variables * rows
-
-    need = 3 * (group + 2) * (frames + others) * variables + 3
-    depth = -(-need // 128) * 128
+
+    channels = (frames + others) * variables
+    depth = -(-(3 * round16((group + 2) * channels) + 3) // 128) * 128
+    quarters = 8 // variables
+    width = lon // 8
     taps = jnp.asarray(np.stack([tap_table(o, frames, variables, group, depth) for o in offsets]))
+    own, coef, back, halo, chalo, ohalo = model_tables(rows, frames, variables, quarters)
+    gather = conv_table(rows, frames, others, variables, group)
+    index = np.stack(
+        [index_rows([gather[c], *halo[c], chalo[c], own, coef, back, ohalo[c]], 256) for c in range(5)]
+    )
+    tables = [gather[0], own, coef, back, halo[0], chalo[0], ohalo[0]]
+    small = [conv_weight, conv_bias.reshape(1, -1), mix_weight, mix_bias.reshape(1, -1)]
+    small += [out_weight, out_bias.reshape(1, -1)]
     with jax.named_scope("weights"):
         weights = call(
-            functools.partial(prep_kernel, group=group, i_of=i_of),
-            [
+            functools.partial(
+                prep_kernel, group=group, channels=channels, relay=paired, i_of=i_of,
+                parity_of=parity_of,
+            ),
+            [struct((48, lon), BF)] * len(relayed[:1])
+            + [
                 struct((frames * group * hid, depth), BF),
                 struct((group * hid, group * hid), BF),
                 struct((variables * group, group * hid), BF),
                 struct((group * hid, 128), F32),
                 struct((variables * group, 128), F32),
-            ],
-            [],
-            conv_weight, conv_bias.reshape(1, -1), mix_weight, mix_bias.reshape(1, -1),
-            out_weight, out_bias.reshape(1, -1), taps,
+            ]
+            + [struct(x.shape, BF) for x in tables],
+            [pltpu.VMEM(x.shape, x.dtype) for x in small]
+            + [pltpu.VMEM(taps.shape[1:], jnp.int32), pltpu.VMEM(index.shape[1:], jnp.int32)]
+            + [pltpu.SemaphoreType.DMA((9,))],
+            *small, taps, jnp.asarray(index), *relayed, fetched=range(9),
         )
-    quarters = 8 // variables
-    width = lon // 8
-    tables = [jnp.asarray(x, BF) for x in model_tables(rows, frames, variables, quarters)]
+    if paired:
+        q_c, *weights = weights
+        pairs = swap_pairs(tiles, bands)[0]
+        late, dnear, dfar = lax.optimization_barrier((q_c, dnear, dfar))
+        r_c = lax.ppermute(late, ("tm", "lat"), pairs)
+    *w_conv, p_conv = weights[:6]
+    p_model = weights[6:]
+    with jax.named_scope("prior"):
+        prior = call(
+            functools.partial(
+                conv_kernel, frames=frames, variables=variables, group=group, chunk=256
+            ),
+            struct(background.shape, F32),
+            [pltpu.VMEM((rows // group, depth, lon), BF)],
+            p_bg, r_bg, near, far, dnear, dfar, *w_conv, p_conv,
+            cost=COST,
+        )
     tall, ctall = rows + 2 * HALO, rows + 2 * CROWS
     with jax.named_scope("model"):
-        adjoint = call(
+        return call(
             functools.partial(
-                model_kernel, rows=rows, frames=frames, variables=variables, own_bg=own_bg,
-                oth_bg=oth_bg, tile_cols=drift_east.shape[1], n_sens=sensors.shape[3],
+                model_kernel, rows=rows, frames=frames, variables=variables,
+                tile_cols=drift_east.shape[1], n_sens=sensors.shape[3],
                 paired=paired, i_of=i_of, parity_of=parity_of,
             ),
             struct(background.shape, F32),
@@ -720,18 +815,7 @@
                 pltpu.VMEM((2 * frames, tall, 8, width), F32),
                 pltpu.VMEM((2, 5, ctall, 8, width), F32),
             ],
-            *received, *sens, *tables,
-        )
-    table = jnp.asarray(conv_table(rows, frames, others, variables, group), BF)
-    with jax.named_scope("prior"):
-        return call(
-            functools.partial(
-                conv_kernel, rows=rows, frames=frames, variables=variables, own_bg=own_bg,
-                oth_bg=oth_bg, group=group, chunk=256, parity_of=parity_of,
-            ),
-            struct(background.shape, F32),
-            [pltpu.VMEM((rows // group, depth, lon), BF)],
-            *received, adjoint, table, *weights,
+            p_bg, q_c, r_c, near, far, dnear, dfar, *sens, prior, *p_model,
         )
 
 

time: 47.9 us -> 26 us (0.54); the launches traced: 47.1 us -> 25.9 us
  local copies, waits for them, and re-layouts: 13.9 us -> 0.94 us
  Pallas kernels: 22.2 us -> 13.5 us
  starting transfers between devices: 6.27 us -> 8.49 us
  waiting for transfers between devices: 4.78 us -> 2.77 us
    unnamed x40 -> x20, local copies, waits for them, and re-layouts: 13.9 us -> 0.94 us
    pallas_call x4, Pallas kernels: 22.2 us -> 13.5 us  [call(): pl.pallas_call(body, out_shape=out_shape, in_specs=[given if n in fetched...]
    ppermute x1, waiting for transfers between devices: 3.33 us -> 0.01 us  [exchange_pairs(): r_dnear = lax.ppermute(dnear, axes, diag_near)]
    ppermute x1, waiting for transfers between devices: 0.01 us -> 2.76 us  [exchange_pairs(): r_far = lax.ppermute(far, axes, next_chip)]
    ppermute x1 -> x2, starting transfers between devices: 3.03 us -> 5.13 us  [the longest x1 2.97 us: exchange_pairs(): r_bg = lax.ppermute(p_bg, axes, across)]
    ppermute x1, waiting for transfers between devices: 1.44 us -> 0.01 us  [exchange_pairs(): r_dfar = lax.ppermute(dfar, axes, diag_far)]
  transfers between devices with their start and end apart: 5 -> 6, of which waited for: 2 -> 1; matrix products, arithmetic and copies ran while one was open for 0% -> 0% of each run, Pallas kernels for 1% -> 34%
where the time goes in v1:
time: 26 us; the launch traced here: 25.9 us
  Pallas kernels  13.5 us (52%)
  starting transfers between devices  8.49 us (33%)
  waiting for transfers between devices  2.77 us (11%)
  local copies, waits for them, and re-layouts  0.94 us (4%)
    pallas_call x4, Pallas kernels, call(): pl.pallas_call(body, out_shape=out_shape, in_specs=[given if n in fetched...  13.5 us
    ppermute x1, starting transfers between devices, exchange_pairs(): r_bg = lax.ppermute(p_bg, axes, across)  2.97 us
    ppermute x1, waiting for transfers between devices, exchange_pairs(): r_far = lax.ppermute(far, axes, next_chip)  2.76 us
    ppermute x1, starting transfers between devices, shards(): r_c = lax.ppermute(late, ('tm', 'lat'), pairs)  2.16 us
    ppermute x1, starting transfers between devices, exchange_pairs(): r_dnear = lax.ppermute(dnear, axes, diag_near)  1.7 us
    ppermute x1, starting transfers between devices, exchange_pairs(): r_dfar = lax.ppermute(dfar, axes, diag_far)  1.52 us
    unnamed x20, local copies, waits for them, and re-layouts  0.94 us
  transfers between devices with their start and end apart: 6, of which 1 were waited for; matrix products, arithmetic and copies ran while one was open for 0% of the time, Pallas kernels for 34%

profile of v1, /device:TPU:0, one launch (start us, length us, event | category | flops | bytes accessed | tf_op | source)
XLA Modules:
  0.0 25.9 jit_solution(7896447823116570842)
XLA Ops:
  0.0 3.0 %collective-permute-start.2 = (bf16[64,2048]{1,0:T(8,128)(2,1)}, bf16[64,2048]{1,0:T(8,128)(2,1)S(1)}, u32[]{:S(2)}, u32[]{:S(2)}) collective-permute-start(bf16[64,2048]{1,0:T(8,128)(2,1)} %bitcast.4), channel_id=1, source_target_pairs={{0,16},{1,17},{2,18},{3,19},{4,20},{5,21},{6,22},{7,23},{8,24},{9,... | collective-permute-start | bytes 786440 | tf_op jit(solution)/shard_map/ppermute | solution.py:661
  3.0 0.0 copy-start.6
  3.0 0.0 copy-start.7
  3.0 0.0 copy-start.8
  3.0 0.0 copy-start.9
  3.0 2.1 %pack.1 = (bf16[32,2048]{1,0:T(8,128)(2,1)}, bf16[32,2048]{1,0:T(8,128)(2,1)}, bf16[32,2048]{1,0:T(8,128)(2,1)}, bf16[8,2048]{1,0:T(8,128)(2,1)}, bf16[8,2048]{1,0:T(8,128)(2,1)}) custom-call(bf16[2,2,16,2048]{3,2,1,0:T(8,128)(2,1)} %bg_in.1, f32[16,1024]{1,0:T(8,128)} %east_in.1, f32[16,1024]{1,0:T(8,128)} %north_in.1, f32[16,1024]{1,0:T(8,128)} %diff_in.1, ...), custom_call_target="tpu_custom_call" | custom-call | tf_op jit(solution)/shard_map/pack/pallas_call | solution.py:610
  5.1 0.0 copy-start
  5.1 0.1 collective-permute-start
  5.2 0.1 collective-permute-start.1
  5.2 1.7 %collective-permute-start.3 = (bf16[8,2048]{1,0:T(8,128)(2,1)}, bf16[8,2048]{1,0:T(8,128)(2,1)S(1)}, u32[]{:S(2)}, u32[]{:S(2)}) collective-permute-start(bf16[8,2048]{1,0:T(8,128)(2,1)} %get-tuple-element.35), channel_id=1, source_target_pairs={{0,17},{1,16},{2,19},{3,18},{4,21},{5,20},{6,23},{7,22},{8,25},{9,... | collective-permute-start | bytes 98312 | tf_op jit(solution)/shard_map/ppermute | solution.py:664
  7.0 1.5 %collective-permute-start.4 = (bf16[8,2048]{1,0:T(8,128)(2,1)}, bf16[8,2048]{1,0:T(8,128)(2,1)S(1)}, u32[]{:S(2)}, u32[]{:S(2)}) collective-permute-start(bf16[8,2048]{1,0:T(8,128)(2,1)} %get-tuple-element.36), channel_id=1, source_target_pairs={{0,16},{1,18},{2,17},{3,20},{4,19},{5,22},{6,21},{7,24},{8,23},{9,... | collective-permute-start | bytes 98312 | tf_op jit(solution)/shard_map/ppermute | solution.py:662
  8.5 0.0 collective-permute-done.refs_9_.near
  8.5 2.8 %collective-permute-done.1.refs_10_.far = bf16[32,2048]{1,0:T(8,128)(2,1)S(1)} collective-permute-done((bf16[32,2048]{1,0:T(8,128)(2,1)}, bf16[32,2048]{1,0:T(8,128)(2,1)S(1)}, u32[]{:S(2)}, u32[]{:S(2)}) %collective-permute-start.1) | collective-permute-done | bytes 131104 | tf_op jit(solution)/shard_map/ppermute | solution.py:663
  11.2 0.0 collective-permute-done.2.r_bg
  11.2 0.0 copy-done.2
  11.2 0.0 copy-done.3
  11.2 0.0 copy-done.4
  11.3 0.0 copy-done.5
  11.3 0.0 copy-done.6
  11.3 0.0 copy-done.7
  11.3 0.0 copy-done.8
  11.3 0.0 copy-done.9
  11.3 0.0 copy-start.1
  11.3 0.9 %copy-done.1 = bf16[32,2048]{1,0:T(8,128)(2,1)S(1)} copy-done((bf16[32,2048]{1,0:T(8,128)(2,1)S(1)}, bf16[32,2048]{1,0:T(8,128)(2,1)}, u32[]{:S(2)}) %copy-start.1) | copy-done | bytes 131096
  12.2 1.0 %weights.1 = (bf16[48,2048]{1,0:T(8,128)(2,1)S(1)}, bf16[512,256]{1,0:T(8,128)(2,1)S(1)}, bf16[256,256]{1,0:T(8,128)(2,1)S(1)}, bf16[16,256]{1,0:T(8,128)(2,1)S(...) custom-call(bf16[32,90]{1,0:T(8,128)(2,1)S(1)} %copy-done.4, ...), custom_call_target="tpu_custom_call" | custom-call | tf_op jit(solution)/shard_map/weights/pallas_call | solution.py:610
  13.2 0.0 collective-permute-done.3.dnear
  13.2 0.0 collective-permute-done.4.dfar
  13.2 2.2 %collective-permute-start.5 = (bf16[48,2048]{1,0:T(8,128)(2,1)S(1)}, bf16[48,2048]{1,0:T(8,128)(2,1)S(1)}, u32[]{:S(2)}, u32[]{:S(2)}) collective-permute-start(bf16[48,2048]{1,0:T(8,128)(2,1)S(1)} %get-tuple-element.37.q_c), channel_id=1, source_target_pairs={{0,16},{1,17},{2,18},{3,19},{4,20},{5,21},{6,22},{7,23},{8,24},{9,... | collective-permute-start | bytes 589832 | tf_op jit(solution)/shard_map/ppermute | solution.py:791
  15.4 0.0 copy-done
  15.4 5.9 %prior.1.rest_0_ = f32[2,2,16,2048]{3,2,1,0:T(8,128)S(1)} custom-call(bf16[64,2048]{1,0:T(8,128)(2,1)S(1)} %bitcast.5, bf16[64,2048]{1,0:T(8,128)(2,1)S(1)} %collective-permute-done.2.r_bg, bf16[32,2048]{1,0:T(8,128)(2,1)S(1)} %collective-permute-done.refs_9_.near, bf16[32,2048]{1,0:T(8,128)(2,1)S(1)} %collective-permute-done.1.refs_10_.far, ...), custom_call_target="tpu_custom_call" | custom-call | flops 100000000 | bytes 60000000 | tf_op jit(solution)/shard_map/prior/pallas_call | solution.py:610
  21.3 0.0 collective-permute-done.5.r_c
  21.3 4.6 %model.1 = f32[2,2,16,2048]{3,2,1,0:T(8,128)} custom-call(bf16[64,2048]{1,0:T(8,128)(2,1)S(1)} %bitcast.6, bf16[48,2048]{1,0:T(8,128)(2,1)S(1)} %get-tuple-element.37.q_c, bf16[48,2048]{1,0:T(8,128)(2,1)S(1)} %collective-permute-done.5.r_c, bf16[32,2048]{1,0:T(8,128)(2,1)S(1)} %collective-permute-done.refs_9_.near, ...), custom_call_target="tpu_custom_call" | custom-call | tf_op jit(solution)/shard_map/model/pallas_call | solution.py:610
  (4 shorter events, 0.0 us)
Async XLA Ops:
  0.0 11.2 %collective-permute-start.2 = (bf16[64,2048]{1,0:T(8,128)(2,1)}, bf16[64,2048]{1,0:T(8,128)(2,1)S(1)}, u32[]{:S(2)}, u32[]{:S(2)}) collective-permute-start(bf16[64,2048]{1,0:T(8,128)(2,1)} %bitcast.4), channel_id=1, source_target_pairs={{0,16},{1,17},{2,18},{3,19},{4,20},{5,21},{6,22},{7,23},{8,24},{9,... | collective-permute-start | bytes 786440 | tf_op jit(solution)/shard_map/ppermute | solution.py:661
  3.0 8.3 %copy-start.2 = (s32[5,8,256]{2,1,0:T(8,128)S(1)}, s32[5,8,256]{2,1,0:T(8,128)}, u32[]{:S(2)}) copy-start(s32[5,8,256]{2,1,0:T(8,128)} %constant.8.clone.refs_7_) | copy-start | bytes 122884
  3.0 8.3 %copy-start.3 = (s32[2,8,256]{2,1,0:T(8,128)S(1)}, s32[2,8,256]{2,1,0:T(8,128)}, u32[]{:S(2)}) copy-start(s32[2,8,256]{2,1,0:T(8,128)} %constant.7.clone.refs_6_) | copy-start | bytes 49156
  3.0 8.3 %copy-start.4 = (bf16[32,90]{1,0:T(8,128)(2,1)S(1)}, bf16[32,90]{1,0:T(8,128)(2,1)}, u32[]{:S(2)}) copy-start(bf16[32,90]{1,0:T(8,128)(2,1)} %refs_0_.1) | copy-start | bytes 17284
  3.0 8.3 %copy-start.5 = (bf16[32,32]{1,0:T(8,128)(2,1)S(1)}, bf16[32,32]{1,0:T(8,128)(2,1)}, u32[]{:S(2)}) copy-start(bf16[32,32]{1,0:T(8,128)(2,1)} %refs_2_.1) | copy-start | bytes 6148
  3.0 8.3 %copy-start.6 = (f32[32]{0:T(128)S(1)}, f32[32]{0:T(128)}, u32[]{:S(2)}) copy-start(f32[32]{0:T(128)} %param.17) | copy-start | bytes 388
  3.0 8.3 %copy-start.7 = (f32[32]{0:T(128)S(1)}, f32[32]{0:T(128)}, u32[]{:S(2)}) copy-start(f32[32]{0:T(128)} %param.19) | copy-start | bytes 388
  3.0 8.3 %copy-start.8 = (bf16[2,32]{1,0:T(2,128)(2,1)S(1)}, bf16[2,32]{1,0:T(2,128)(2,1)}, u32[]{:S(2)}) copy-start(bf16[2,32]{1,0:T(2,128)(2,1)} %refs_4_.1) | copy-start | bytes 388
  3.0 8.3 %copy-start.9 = (f32[2]{0:T(128)S(1)}, f32[2]{0:T(128)}, u32[]{:S(2)}) copy-start(f32[2]{0:T(128)} %param.21) | copy-start | bytes 28
  5.1 10.3 %copy-start = (bf16[2,2,16,2048]{3,2,1,0:T(8,128)(2,1)S(1)}, bf16[2,2,16,2048]{3,2,1,0:T(8,128)(2,1)}, u32[]{:S(2)}) copy-start(bf16[2,2,16,2048]{3,2,1,0:T(8,128)(2,1)} %bg_in.1) | copy-start | bytes 786436
  5.1 3.4 %collective-permute-start = (bf16[32,2048]{1,0:T(8,128)(2,1)}, bf16[32,2048]{1,0:T(8,128)(2,1)S(1)}, u32[]{:S(2)}, u32[]{:S(2)}) collective-permute-start(bf16[32,2048]{1,0:T(8,128)(2,1)} %get-tuple-element.30), channel_id=1, source_target_pairs={{0,1},{1,0},{2,3},{3,2},{4,5},{5,4},{6,7},{7,6},{8,9},{9,8},{10,11... | collective-permute-start | bytes 393224 | tf_op jit(solution)/shard_map/ppermute | solution.py:665
  5.2 6.1 %collective-permute-start.1 = (bf16[32,2048]{1,0:T(8,128)(2,1)}, bf16[32,2048]{1,0:T(8,128)(2,1)S(1)}, u32[]{:S(2)}, u32[]{:S(2)}) collective-permute-start(bf16[32,2048]{1,0:T(8,128)(2,1)} %get-tuple-element.31), channel_id=1, source_target_pairs={{0,16},{1,2},{2,1},{3,4},{4,3},{5,6},{6,5},{7,8},{8,7},{9,10},{10,... | collective-permute-start | bytes 393224 | tf_op jit(solution)/shard_map/ppermute | solution.py:663
  5.2 7.9 %collective-permute-start.3 = (bf16[8,2048]{1,0:T(8,128)(2,1)}, bf16[8,2048]{1,0:T(8,128)(2,1)S(1)}, u32[]{:S(2)}, u32[]{:S(2)}) collective-permute-start(bf16[8,2048]{1,0:T(8,128)(2,1)} %get-tuple-element.35), channel_id=1, source_target_pairs={{0,17},{1,16},{2,19},{3,18},{4,21},{5,20},{6,23},{7,22},{8,25},{9,... | collective-permute-start | bytes 98312 | tf_op jit(solution)/shard_map/ppermute | solution.py:664
  7.0 6.2 %collective-permute-start.4 = (bf16[8,2048]{1,0:T(8,128)(2,1)}, bf16[8,2048]{1,0:T(8,128)(2,1)S(1)}, u32[]{:S(2)}, u32[]{:S(2)}) collective-permute-start(bf16[8,2048]{1,0:T(8,128)(2,1)} %get-tuple-element.36), channel_id=1, source_target_pairs={{0,16},{1,18},{2,17},{3,20},{4,19},{5,22},{6,21},{7,24},{8,23},{9,... | collective-permute-start | bytes 98312 | tf_op jit(solution)/shard_map/ppermute | solution.py:662
  11.3 0.9 %copy-start.1 = (bf16[32,2048]{1,0:T(8,128)(2,1)S(1)}, bf16[32,2048]{1,0:T(8,128)(2,1)}, u32[]{:S(2)}) copy-start(bf16[32,2048]{1,0:T(8,128)(2,1)} %get-tuple-element.29.refs_8_) | copy-start | bytes 393220
  13.2 8.0 %collective-permute-start.5 = (bf16[48,2048]{1,0:T(8,128)(2,1)S(1)}, bf16[48,2048]{1,0:T(8,128)(2,1)S(1)}, u32[]{:S(2)}, u32[]{:S(2)}) collective-permute-start(bf16[48,2048]{1,0:T(8,128)(2,1)S(1)} %get-tuple-element.37.q_c), channel_id=1, source_target_pairs={{0,16},{1,17},{2,18},{3,19},{4,20},{5,21},{6,22},{7,23},{8,24},{9,... | collective-permute-start | bytes 589832 | tf_op jit(solution)/shard_map/ppermute | solution.py:791

commit v2 on v1

--- a/solution.py
+++ b/solution.py
@@ -244,20 +244,20 @@
         dfar[:, cut] = message[72:80]
 
 
-def prep_kernel(*refs, group, channels, relay, i_of, parity_of):
+def relay_kernel(near, far, out):
+    edge = near.shape[0] - 8
+    out[0:8, :] = near[edge : edge + 8, :]
+    out[8:16, :] = far[edge : edge + 8, :]
+
+
+def prep_kernel(*refs, group, channels, i_of, parity_of):
     sources, rest = refs[:8], refs[8:]
-    if relay:
-        p_c, near, far, q_c, *rest = rest
     w1, w2, w3, b2, b3, p_conv, p_own, p_coef, p_out, p_halo, p_chalo, p_ohalo = rest[:12]
     conv_w, conv_b, mix_w, mix_b, out_w, out_b, taps, index, sems = rest[12:]
     hid = mix_w.shape[0]
     case = case_of(parity_of(), lax.axis_index("lat"), lax.axis_size("lat"))
     moves = [*zip(sources[:6], (conv_w, conv_b, mix_w, mix_b, out_w, out_b))]
     moves += [(sources[6].at[i_of()], taps), (sources[7].at[case], index)]
-    if relay:
-        moves.append((p_c, q_c.at[0:32]))
-        q_c[32:40, :] = near[24:32, :]
-        q_c[40:48, :] = far[24:32, :]
     fetch(moves, sems)
     columns = index[...].astype(F32).T
 
@@ -329,7 +329,7 @@
 
 
 def model_kernel(
-    p_bg, q_c, r_c, near, far, dnear, dfar, *rest,
+    p_bg, p_c, r_c, r_e, near, far, dnear, dfar, *rest,
     rows, frames, variables, tile_cols, n_sens, paired, i_of, parity_of,
 ):
     sens = None if paired else rest[0]
@@ -361,7 +361,7 @@
 
     ctall = rows + 2 * CROWS
     for source in range(2):
-        big = q_c if source == 0 else r_c
+        big = p_c if source == 0 else r_c
         spot = me_t if source == 0 else 1 - me_t
         pieces = []
         for side in range(2):
@@ -377,7 +377,7 @@
         kk = dot(scaled, pieces[2]).reshape(rows, 8, width) + K_MID
         rim = []
         for q in range(quarters):
-            for message in (near[16:32], far[16:32]) if source == 0 else (r_c[32:48],):
+            for message in (near[16:32], far[16:32]) if source == 0 else (r_e,):
                 for side in range(2):
                     cut = slice(side * half + q * width, side * half + (q + 1) * width)
                     rim.append(message[:, cut])
@@ -477,7 +477,7 @@
             return [sens[...].astype(F32)[first + n : first + n + 1] for n in range(count)]
         if band in (1, 3):
             at = slice(rows, rows + 16)
-            mine, other = q_c[at, half:lon].astype(F32), r_c[at, half:lon].astype(F32)
+            mine, other = p_c[at, half:lon].astype(F32), r_c[at, half:lon].astype(F32)
             n = 14 if band == 1 else 12
             return [jnp.where(me_t == h, mine[n : n + 1], other[n + 1 : n + 2])]
         from_far = parity == (0 if band == 0 else 1)
@@ -588,17 +588,19 @@
     hidden = w2.shape[0]
     bias2, bias3 = widen(b2[...], chunk), widen(b3[...], chunk)
     pending = []
+    wide2 = jnp.concatenate([bias2] * frames, axis=1)
     for n in range(lon // chunk):
         cut = slice(n * chunk, (n + 1) * chunk)
         for g in range(groups):
             first = dot(w1[...], window[g, :, cut])
-            for t in range(frames):
-                one = gelu(first[t * hidden : (t + 1) * hidden])
-                pending.append((t, g, cut, gelu(dot(w2[...], one) + bias2)))
-    for t, g, cut, two in pending:
-        score = dot(w3[...], two) + bias3
-        for v in range(variables):
-            out[t, v, g * group : (g + 1) * group, cut] = score[v * group : (v + 1) * group]
+            one = [gelu(first[t * hidden : (t + 1) * hidden]) for t in range(frames)]
+            pending.append((g, cut, gelu(dot(w2[...], jnp.concatenate(one, axis=1)) + wide2)))
+    for g, cut, two in pending:
+        scores = dot(w3[...], two)
+        for t in range(frames):
+            score = scores[:, t * chunk : (t + 1) * chunk] + bias3
+            for v in range(variables):
+                out[t, v, g * group : (g + 1) * group, cut] = score[v * group : (v + 1) * group]
 
 
 def call(body, out_shape, scratch, *args, fetched=(), limit=VMEM_BYTES, cost=None):
@@ -720,9 +722,9 @@
         diagonal = lax.ppermute(edge_fields(around, 1, bottom), "lat", pairs)
         received.append((message, diagonal, lax.ppermute(edge_coefs(1, bottom), "lat", pairs)))
     (near, dnear, c_near), (far, dfar, c_far) = received
-    r_c = jnp.concatenate([block(1), c_near, c_far], axis=0)
+    r_e = jnp.concatenate([c_near, c_far], axis=0)
     p_bg, r_bg = background.reshape(-1, lon), around.reshape(-1, lon)
-    return p_bg, r_bg, block(0), r_c, near, far, dnear, dfar, sens
+    return p_bg, r_bg, block(0), block(1), r_e, near, far, dnear, dfar, sens
 
 
 def shards(
@@ -741,14 +743,13 @@
         offsets = [[*range(2 * frames)], [*range(frames), *range(-frames, 0)]]
         i_of = lambda: lax.axis_index("tm")
         parity_of = lambda: lax.axis_index("lat") % 2
-        near, far, r_bg = lax.optimization_barrier((near, far, r_bg))
-        relayed, sens = (p_c, near, far), ()
+        sens = ()
     else:
-        p_bg, r_bg, q_c, r_c, near, far, dnear, dfar, sens = exchange_gathered(*arrays)
+        p_bg, r_bg, p_c, r_c, r_e, near, far, dnear, dfar, sens = exchange_gathered(*arrays)
         offsets = [[*range(frames), *range(-frames, 0), *range(frames, 2 * frames)]]
         i_of = lambda: 0
         parity_of = lambda: 0
-        relayed, sens = (), (sens,)
+        sens = (sens,)
     others = len(offsets[0]) - frames
 
     channels = (frames + others) * variables
@@ -767,11 +768,9 @@
     with jax.named_scope("weights"):
         weights = call(
             functools.partial(
-                prep_kernel, group=group, channels=channels, relay=paired, i_of=i_of,
-                parity_of=parity_of,
+                prep_kernel, group=group, channels=channels, i_of=i_of, parity_of=parity_of
             ),
-            [struct((48, lon), BF)] * len(relayed[:1])
-            + [
+            [
                 struct((frames * group * hid, depth), BF),
                 struct((group * hid, group * hid), BF),
                 struct((variables * group, group * hid), BF),
@@ -781,14 +780,17 @@
             + [struct(x.shape, BF) for x in tables],
             [pltpu.VMEM(x.shape, x.dtype) for x in small]
             + [pltpu.VMEM(taps.shape[1:], jnp.int32), pltpu.VMEM(index.shape[1:], jnp.int32)]
-            + [pltpu.SemaphoreType.DMA((9,))],
-            *small, taps, jnp.asarray(index), *relayed, fetched=range(9),
+            + [pltpu.SemaphoreType.DMA((8,))],
+            *small, taps, jnp.asarray(index), fetched=range(8),
         )
     if paired:
-        q_c, *weights = weights
+        *weights, near, far, r_bg = lax.optimization_barrier((*weights, near, far, r_bg))
+        with jax.named_scope("relay"):
+            edges = call(relay_kernel, struct((16, lon), BF), [], near, far)
         pairs = swap_pairs(tiles, bands)[0]
-        late, dnear, dfar = lax.optimization_barrier((q_c, dnear, dfar))
+        late, edges, dnear, dfar = lax.optimization_barrier((p_c, edges, dnear, dfar))
         r_c = lax.ppermute(late, ("tm", "lat"), pairs)
+        r_e = lax.ppermute(edges, ("tm", "lat"), pairs)
     *w_conv, p_conv = weights[:6]
     p_model = weights[6:]
     with jax.named_scope("prior"):
@@ -815,7 +817,7 @@
                 pltpu.VMEM((2 * frames, tall, 8, width), F32),
                 pltpu.VMEM((2, 5, ctall, 8, width), F32),
             ],
-            p_bg, q_c, r_c, near, far, dnear, dfar, *sens, prior, *p_model,
+            p_bg, p_c, r_c, r_e, near, far, dnear, dfar, *sens, prior, *p_model,
         )
 
 

time: 26 us -> 24.7 us (0.950)
  local copies, waits for them, and re-layouts: 0.94 us -> 0.04 us
  Pallas kernels: 13.5 us -> 13.1 us
    ppermute x1, waiting for transfers between devices: 0.01 us -> 0.98 us  [exchange_pairs(): r_dfar = lax.ppermute(dfar, axes, diag_far)]
    unnamed x20, local copies, waits for them, and re-layouts: 0.94 us -> 0.04 us
    ppermute x1, waiting for transfers between devices: 2.76 us -> 1.87 us  [exchange_pairs(): r_far = lax.ppermute(far, axes, next_chip)]
    pallas_call x4 -> x5, Pallas kernels: 13.5 us -> 13.1 us  [call(): pl.pallas_call(body, out_shape=out_shape, in_specs=[given if n in fetched...]
  transfers between devices with their start and end apart: 6 -> 7, of which waited for: 1 -> 3; matrix products, arithmetic and copies ran while one was open for 0% -> 0% of each run, Pallas kernels for 34% -> 35%
where the time goes in v2:
time: 24.7 us; the launch traced here: 24.5 us
  Pallas kernels  13.1 us (53%)
  starting transfers between devices  8.36 us (34%)
  waiting for transfers between devices  2.92 us (12%)
    pallas_call x5, Pallas kernels, call(): pl.pallas_call(body, out_shape=out_shape, in_specs=[given if n in fetched...  13.1 us
    ppermute x1, starting transfers between devices, exchange_pairs(): r_bg = lax.ppermute(p_bg, axes, across)  2.97 us
    ppermute x1, starting transfers between devices, shards(): r_c = lax.ppermute(late, ('tm', 'lat'), pairs)  1.95 us
    ppermute x1, waiting for transfers between devices, exchange_pairs(): r_far = lax.ppermute(far, axes, next_chip)  1.87 us
    ppermute x1, starting transfers between devices, exchange_pairs(): r_dnear = lax.ppermute(dnear, axes, diag_near)  1.7 us
    ppermute x1, starting transfers between devices, exchange_pairs(): r_dfar = lax.ppermute(dfar, axes, diag_far)  1.52 us
    ppermute x1, waiting for transfers between devices, exchange_pairs(): r_dfar = lax.ppermute(dfar, axes, diag_far)  0.98 us
  transfers between devices with their start and end apart: 7, of which 3 were waited for; matrix products, arithmetic and copies ran while one was open for 0% of the time, Pallas kernels for 35%

profile of v2, /device:TPU:0, one launch (start us, length us, event | category | flops | bytes accessed | tf_op | source)
XLA Modules:
  0.0 24.5 jit_solution(6281861324978362133)
XLA Ops:
  0.0 3.0 %collective-permute-start.2 = (bf16[64,2048]{1,0:T(8,128)(2,1)}, bf16[64,2048]{1,0:T(8,128)(2,1)S(1)}, u32[]{:S(2)}, u32[]{:S(2)}) collective-permute-start(bf16[64,2048]{1,0:T(8,128)(2,1)} %bitcast.4), channel_id=1, source_target_pairs={{0,16},{1,17},{2,18},{3,19},{4,20},{5,21},{6,22},{7,23},{8,24},{9,... | collective-permute-start | bytes 786440 | tf_op jit(solution)/shard_map/ppermute | solution.py:663
  3.0 0.0 copy-start.6
  3.0 0.0 copy-start.7
  3.0 0.0 copy-start.8
  3.0 0.0 copy-start.9
  3.0 2.1 %pack.1 = (bf16[32,2048]{1,0:T(8,128)(2,1)}, bf16[32,2048]{1,0:T(8,128)(2,1)}, bf16[32,2048]{1,0:T(8,128)(2,1)}, bf16[8,2048]{1,0:T(8,128)(2,1)}, bf16[8,2048]{1,0:T(8,128)(2,1)}) custom-call(bf16[2,2,16,2048]{3,2,1,0:T(8,128)(2,1)} %bg_in.1, f32[16,1024]{1,0:T(8,128)} %east_in.1, f32[16,1024]{1,0:T(8,128)} %north_in.1, f32[16,1024]{1,0:T(8,128)} %diff_in.1, ...), custom_call_target="tpu_custom_call" | custom-call | tf_op jit(solution)/shard_map/pack/pallas_call | solution.py:612
  5.1 0.0 copy-start
  5.1 0.1 collective-permute-start
  5.2 0.1 collective-permute-start.1
  5.3 1.7 %collective-permute-start.3 = (bf16[8,2048]{1,0:T(8,128)(2,1)}, bf16[8,2048]{1,0:T(8,128)(2,1)S(1)}, u32[]{:S(2)}, u32[]{:S(2)}) collective-permute-start(bf16[8,2048]{1,0:T(8,128)(2,1)} %get-tuple-element.58), channel_id=1, source_target_pairs={{0,17},{1,16},{2,19},{3,18},{4,21},{5,20},{6,23},{7,22},{8,25},{9,... | collective-permute-start | bytes 98312 | tf_op jit(solution)/shard_map/ppermute | solution.py:666
  7.0 1.5 %collective-permute-start.4 = (bf16[8,2048]{1,0:T(8,128)(2,1)}, bf16[8,2048]{1,0:T(8,128)(2,1)S(1)}, u32[]{:S(2)}, u32[]{:S(2)}) collective-permute-start(bf16[8,2048]{1,0:T(8,128)(2,1)} %get-tuple-element.59), channel_id=1, source_target_pairs={{0,16},{1,18},{2,17},{3,20},{4,19},{5,22},{6,21},{7,24},{8,23},{9,... | collective-permute-start | bytes 98312 | tf_op jit(solution)/shard_map/ppermute | solution.py:664
  8.5 0.0 copy-done.2
  8.5 0.0 copy-done.3
  8.5 0.0 copy-done.4
  8.5 0.0 copy-done.5
  8.5 0.0 copy-done.6
  8.5 0.0 copy-done.7
  8.5 0.0 copy-done.8
  8.5 0.8 %weights.1 = (bf16[512,256]{1,0:T(8,128)(2,1)S(1)}, bf16[256,256]{1,0:T(8,128)(2,1)S(1)}, bf16[16,256]{1,0:T(8,128)(2,1)S(1)}, f32[256,128]{1,0:T(8,128)S(1)}, f...) custom-call(bf16[32,90]{1,0:T(8,128)(2,1)S(1)} %copy-done.4, ...), custom_call_target="tpu_custom_call" | custom-call | tf_op jit(solution)/shard_map/weights/pallas_call | solution.py:612
  9.4 0.0 collective-permute-done.near
  9.4 1.9 %collective-permute-done.1.far = bf16[32,2048]{1,0:T(8,128)(2,1)S(1)} collective-permute-done((bf16[32,2048]{1,0:T(8,128)(2,1)}, bf16[32,2048]{1,0:T(8,128)(2,1)S(1)}, u32[]{:S(2)}, u32[]{:S(2)}) %collective-permute-start.1) | collective-permute-done | bytes 131104 | tf_op jit(solution)/shard_map/ppermute | solution.py:665
  11.2 0.0 collective-permute-done.2.r_bg
  11.3 0.1 collective-permute-done.3.dnear
  11.3 1.0 %collective-permute-done.4.dfar = bf16[8,2048]{1,0:T(8,128)(2,1)S(1)} collective-permute-done((bf16[8,2048]{1,0:T(8,128)(2,1)}, bf16[8,2048]{1,0:T(8,128)(2,1)S(1)}, u32[]{:S(2)}, u32[]{:S(2)}) %collective-permute-start.4) | collective-permute-done | bytes 32800 | tf_op jit(solution)/shard_map/ppermute | solution.py:664
  12.3 0.0 copy-done.1
  12.3 1.9 %collective-permute-start.5 = (bf16[32,2048]{1,0:T(8,128)(2,1)S(1)}, bf16[32,2048]{1,0:T(8,128)(2,1)S(1)}, u32[]{:S(2)}, u32[]{:S(2)}) collective-permute-start(bf16[32,2048]{1,0:T(8,128)(2,1)S(1)} %copy-done.1), channel_id=1, source_target_pairs={{0,16},{1,17},{2,18},{3,19},{4,20},{5,21},{6,22},{7,23},{8,24},{9,... | collective-permute-start | bytes 393224 | tf_op jit(solution)/shard_map/ppermute | solution.py:792
  14.2 0.1 collective-permute-start.6
  14.3 0.0 copy-done
  14.3 5.6 %prior.1.rest_0_ = f32[2,2,16,2048]{3,2,1,0:T(8,128)S(1)} custom-call(bf16[64,2048]{1,0:T(8,128)(2,1)S(1)} %bitcast.5, bf16[64,2048]{1,0:T(8,128)(2,1)S(1)} %collective-permute-done.2.r_bg, bf16[32,2048]{1,0:T(8,128)(2,1)S(1)} %collective-permute-done.near, bf16[32,2048]{1,0:T(8,128)(2,1)S(1)} %collective-permute-done.1.far, ...), custom_call_target="tpu_custom_call" | custom-call | flops 100000000 | bytes 60000000 | tf_op jit(solution)/shard_map/prior/pallas_call | solution.py:612
  19.9 0.0 collective-permute-done.6.r_e
  19.9 0.0 collective-permute-done.5.r_c
  20.0 4.6 %model.1 = f32[2,2,16,2048]{3,2,1,0:T(8,128)} custom-call(bf16[64,2048]{1,0:T(8,128)(2,1)S(1)} %bitcast.6, bf16[32,2048]{1,0:T(8,128)(2,1)S(1)} %copy-done.1, bf16[32,2048]{1,0:T(8,128)(2,1)S(1)} %collective-permute-done.5.r_c, bf16[16,2048]{1,0:T(8,128)(2,1)S(1)} %collective-permute-done.6.r_e, bf16[32,2048]{1,0:T(8,128)(2,1)S(1)} %collective-permute-done.near, ...), custom_call_target="tpu_custom_call" | custom-call | tf_op jit(solution)/shard_map/model/pallas_call | solution.py:612
  (7 shorter events, 0.0 us)
Async XLA Ops:
  0.0 11.2 %collective-permute-start.2 = (bf16[64,2048]{1,0:T(8,128)(2,1)}, bf16[64,2048]{1,0:T(8,128)(2,1)S(1)}, u32[]{:S(2)}, u32[]{:S(2)}) collective-permute-start(bf16[64,2048]{1,0:T(8,128)(2,1)} %bitcast.4), channel_id=1, source_target_pairs={{0,16},{1,17},{2,18},{3,19},{4,20},{5,21},{6,22},{7,23},{8,24},{9,... | collective-permute-start | bytes 786440 | tf_op jit(solution)/shard_map/ppermute | solution.py:663
  3.0 5.5 %copy-start.2 = (s32[5,8,256]{2,1,0:T(8,128)S(1)}, s32[5,8,256]{2,1,0:T(8,128)}, u32[]{:S(2)}) copy-start(s32[5,8,256]{2,1,0:T(8,128)} %constant.8.clone.refs_7_) | copy-start | bytes 122884
  3.0 5.5 %copy-start.3 = (s32[2,8,256]{2,1,0:T(8,128)S(1)}, s32[2,8,256]{2,1,0:T(8,128)}, u32[]{:S(2)}) copy-start(s32[2,8,256]{2,1,0:T(8,128)} %constant.7.clone.refs_6_) | copy-start | bytes 49156
  3.0 5.5 %copy-start.4 = (bf16[32,90]{1,0:T(8,128)(2,1)S(1)}, bf16[32,90]{1,0:T(8,128)(2,1)}, u32[]{:S(2)}) copy-start(bf16[32,90]{1,0:T(8,128)(2,1)} %refs_0_.1) | copy-start | bytes 17284
  3.0 5.5 %copy-start.5 = (bf16[32,32]{1,0:T(8,128)(2,1)S(1)}, bf16[32,32]{1,0:T(8,128)(2,1)}, u32[]{:S(2)}) copy-start(bf16[32,32]{1,0:T(8,128)(2,1)} %refs_2_.1) | copy-start | bytes 6148
  3.0 5.5 %copy-start.6 = (f32[32]{0:T(128)S(1)}, f32[32]{0:T(128)}, u32[]{:S(2)}) copy-start(f32[32]{0:T(128)} %param.17) | copy-start | bytes 388
  3.0 5.5 %copy-start.7 = (f32[32]{0:T(128)S(1)}, f32[32]{0:T(128)}, u32[]{:S(2)}) copy-start(f32[32]{0:T(128)} %param.19) | copy-start | bytes 388
  3.0 5.5 %copy-start.8 = (bf16[2,32]{1,0:T(2,128)(2,1)S(1)}, bf16[2,32]{1,0:T(2,128)(2,1)}, u32[]{:S(2)}) copy-start(bf16[2,32]{1,0:T(2,128)(2,1)} %refs_4_.1) | copy-start | bytes 388
  3.0 5.5 %copy-start.9 = (f32[2]{0:T(128)S(1)}, f32[2]{0:T(128)}, u32[]{:S(2)}) copy-start(f32[2]{0:T(128)} %param.21) | copy-start | bytes 28
  5.1 9.2 %copy-start = (bf16[2,2,16,2048]{3,2,1,0:T(8,128)(2,1)S(1)}, bf16[2,2,16,2048]{3,2,1,0:T(8,128)(2,1)}, u32[]{:S(2)}) copy-start(bf16[2,2,16,2048]{3,2,1,0:T(8,128)(2,1)} %bg_in.1) | copy-start | bytes 786436
  5.1 4.3 %collective-permute-start = (bf16[32,2048]{1,0:T(8,128)(2,1)}, bf16[32,2048]{1,0:T(8,128)(2,1)S(1)}, u32[]{:S(2)}, u32[]{:S(2)}) collective-permute-start(bf16[32,2048]{1,0:T(8,128)(2,1)} %get-tuple-element.54), channel_id=1, source_target_pairs={{0,1},{1,0},{2,3},{3,2},{4,5},{5,4},{6,7},{7,6},{8,9},{9,8},{10,11... | collective-permute-start | bytes 393224 | tf_op jit(solution)/shard_map/ppermute | solution.py:667
  5.2 6.0 %collective-permute-start.1 = (bf16[32,2048]{1,0:T(8,128)(2,1)}, bf16[32,2048]{1,0:T(8,128)(2,1)S(1)}, u32[]{:S(2)}, u32[]{:S(2)}) collective-permute-start(bf16[32,2048]{1,0:T(8,128)(2,1)} %get-tuple-element.55), channel_id=1, source_target_pairs={{0,16},{1,2},{2,1},{3,4},{4,3},{5,6},{6,5},{7,8},{8,7},{9,10},{10,... | collective-permute-start | bytes 393224 | tf_op jit(solution)/shard_map/ppermute | solution.py:665
  5.3 6.0 %collective-permute-start.3 = (bf16[8,2048]{1,0:T(8,128)(2,1)}, bf16[8,2048]{1,0:T(8,128)(2,1)S(1)}, u32[]{:S(2)}, u32[]{:S(2)}) collective-permute-start(bf16[8,2048]{1,0:T(8,128)(2,1)} %get-tuple-element.58), channel_id=1, source_target_pairs={{0,17},{1,16},{2,19},{3,18},{4,21},{5,20},{6,23},{7,22},{8,25},{9,... | collective-permute-start | bytes 98312 | tf_op jit(solution)/shard_map/ppermute | solution.py:666
  7.0 5.3 %collective-permute-start.4 = (bf16[8,2048]{1,0:T(8,128)(2,1)}, bf16[8,2048]{1,0:T(8,128)(2,1)S(1)}, u32[]{:S(2)}, u32[]{:S(2)}) collective-permute-start(bf16[8,2048]{1,0:T(8,128)(2,1)} %get-tuple-element.59), channel_id=1, source_target_pairs={{0,16},{1,18},{2,17},{3,20},{4,19},{5,22},{6,21},{7,24},{8,23},{9,... | collective-permute-start | bytes 98312 | tf_op jit(solution)/shard_map/ppermute | solution.py:664
  11.2 1.1 %copy-start.1 = (bf16[32,2048]{1,0:T(8,128)(2,1)S(1)}, bf16[32,2048]{1,0:T(8,128)(2,1)}, u32[]{:S(2)}) copy-start(bf16[32,2048]{1,0:T(8,128)(2,1)} %get-tuple-element.60.p_c) | copy-start | bytes 393220
  12.3 7.7 %collective-permute-start.5 = (bf16[32,2048]{1,0:T(8,128)(2,1)S(1)}, bf16[32,2048]{1,0:T(8,128)(2,1)S(1)}, u32[]{:S(2)}, u32[]{:S(2)}) collective-permute-start(bf16[32,2048]{1,0:T(8,128)(2,1)S(1)} %copy-done.1), channel_id=1, source_target_pairs={{0,16},{1,17},{2,18},{3,19},{4,20},{5,21},{6,22},{7,23},{8,24},{9,... | collective-permute-start | bytes 393224 | tf_op jit(solution)/shard_map/ppermute | solution.py:792
  14.2 5.7 %collective-permute-start.6 = (bf16[16,2048]{1,0:T(8,128)(2,1)S(1)}, bf16[16,2048]{1,0:T(8,128)(2,1)S(1)}, u32[]{:S(2)}, u32[]{:S(2)}) collective-permute-start(bf16[16,2048]{1,0:T(8,128)(2,1)S(1)} %relay.1), channel_id=1, source_target_pairs={{0,16},{1,17},{2,18},{3,19},{4,20},{5,21},{6,22},{7,23},{8,24},{9,... | collective-permute-start | bytes 196616 | tf_op jit(solution)/shard_map/ppermute | solution.py:793

commit v3 on v2

--- a/solution.py
+++ b/solution.py
@@ -244,7 +244,7 @@
         dfar[:, cut] = message[72:80]
 
 
-def relay_kernel(near, far, out):
+def relay_kernel(far, near, out):
     edge = near.shape[0] - 8
     out[0:8, :] = near[edge : edge + 8, :]
     out[8:16, :] = far[edge : edge + 8, :]
@@ -506,10 +506,12 @@
     def assimilate(g, row_list, where_row, quarter, lane_of, values):
         total = where_row.shape[1]
         lanes_bf = lax.broadcasted_iota(jnp.int32, (width, total), 0).astype(F32).astype(BF)
-        onehot = jnp.where(lanes_bf == lane_of.astype(F32).astype(BF), BF(1), BF(0))
+        apart = jnp.abs(lanes_bf - lane_of.astype(F32).astype(BF))
+        onehot = jnp.maximum(BF(1) - apart, BF(0))
         stack = jnp.concatenate([forecast[g, HALO + r] for r in row_list], axis=0)
-        high, low = split2(stack)
-        picked = dot(high, onehot) + dot(low, onehot)
+        size = 8 * len(row_list)
+        picked = dot(jnp.concatenate(split2(stack), axis=0), onehot)
+        picked = picked[:size] + picked[size:]
         shape = (8, total)
         here_q = (lax.broadcasted_iota(jnp.int32, shape, 0) >> (variables.bit_length() - 1)) == quarter
         variable = lax.broadcasted_iota(jnp.int32, shape, 0) & (variables - 1)
@@ -522,8 +524,8 @@
         misfit = jnp.where(here_q, misfit - target, 0.0)
         row_f = where_row.astype(F32)
         weighted = jnp.concatenate([jnp.where(row_f == float(r), misfit, 0.0) for r in row_list], axis=0)
-        high, low = split2(weighted)
-        return (dot_t(high, onehot) + dot_t(low, onehot)).reshape(len(row_list), 8, width)
+        sums = dot_t(jnp.concatenate(split2(weighted), axis=0), onehot)
+        return (sums[:size] + sums[size:]).reshape(len(row_list), 8, width)
 
     far_away = -(1 << 20)
     for t in range(frames):
@@ -545,11 +547,12 @@
         low = HALO - SUB + step + 1
         backward(buffers[step % 2], buffers[(step + 1) % 2], low, tall - low)
     result = buffers[SUB % 2]
+    twice = jnp.concatenate([p_out[...], p_out[...]], axis=1)
 
     for t in range(frames):
         for h in range(2):
-            high, low = split2(result[t * 2 + h, HALO : HALO + rows].reshape(rows * 8, width))
-            back = dot(p_out[...], high) + dot(p_out[...], low)
+            parts = split2(result[t * 2 + h, HALO : HALO + rows].reshape(rows * 8, width))
+            back = dot(twice, jnp.concatenate(parts, axis=0))
             for q in range(quarters):
                 cut = slice(h * half + q * width, h * half + (q + 1) * width)
                 for v in range(variables):
@@ -564,9 +567,10 @@
 
 def shifted(chosen, window, depth):
     tall, lon = chosen.shape
-    window[0:tall] = pltpu.roll(chosen, 1, 1).astype(BF)
-    window[tall : 2 * tall] = chosen.astype(BF)
-    window[2 * tall : 3 * tall] = pltpu.roll(chosen, lon - 1, 1).astype(BF)
+    packed = chosen.astype(BF)
+    window[0:tall] = pltpu.roll(packed, 1, 1)
+    window[tall : 2 * tall] = packed
+    window[2 * tall : 3 * tall] = pltpu.roll(packed, lon - 1, 1)
     ones = lax.broadcasted_iota(jnp.int32, (depth - 3 * tall, lon), 0) < 3
     window[3 * tall : depth] = jnp.where(ones, 1.0, 0.0).astype(BF)
 
@@ -784,11 +788,11 @@
             *small, taps, jnp.asarray(index), fetched=range(8),
         )
     if paired:
-        *weights, near, far, r_bg = lax.optimization_barrier((*weights, near, far, r_bg))
+        far, near, r_bg, *weights = lax.optimization_barrier((far, near, r_bg, *weights))
         with jax.named_scope("relay"):
-            edges = call(relay_kernel, struct((16, lon), BF), [], near, far)
+            edges = call(relay_kernel, struct((16, lon), BF), [], far, near)
         pairs = swap_pairs(tiles, bands)[0]
-        late, edges, dnear, dfar = lax.optimization_barrier((p_c, edges, dnear, dfar))
+        dfar, dnear, late, edges = lax.optimization_barrier((dfar, dnear, p_c, edges))
         r_c = lax.ppermute(late, ("tm", "lat"), pairs)
         r_e = lax.ppermute(edges, ("tm", "lat"), pairs)
     *w_conv, p_conv = weights[:6]

time: 24.7 us -> 24.4 us (0.988)
  waiting for transfers between devices: 2.92 us -> 1.7 us
  starting transfers between devices: 8.36 us -> 9.55 us
  Pallas kernels: 13.1 us -> 12.8 us
    ppermute x1, starting transfers between devices: 0.07 us -> 1.59 us  [exchange_pairs(): r_near = lax.ppermute(near, axes, on_chip)]
    ppermute x1, waiting for transfers between devices: 1.87 us -> 0.57 us  [exchange_pairs(): r_far = lax.ppermute(far, axes, next_chip)]
    ppermute x1, starting transfers between devices: 1.52 us -> 0.51 us  [exchange_pairs(): r_dfar = lax.ppermute(dfar, axes, diag_far)]
    ppermute x1, starting transfers between devices: 1.7 us -> 2.22 us  [exchange_pairs(): r_dnear = lax.ppermute(dnear, axes, diag_near)]
    pallas_call x5, Pallas kernels: 13.1 us -> 12.8 us  [call(): pl.pallas_call(body, out_shape=out_shape, in_specs=[given if n in fetched...]
  transfers between devices with their start and end apart: 7 -> 7, of which waited for: 3 -> 3; matrix products, arithmetic and copies ran while one was open for 0% -> 0% of each run, Pallas kernels for 35% -> 34%
where the time goes in v3:
time: 24.4 us; the launch traced here: 24.2 us
  Pallas kernels  12.8 us (52%)
  starting transfers between devices  9.55 us (39%)
  waiting for transfers between devices  1.7 us (7%)
    pallas_call x5, Pallas kernels, call(): pl.pallas_call(body, out_shape=out_shape, in_specs=[given if n in fetched...  12.8 us
    ppermute x1, starting transfers between devices, exchange_pairs(): r_bg = lax.ppermute(p_bg, axes, across)  2.97 us
    ppermute x1, starting transfers between devices, exchange_pairs(): r_dnear = lax.ppermute(dnear, axes, diag_near)  2.22 us
    ppermute x1, starting transfers between devices, shards(): r_c = lax.ppermute(late, ('tm', 'lat'), pairs)  2.16 us
    ppermute x1, starting transfers between devices, exchange_pairs(): r_near = lax.ppermute(near, axes, on_chip)  1.59 us
    ppermute x1, waiting for transfers between devices, exchange_pairs(): r_dfar = lax.ppermute(dfar, axes, diag_far)  0.81 us
    ppermute x1, waiting for transfers between devices, exchange_pairs(): r_far = lax.ppermute(far, axes, next_chip)  0.57 us
    ppermute x1, starting transfers between devices, exchange_pairs(): r_dfar = lax.ppermute(dfar, axes, diag_far)  0.51 us
  transfers between devices with their start and end apart: 7, of which 3 were waited for; matrix products, arithmetic and copies ran while one was open for 0% of the time, Pallas kernels for 34%

profile of v3, /device:TPU:0, one launch (start us, length us, event | category | flops | bytes accessed | tf_op | source)
XLA Modules:
  0.0 24.2 jit_solution(12167002572548341389)
XLA Ops:
  0.0 3.0 %collective-permute-start.4 = (bf16[64,2048]{1,0:T(8,128)(2,1)}, bf16[64,2048]{1,0:T(8,128)(2,1)S(1)}, u32[]{:S(2)}, u32[]{:S(2)}) collective-permute-start(bf16[64,2048]{1,0:T(8,128)(2,1)} %bitcast.4), channel_id=1, source_target_pairs={{0,16},{1,17},{2,18},{3,19},{4,20},{5,21},{6,22},{7,23},{8,24},{9,... | collective-permute-start | bytes 786440 | tf_op jit(solution)/shard_map/ppermute | solution.py:667
  3.0 0.0 copy-start.6
  3.0 0.0 copy-start.7
  3.0 0.0 copy-start.8
  3.0 0.0 copy-start.9
  3.0 2.1 %pack.1 = (bf16[32,2048]{1,0:T(8,128)(2,1)}, bf16[32,2048]{1,0:T(8,128)(2,1)}, bf16[32,2048]{1,0:T(8,128)(2,1)}, bf16[8,2048]{1,0:T(8,128)(2,1)}, bf16[8,2048]{1,0:T(8,128)(2,1)}) custom-call(bf16[2,2,16,2048]{3,2,1,0:T(8,128)(2,1)} %bg_in.1, f32[16,1024]{1,0:T(8,128)} %east_in.1, f32[16,1024]{1,0:T(8,128)} %north_in.1, f32[16,1024]{1,0:T(8,128)} %diff_in.1, ...), custom_call_target="tpu_custom_call" | custom-call | tf_op jit(solution)/shard_map/pack/pallas_call | solution.py:616
  5.1 0.0 copy-start
  5.1 0.1 collective-permute-start.2
  5.2 1.6 %collective-permute-start.3 = (bf16[32,2048]{1,0:T(8,128)(2,1)}, bf16[32,2048]{1,0:T(8,128)(2,1)S(1)}, u32[]{:S(2)}, u32[]{:S(2)}) collective-permute-start(bf16[32,2048]{1,0:T(8,128)(2,1)} %get-tuple-element.45), channel_id=1, source_target_pairs={{0,1},{1,0},{2,3},{3,2},{4,5},{5,4},{6,7},{7,6},{8,9},{9,8},{10,11... | collective-permute-start | bytes 393224 | tf_op jit(solution)/shard_map/ppermute | solution.py:671
  6.8 0.5 %collective-permute-start = (bf16[8,2048]{1,0:T(8,128)(2,1)}, bf16[8,2048]{1,0:T(8,128)(2,1)S(1)}, u32[]{:S(2)}, u32[]{:S(2)}) collective-permute-start(bf16[8,2048]{1,0:T(8,128)(2,1)} %get-tuple-element.42), channel_id=1, source_target_pairs={{0,16},{1,18},{2,17},{3,20},{4,19},{5,22},{6,21},{7,24},{8,23},{9,... | collective-permute-start | bytes 98312 | tf_op jit(solution)/shard_map/ppermute | solution.py:668
  7.3 2.2 %collective-permute-start.1 = (bf16[8,2048]{1,0:T(8,128)(2,1)}, bf16[8,2048]{1,0:T(8,128)(2,1)S(1)}, u32[]{:S(2)}, u32[]{:S(2)}) collective-permute-start(bf16[8,2048]{1,0:T(8,128)(2,1)} %get-tuple-element.43), channel_id=1, source_target_pairs={{0,17},{1,16},{2,19},{3,18},{4,21},{5,20},{6,23},{7,22},{8,25},{9,... | collective-permute-start | bytes 98312 | tf_op jit(solution)/shard_map/ppermute | solution.py:670
  9.5 0.0 copy-done.2
  9.5 0.0 copy-done.3
  9.5 0.0 copy-done.4
  9.5 0.0 copy-done.5
  9.5 0.0 copy-done.6
  9.5 0.0 copy-done.7
  9.5 0.0 copy-done.8
  9.6 0.0 copy-done.9
  9.6 0.8 %weights.1 = (bf16[512,256]{1,0:T(8,128)(2,1)S(1)}, bf16[256,256]{1,0:T(8,128)(2,1)S(1)}, bf16[16,256]{1,0:T(8,128)(2,1)S(1)}, f32[256,128]{1,0:T(8,128)S(1)}, f...) custom-call(bf16[32,90]{1,0:T(8,128)(2,1)S(1)} %copy-done.4, ...), custom_call_target="tpu_custom_call" | custom-call | tf_op jit(solution)/shard_map/weights/pallas_call | solution.py:616
  10.4 0.6 %collective-permute-done.2.far = bf16[32,2048]{1,0:T(8,128)(2,1)S(1)} collective-permute-done((bf16[32,2048]{1,0:T(8,128)(2,1)}, bf16[32,2048]{1,0:T(8,128)(2,1)S(1)}, u32[]{:S(2)}, u32[]{:S(2)}) %collective-permute-start.2) | collective-permute-done | bytes 131104 | tf_op jit(solution)/shard_map/ppermute | solution.py:669
  11.0 0.0 collective-permute-done.3.near
  11.0 0.0 collective-permute-done.4.r_bg
  11.0 0.8 %collective-permute-done.dfar = bf16[8,2048]{1,0:T(8,128)(2,1)S(1)} collective-permute-done((bf16[8,2048]{1,0:T(8,128)(2,1)}, bf16[8,2048]{1,0:T(8,128)(2,1)S(1)}, u32[]{:S(2)}, u32[]{:S(2)}) %collective-permute-start) | collective-permute-done | bytes 32800 | tf_op jit(solution)/shard_map/ppermute | solution.py:668
  11.8 0.3 %collective-permute-done.1.dnear = bf16[8,2048]{1,0:T(8,128)(2,1)S(1)} collective-permute-done((bf16[8,2048]{1,0:T(8,128)(2,1)}, bf16[8,2048]{1,0:T(8,128)(2,1)S(1)}, u32[]{:S(2)}, u32[]{:S(2)}) %collective-permute-start.1) | collective-permute-done | bytes 32800 | tf_op jit(solution)/shard_map/ppermute | solution.py:670
  12.1 0.0 copy-done.1
  12.1 2.2 %collective-permute-start.5 = (bf16[32,2048]{1,0:T(8,128)(2,1)S(1)}, bf16[32,2048]{1,0:T(8,128)(2,1)S(1)}, u32[]{:S(2)}, u32[]{:S(2)}) collective-permute-start(bf16[32,2048]{1,0:T(8,128)(2,1)S(1)} %copy-done.1), channel_id=1, source_target_pairs={{0,16},{1,17},{2,18},{3,19},{4,20},{5,21},{6,22},{7,23},{8,24},{9,... | collective-permute-start | bytes 393224 | tf_op jit(solution)/shard_map/ppermute | solution.py:796
  14.2 0.0 collective-permute-start.6
  14.3 5.4 %prior.1.rest_0_ = f32[2,2,16,2048]{3,2,1,0:T(8,128)S(1)} custom-call(bf16[64,2048]{1,0:T(8,128)(2,1)S(1)} %bitcast.5, bf16[64,2048]{1,0:T(8,128)(2,1)S(1)} %collective-permute-done.4.r_bg, bf16[32,2048]{1,0:T(8,128)(2,1)S(1)} %collective-permute-done.3.near, bf16[32,2048]{1,0:T(8,128)(2,1)S(1)} %collective-permute-done.2.far, ...), custom_call_target="tpu_custom_call" | custom-call | flops 100000000 | bytes 60000000 | tf_op jit(solution)/shard_map/prior/pallas_call | solution.py:616
  19.7 0.0 collective-permute-done.6.r_e
  19.7 0.0 collective-permute-done.5.r_c
  19.7 4.5 %model.1 = f32[2,2,16,2048]{3,2,1,0:T(8,128)} custom-call(bf16[64,2048]{1,0:T(8,128)(2,1)S(1)} %bitcast.6, bf16[32,2048]{1,0:T(8,128)(2,1)S(1)} %copy-done.1, bf16[32,2048]{1,0:T(8,128)(2,1)S(1)} %collective-permute-done.5.r_c, bf16[16,2048]{1,0:T(8,128)(2,1)S(1)} %collective-permute-done.6.r_e, bf16[32,2048]{1,0:T(8,128)(2,1)S(1)} %collective-permute-done.3.near, ...), custom_call_target="tpu_custom_call" | custom-call | tf_op jit(solution)/shard_map/model/pallas_call | solution.py:616
  (7 shorter events, 0.0 us)
Async XLA Ops:
  0.0 11.0 %collective-permute-start.4 = (bf16[64,2048]{1,0:T(8,128)(2,1)}, bf16[64,2048]{1,0:T(8,128)(2,1)S(1)}, u32[]{:S(2)}, u32[]{:S(2)}) collective-permute-start(bf16[64,2048]{1,0:T(8,128)(2,1)} %bitcast.4), channel_id=1, source_target_pairs={{0,16},{1,17},{2,18},{3,19},{4,20},{5,21},{6,22},{7,23},{8,24},{9,... | collective-permute-start | bytes 786440 | tf_op jit(solution)/shard_map/ppermute | solution.py:667
  3.0 6.5 %copy-start.2 = (s32[5,8,256]{2,1,0:T(8,128)S(1)}, s32[5,8,256]{2,1,0:T(8,128)}, u32[]{:S(2)}) copy-start(s32[5,8,256]{2,1,0:T(8,128)} %constant.8.clone.refs_7_) | copy-start | bytes 122884
  3.0 6.5 %copy-start.3 = (s32[2,8,256]{2,1,0:T(8,128)S(1)}, s32[2,8,256]{2,1,0:T(8,128)}, u32[]{:S(2)}) copy-start(s32[2,8,256]{2,1,0:T(8,128)} %constant.7.clone.refs_6_) | copy-start | bytes 49156
  3.0 6.5 %copy-start.4 = (bf16[32,90]{1,0:T(8,128)(2,1)S(1)}, bf16[32,90]{1,0:T(8,128)(2,1)}, u32[]{:S(2)}) copy-start(bf16[32,90]{1,0:T(8,128)(2,1)} %refs_0_.1) | copy-start | bytes 17284
  3.0 6.5 %copy-start.5 = (bf16[32,32]{1,0:T(8,128)(2,1)S(1)}, bf16[32,32]{1,0:T(8,128)(2,1)}, u32[]{:S(2)}) copy-start(bf16[32,32]{1,0:T(8,128)(2,1)} %refs_2_.1) | copy-start | bytes 6148
  3.0 6.5 %copy-start.6 = (f32[32]{0:T(128)S(1)}, f32[32]{0:T(128)}, u32[]{:S(2)}) copy-start(f32[32]{0:T(128)} %param.17) | copy-start | bytes 388
  3.0 6.5 %copy-start.7 = (f32[32]{0:T(128)S(1)}, f32[32]{0:T(128)}, u32[]{:S(2)}) copy-start(f32[32]{0:T(128)} %param.19) | copy-start | bytes 388
  3.0 6.5 %copy-start.8 = (bf16[2,32]{1,0:T(2,128)(2,1)S(1)}, bf16[2,32]{1,0:T(2,128)(2,1)}, u32[]{:S(2)}) copy-start(bf16[2,32]{1,0:T(2,128)(2,1)} %refs_4_.1) | copy-start | bytes 388
  3.0 6.5 %copy-start.9 = (f32[2]{0:T(128)S(1)}, f32[2]{0:T(128)}, u32[]{:S(2)}) copy-start(f32[2]{0:T(128)} %param.21) | copy-start | bytes 28
  5.1 9.2 %copy-start = (bf16[2,2,16,2048]{3,2,1,0:T(8,128)(2,1)S(1)}, bf16[2,2,16,2048]{3,2,1,0:T(8,128)(2,1)}, u32[]{:S(2)}) copy-start(bf16[2,2,16,2048]{3,2,1,0:T(8,128)(2,1)} %bg_in.1) | copy-start | bytes 786436
  5.1 5.8 %collective-permute-start.2 = (bf16[32,2048]{1,0:T(8,128)(2,1)}, bf16[32,2048]{1,0:T(8,128)(2,1)S(1)}, u32[]{:S(2)}, u32[]{:S(2)}) collective-permute-start(bf16[32,2048]{1,0:T(8,128)(2,1)} %get-tuple-element.44), channel_id=1, source_target_pairs={{0,16},{1,2},{2,1},{3,4},{4,3},{5,6},{6,5},{7,8},{8,7},{9,10},{10,... | collective-permute-start | bytes 393224 | tf_op jit(solution)/shard_map/ppermute | solution.py:669
  5.2 5.8 %collective-permute-start.3 = (bf16[32,2048]{1,0:T(8,128)(2,1)}, bf16[32,2048]{1,0:T(8,128)(2,1)S(1)}, u32[]{:S(2)}, u32[]{:S(2)}) collective-permute-start(bf16[32,2048]{1,0:T(8,128)(2,1)} %get-tuple-element.45), channel_id=1, source_target_pairs={{0,1},{1,0},{2,3},{3,2},{4,5},{5,4},{6,7},{7,6},{8,9},{9,8},{10,11... | collective-permute-start | bytes 393224 | tf_op jit(solution)/shard_map/ppermute | solution.py:671
  6.8 5.0 %collective-permute-start = (bf16[8,2048]{1,0:T(8,128)(2,1)}, bf16[8,2048]{1,0:T(8,128)(2,1)S(1)}, u32[]{:S(2)}, u32[]{:S(2)}) collective-permute-start(bf16[8,2048]{1,0:T(8,128)(2,1)} %get-tuple-element.42), channel_id=1, source_target_pairs={{0,16},{1,18},{2,17},{3,20},{4,19},{5,22},{6,21},{7,24},{8,23},{9,... | collective-permute-start | bytes 98312 | tf_op jit(solution)/shard_map/ppermute | solution.py:668
  7.3 4.8 %collective-permute-start.1 = (bf16[8,2048]{1,0:T(8,128)(2,1)}, bf16[8,2048]{1,0:T(8,128)(2,1)S(1)}, u32[]{:S(2)}, u32[]{:S(2)}) collective-permute-start(bf16[8,2048]{1,0:T(8,128)(2,1)} %get-tuple-element.43), channel_id=1, source_target_pairs={{0,17},{1,16},{2,19},{3,18},{4,21},{5,20},{6,23},{7,22},{8,25},{9,... | collective-permute-start | bytes 98312 | tf_op jit(solution)/shard_map/ppermute | solution.py:670
  11.0 1.1 %copy-start.1 = (bf16[32,2048]{1,0:T(8,128)(2,1)S(1)}, bf16[32,2048]{1,0:T(8,128)(2,1)}, u32[]{:S(2)}) copy-start(bf16[32,2048]{1,0:T(8,128)(2,1)} %get-tuple-element.60.p_c) | copy-start | bytes 393220
  12.1 7.6 %collective-permute-start.5 = (bf16[32,2048]{1,0:T(8,128)(2,1)S(1)}, bf16[32,2048]{1,0:T(8,128)(2,1)S(1)}, u32[]{:S(2)}, u32[]{:S(2)}) collective-permute-start(bf16[32,2048]{1,0:T(8,128)(2,1)S(1)} %copy-done.1), channel_id=1, source_target_pairs={{0,16},{1,17},{2,18},{3,19},{4,20},{5,21},{6,22},{7,23},{8,24},{9,... | collective-permute-start | bytes 393224 | tf_op jit(solution)/shard_map/ppermute | solution.py:796
  14.2 5.4 %collective-permute-start.6 = (bf16[16,2048]{1,0:T(8,128)(2,1)S(1)}, bf16[16,2048]{1,0:T(8,128)(2,1)S(1)}, u32[]{:S(2)}, u32[]{:S(2)}) collective-permute-start(bf16[16,2048]{1,0:T(8,128)(2,1)S(1)} %relay.1), channel_id=1, source_target_pairs={{0,16},{1,17},{2,18},{3,19},{4,20},{5,21},{6,22},{7,23},{8,24},{9,... | collective-permute-start | bytes 196616 | tf_op jit(solution)/shard_map/ppermute | solution.py:797

commit v4 on v3

--- a/solution.py
+++ b/solution.py
@@ -244,10 +244,15 @@
         dfar[:, cut] = message[72:80]
 
 
-def relay_kernel(far, near, out):
-    edge = near.shape[0] - 8
-    out[0:8, :] = near[edge : edge + 8, :]
-    out[8:16, :] = far[edge : edge + 8, :]
+def hold_kernel(source, out):
+    out[...] = source[...]
+
+
+def relay_kernel(far, near, p_c, out):
+    own, edge = p_c.shape[0], near.shape[0] - 8
+    out[0:own, :] = p_c[...]
+    out[own : own + 8, :] = near[edge : edge + 8, :]
+    out[own + 8 : own + 16, :] = far[edge : edge + 8, :]
 
 
 def prep_kernel(*refs, group, channels, i_of, parity_of):
@@ -329,7 +334,7 @@
 
 
 def model_kernel(
-    p_bg, p_c, r_c, r_e, near, far, dnear, dfar, *rest,
+    p_bg, p_c, r_c, near, far, dnear, dfar, *rest,
     rows, frames, variables, tile_cols, n_sens, paired, i_of, parity_of,
 ):
     sens = None if paired else rest[0]
@@ -377,7 +382,7 @@
         kk = dot(scaled, pieces[2]).reshape(rows, 8, width) + K_MID
         rim = []
         for q in range(quarters):
-            for message in (near[16:32], far[16:32]) if source == 0 else (r_e,):
+            for message in (near[16:32], far[16:32]) if source == 0 else (r_c[2 * rows : 2 * rows + 16],):
                 for side in range(2):
                     cut = slice(side * half + q * width, side * half + (q + 1) * width)
                     rim.append(message[:, cut])
@@ -726,9 +731,9 @@
         diagonal = lax.ppermute(edge_fields(around, 1, bottom), "lat", pairs)
         received.append((message, diagonal, lax.ppermute(edge_coefs(1, bottom), "lat", pairs)))
     (near, dnear, c_near), (far, dfar, c_far) = received
-    r_e = jnp.concatenate([c_near, c_far], axis=0)
     p_bg, r_bg = background.reshape(-1, lon), around.reshape(-1, lon)
-    return p_bg, r_bg, block(0), block(1), r_e, near, far, dnear, dfar, sens
+    r_c = jnp.concatenate([block(1), c_near, c_far], axis=0)
+    return p_bg, r_bg, block(0), r_c, near, far, dnear, dfar, sens
 
 
 def shards(
@@ -749,7 +754,7 @@
         parity_of = lambda: lax.axis_index("lat") % 2
         sens = ()
     else:
-        p_bg, r_bg, p_c, r_c, r_e, near, far, dnear, dfar, sens = exchange_gathered(*arrays)
+        p_bg, r_bg, p_c, r_c, near, far, dnear, dfar, sens = exchange_gathered(*arrays)
         offsets = [[*range(frames), *range(-frames, 0), *range(frames, 2 * frames)]]
         i_of = lambda: 0
         parity_of = lambda: 0
@@ -788,13 +793,14 @@
             *small, taps, jnp.asarray(index), fetched=range(8),
         )
     if paired:
-        far, near, r_bg, *weights = lax.optimization_barrier((far, near, r_bg, *weights))
+        with jax.named_scope("own_coefs"):
+            p_c = call(hold_kernel, struct(p_c.shape, BF), [], p_c)
+        held = (far, near, r_bg, p_c, *weights)
+        far, near, r_bg, p_c, *weights = lax.optimization_barrier(held)
         with jax.named_scope("relay"):
-            edges = call(relay_kernel, struct((16, lon), BF), [], far, near)
-        pairs = swap_pairs(tiles, bands)[0]
-        dfar, dnear, late, edges = lax.optimization_barrier((dfar, dnear, p_c, edges))
-        r_c = lax.ppermute(late, ("tm", "lat"), pairs)
-        r_e = lax.ppermute(edges, ("tm", "lat"), pairs)
+            late = call(relay_kernel, struct((2 * rows + 16, lon), BF), [], far, near, p_c)
+        dfar, dnear, late = lax.optimization_barrier((dfar, dnear, late))
+        r_c = lax.ppermute(late, ("tm", "lat"), swap_pairs(tiles, bands)[0])
     *w_conv, p_conv = weights[:6]
     p_model = weights[6:]
     with jax.named_scope("prior"):
@@ -821,7 +827,7 @@
                 pltpu.VMEM((2 * frames, tall, 8, width), F32),
                 pltpu.VMEM((2, 5, ctall, 8, width), F32),
             ],
-            p_bg, p_c, r_c, r_e, near, far, dnear, dfar, *sens, prior, *p_model,
+            p_bg, p_c, r_c, near, far, dnear, dfar, *sens, prior, *p_model,
         )
 
 

time: 24.4 us -> 24.1 us (0.988)
  waiting for transfers between devices: 1.7 us -> 0.02 us
  local copies, waits for them, and re-layouts: 0.04 us -> 1.65 us
  starting transfers between devices: 9.55 us -> 9.06 us
    unnamed x20, local copies, waits for them, and re-layouts: 0.04 us -> 1.65 us
    ppermute x1, waiting for transfers between devices: 0.81 us -> 0.01 us  [exchange_pairs(): r_dfar = lax.ppermute(dfar, axes, diag_far)]
    ppermute x1, waiting for transfers between devices: 0.57 us -> 0.01 us  [exchange_pairs(): r_far = lax.ppermute(far, axes, next_chip)]
    ppermute x2 -> x1, starting transfers between devices: 2.19 us -> 1.7 us  [shards(): r_c = lax.ppermute(late, ('tm', 'lat'), swap_pairs(tiles, bands)[0])]
    ppermute x1, waiting for transfers between devices: 0.3 us -> 0.01 us  [exchange_pairs(): r_dnear = lax.ppermute(dnear, axes, diag_near)]
    pallas_call x5 -> x6, Pallas kernels: 12.8 us -> 13 us  [call(): pl.pallas_call(body, out_shape=out_shape, in_specs=[given if n in fetched...]
  transfers between devices with their start and end apart: 7 -> 6, of which waited for: 3 -> 0; matrix products, arithmetic and copies ran while one was open for 0% -> 0% of each run, Pallas kernels for 34% -> 35%
where the time goes in v4:
time: 24.1 us; the launch traced here: 23.9 us
  Pallas kernels  13 us (54%)
  starting transfers between devices  9.06 us (38%)
  local copies, waits for them, and re-layouts  1.65 us (7%)
    pallas_call x6, Pallas kernels, call(): pl.pallas_call(body, out_shape=out_shape, in_specs=[given if n in fetched...  13 us
    ppermute x1, starting transfers between devices, exchange_pairs(): r_bg = lax.ppermute(p_bg, axes, across)  2.97 us
    ppermute x1, starting transfers between devices, exchange_pairs(): r_dnear = lax.ppermute(dnear, axes, diag_near)  2.22 us
    ppermute x1, starting transfers between devices, shards(): r_c = lax.ppermute(late, ('tm', 'lat'), swap_pairs(tiles, bands)[0])  1.7 us
    unnamed x20, local copies, waits for them, and re-layouts  1.65 us
    ppermute x1, starting transfers between devices, exchange_pairs(): r_near = lax.ppermute(near, axes, on_chip)  1.59 us
    ppermute x1, starting transfers between devices, exchange_pairs(): r_dfar = lax.ppermute(dfar, axes, diag_far)  0.51 us
  transfers between devices with their start and end apart: 6, of which 0 were waited for; matrix products, arithmetic and copies ran while one was open for 0% of the time, Pallas kernels for 35%

profile of v4, /device:TPU:0, one launch (start us, length us, event | category | flops | bytes accessed | tf_op | source)
XLA Modules:
  0.0 23.9 jit_solution(15839282050750211057)
XLA Ops:
  0.0 3.0 %collective-permute-start.2 = (bf16[64,2048]{1,0:T(8,128)(2,1)}, bf16[64,2048]{1,0:T(8,128)(2,1)S(1)}, u32[]{:S(2)}, u32[]{:S(2)}) collective-permute-start(bf16[64,2048]{1,0:T(8,128)(2,1)} %bitcast.4), channel_id=1, source_target_pairs={{0,16},{1,17},{2,18},{3,19},{4,20},{5,21},{6,22},{7,23},{8,24},{9,... | collective-permute-start | bytes 786440 | tf_op jit(solution)/shard_map/ppermute | solution.py:672
  3.0 2.0 %pack.1 = (bf16[32,2048]{1,0:T(8,128)(2,1)}, bf16[32,2048]{1,0:T(8,128)(2,1)}, bf16[32,2048]{1,0:T(8,128)(2,1)}, bf16[8,2048]{1,0:T(8,128)(2,1)}, bf16[8,2048]{1,0:T(8,128)(2,1)}) custom-call(bf16[2,2,16,2048]{3,2,1,0:T(8,128)(2,1)} %bg_in.1, f32[16,1024]{1,0:T(8,128)} %east_in.1, f32[16,1024]{1,0:T(8,128)} %north_in.1, f32[16,1024]{1,0:T(8,128)} %diff_in.1, ...), custom_call_target="tpu_custom_call" | custom-call | tf_op jit(solution)/shard_map/pack/pallas_call | solution.py:621
  5.0 0.1 collective-permute-start
  5.0 1.6 %collective-permute-start.1 = (bf16[32,2048]{1,0:T(8,128)(2,1)}, bf16[32,2048]{1,0:T(8,128)(2,1)S(1)}, u32[]{:S(2)}, u32[]{:S(2)}) collective-permute-start(bf16[32,2048]{1,0:T(8,128)(2,1)} %get-tuple-element.42), channel_id=1, source_target_pairs={{0,1},{1,0},{2,3},{3,2},{4,5},{5,4},{6,7},{7,6},{8,9},{9,8},{10,11... | collective-permute-start | bytes 393224 | tf_op jit(solution)/shard_map/ppermute | solution.py:676
  6.6 0.5 %collective-permute-start.3 = (bf16[8,2048]{1,0:T(8,128)(2,1)}, bf16[8,2048]{1,0:T(8,128)(2,1)S(1)}, u32[]{:S(2)}, u32[]{:S(2)}) collective-permute-start(bf16[8,2048]{1,0:T(8,128)(2,1)} %get-tuple-element.57), channel_id=1, source_target_pairs={{0,16},{1,18},{2,17},{3,20},{4,19},{5,22},{6,21},{7,24},{8,23},{9,... | collective-permute-start | bytes 98312 | tf_op jit(solution)/shard_map/ppermute | solution.py:673
  7.1 2.2 %collective-permute-start.4 = (bf16[8,2048]{1,0:T(8,128)(2,1)}, bf16[8,2048]{1,0:T(8,128)(2,1)S(1)}, u32[]{:S(2)}, u32[]{:S(2)}) collective-permute-start(bf16[8,2048]{1,0:T(8,128)(2,1)} %get-tuple-element.58), channel_id=1, source_target_pairs={{0,17},{1,16},{2,19},{3,18},{4,21},{5,20},{6,23},{7,22},{8,25},{9,... | collective-permute-start | bytes 98312 | tf_op jit(solution)/shard_map/ppermute | solution.py:675
  9.4 0.0 copy-start.1
  9.4 0.9 %copy-done.1 = bf16[32,2048]{1,0:T(8,128)(2,1)S(1)} copy-done((bf16[32,2048]{1,0:T(8,128)(2,1)S(1)}, bf16[32,2048]{1,0:T(8,128)(2,1)}, u32[]{:S(2)}) %copy-start.1) | copy-done | bytes 131096
  10.3 0.0 copy-start.9
  10.3 0.0 copy-start.6
  10.3 0.0 copy-start.7
  10.3 0.0 copy-start.8
  10.3 0.7 %copy-done.2 = s32[5,8,256]{2,1,0:T(8,128)S(1)} copy-done((s32[5,8,256]{2,1,0:T(8,128)S(1)}, s32[5,8,256]{2,1,0:T(8,128)}, u32[]{:S(2)}) %copy-start.2) | copy-done | bytes 40984
  11.0 0.0 copy-done.3
  11.0 0.0 copy-done.4
  11.1 0.0 copy-done.5
  11.1 0.0 copy-done.9
  11.1 0.0 copy-done.6
  11.1 0.0 copy-done.7
  11.1 0.0 copy-done.8
  11.1 0.8 %weights.1 = (bf16[512,256]{1,0:T(8,128)(2,1)S(1)}, bf16[256,256]{1,0:T(8,128)(2,1)S(1)}, bf16[16,256]{1,0:T(8,128)(2,1)S(1)}, f32[256,128]{1,0:T(8,128)S(1)}, f...) custom-call(bf16[32,90]{1,0:T(8,128)(2,1)S(1)} %copy-done.4, ...), custom_call_target="tpu_custom_call" | custom-call | tf_op jit(solution)/shard_map/weights/pallas_call | solution.py:621
  11.9 0.0 collective-permute-done.far
  11.9 0.0 collective-permute-done.1.near
  11.9 0.0 collective-permute-done.2.r_bg
  11.9 0.0 copy-start
  12.0 0.0 collective-permute-done.3.dfar
  12.0 0.0 collective-permute-done.4.dnear
  12.0 1.7 %collective-permute-start.5 = (bf16[48,2048]{1,0:T(8,128)(2,1)S(1)}, bf16[48,2048]{1,0:T(8,128)(2,1)S(1)}, u32[]{:S(2)}, u32[]{:S(2)}) collective-permute-start(bf16[48,2048]{1,0:T(8,128)(2,1)S(1)} %relay.1), channel_id=1, source_target_pairs={{0,16},{1,17},{2,18},{3,19},{4,20},{5,21},{6,22},{7,23},{8,24},{9,... | collective-permute-start | bytes 589832 | tf_op jit(solution)/shard_map/ppermute | solution.py:803
  13.7 0.0 copy-done
  13.7 5.6 %prior.1.rest_0_ = f32[2,2,16,2048]{3,2,1,0:T(8,128)S(1)} custom-call(bf16[64,2048]{1,0:T(8,128)(2,1)S(1)} %bitcast.5, bf16[64,2048]{1,0:T(8,128)(2,1)S(1)} %collective-permute-done.2.r_bg, bf16[32,2048]{1,0:T(8,128)(2,1)S(1)} %collective-permute-done.1.near, bf16[32,2048]{1,0:T(8,128)(2,1)S(1)} %collective-permute-done.far, ...), custom_call_target="tpu_custom_call" | custom-call | flops 100000000 | bytes 60000000 | tf_op jit(solution)/shard_map/prior/pallas_call | solution.py:621
  19.3 0.0 collective-permute-done.5.r_c
  19.3 4.5 %model.1 = f32[2,2,16,2048]{3,2,1,0:T(8,128)} custom-call(bf16[64,2048]{1,0:T(8,128)(2,1)S(1)} %bitcast.6, bf16[32,2048]{1,0:T(8,128)(2,1)S(1)} %own_coefs.1.p_c, bf16[48,2048]{1,0:T(8,128)(2,1)S(1)} %collective-permute-done.5.r_c, bf16[32,2048]{1,0:T(8,128)(2,1)S(1)} %collective-permute-done.1.near, bf16[32,2048]{1,0:T(8,128)(2,1)S(1)} %collective-permute-done.far, ...), custom_call_target="tpu_custom_call" | custom-call | tf_op jit(solution)/shard_map/model/pallas_call | solution.py:621
  (6 shorter events, 0.0 us)
Async XLA Ops:
  0.0 11.9 %collective-permute-start.2 = (bf16[64,2048]{1,0:T(8,128)(2,1)}, bf16[64,2048]{1,0:T(8,128)(2,1)S(1)}, u32[]{:S(2)}, u32[]{:S(2)}) collective-permute-start(bf16[64,2048]{1,0:T(8,128)(2,1)} %bitcast.4), channel_id=1, source_target_pairs={{0,16},{1,17},{2,18},{3,19},{4,20},{5,21},{6,22},{7,23},{8,24},{9,... | collective-permute-start | bytes 786440 | tf_op jit(solution)/shard_map/ppermute | solution.py:672
  5.0 6.9 %collective-permute-start = (bf16[32,2048]{1,0:T(8,128)(2,1)}, bf16[32,2048]{1,0:T(8,128)(2,1)S(1)}, u32[]{:S(2)}, u32[]{:S(2)}) collective-permute-start(bf16[32,2048]{1,0:T(8,128)(2,1)} %get-tuple-element.41), channel_id=1, source_target_pairs={{0,16},{1,2},{2,1},{3,4},{4,3},{5,6},{6,5},{7,8},{8,7},{9,10},{10,... | collective-permute-start | bytes 393224 | tf_op jit(solution)/shard_map/ppermute | solution.py:674
  5.0 6.9 %collective-permute-start.1 = (bf16[32,2048]{1,0:T(8,128)(2,1)}, bf16[32,2048]{1,0:T(8,128)(2,1)S(1)}, u32[]{:S(2)}, u32[]{:S(2)}) collective-permute-start(bf16[32,2048]{1,0:T(8,128)(2,1)} %get-tuple-element.42), channel_id=1, source_target_pairs={{0,1},{1,0},{2,3},{3,2},{4,5},{5,4},{6,7},{7,6},{8,9},{9,8},{10,11... | collective-permute-start | bytes 393224 | tf_op jit(solution)/shard_map/ppermute | solution.py:676
  6.6 5.3 %collective-permute-start.3 = (bf16[8,2048]{1,0:T(8,128)(2,1)}, bf16[8,2048]{1,0:T(8,128)(2,1)S(1)}, u32[]{:S(2)}, u32[]{:S(2)}) collective-permute-start(bf16[8,2048]{1,0:T(8,128)(2,1)} %get-tuple-element.57), channel_id=1, source_target_pairs={{0,16},{1,18},{2,17},{3,20},{4,19},{5,22},{6,21},{7,24},{8,23},{9,... | collective-permute-start | bytes 98312 | tf_op jit(solution)/shard_map/ppermute | solution.py:673
  7.1 4.8 %collective-permute-start.4 = (bf16[8,2048]{1,0:T(8,128)(2,1)}, bf16[8,2048]{1,0:T(8,128)(2,1)S(1)}, u32[]{:S(2)}, u32[]{:S(2)}) collective-permute-start(bf16[8,2048]{1,0:T(8,128)(2,1)} %get-tuple-element.58), channel_id=1, source_target_pairs={{0,17},{1,16},{2,19},{3,18},{4,21},{5,20},{6,23},{7,22},{8,25},{9,... | collective-permute-start | bytes 98312 | tf_op jit(solution)/shard_map/ppermute | solution.py:675
  9.4 0.9 %copy-start.1 = (bf16[32,2048]{1,0:T(8,128)(2,1)S(1)}, bf16[32,2048]{1,0:T(8,128)(2,1)}, u32[]{:S(2)}) copy-start(bf16[32,2048]{1,0:T(8,128)(2,1)} %get-tuple-element.43.source) | copy-start | bytes 393220
  10.3 0.8 %copy-start.2 = (s32[5,8,256]{2,1,0:T(8,128)S(1)}, s32[5,8,256]{2,1,0:T(8,128)}, u32[]{:S(2)}) copy-start(s32[5,8,256]{2,1,0:T(8,128)} %constant.8.clone.refs_7_) | copy-start | bytes 122884
  10.3 0.8 %copy-start.3 = (s32[2,8,256]{2,1,0:T(8,128)S(1)}, s32[2,8,256]{2,1,0:T(8,128)}, u32[]{:S(2)}) copy-start(s32[2,8,256]{2,1,0:T(8,128)} %constant.7.clone.refs_6_) | copy-start | bytes 49156
  10.3 0.8 %copy-start.4 = (bf16[32,90]{1,0:T(8,128)(2,1)S(1)}, bf16[32,90]{1,0:T(8,128)(2,1)}, u32[]{:S(2)}) copy-start(bf16[32,90]{1,0:T(8,128)(2,1)} %refs_0_.1) | copy-start | bytes 17284
  10.3 0.8 %copy-start.5 = (bf16[32,32]{1,0:T(8,128)(2,1)S(1)}, bf16[32,32]{1,0:T(8,128)(2,1)}, u32[]{:S(2)}) copy-start(bf16[32,32]{1,0:T(8,128)(2,1)} %refs_2_.1) | copy-start | bytes 6148
  10.3 0.8 %copy-start.9 = (f32[2]{0:T(128)S(1)}, f32[2]{0:T(128)}, u32[]{:S(2)}) copy-start(f32[2]{0:T(128)} %param.21) | copy-start | bytes 28
  10.3 0.8 %copy-start.6 = (f32[32]{0:T(128)S(1)}, f32[32]{0:T(128)}, u32[]{:S(2)}) copy-start(f32[32]{0:T(128)} %param.17) | copy-start | bytes 388
  10.3 0.8 %copy-start.7 = (f32[32]{0:T(128)S(1)}, f32[32]{0:T(128)}, u32[]{:S(2)}) copy-start(f32[32]{0:T(128)} %param.19) | copy-start | bytes 388
  10.3 0.7 %copy-start.8 = (bf16[2,32]{1,0:T(2,128)(2,1)S(1)}, bf16[2,32]{1,0:T(2,128)(2,1)}, u32[]{:S(2)}) copy-start(bf16[2,32]{1,0:T(2,128)(2,1)} %refs_4_.1) | copy-start | bytes 388
  11.9 1.8 %copy-start = (bf16[2,2,16,2048]{3,2,1,0:T(8,128)(2,1)S(1)}, bf16[2,2,16,2048]{3,2,1,0:T(8,128)(2,1)}, u32[]{:S(2)}) copy-start(bf16[2,2,16,2048]{3,2,1,0:T(8,128)(2,1)} %bg_in.1) | copy-start | bytes 786436
  12.0 7.3 %collective-permute-start.5 = (bf16[48,2048]{1,0:T(8,128)(2,1)S(1)}, bf16[48,2048]{1,0:T(8,128)(2,1)S(1)}, u32[]{:S(2)}, u32[]{:S(2)}) collective-permute-start(bf16[48,2048]{1,0:T(8,128)(2,1)S(1)} %relay.1), channel_id=1, source_target_pairs={{0,16},{1,17},{2,18},{3,19},{4,20},{5,21},{6,22},{7,23},{8,24},{9,... | collective-permute-start | bytes 589832 | tf_op jit(solution)/shard_map/ppermute | solution.py:803

commit v5 on v4

--- a/solution.py
+++ b/solution.py
@@ -799,7 +799,7 @@
         far, near, r_bg, p_c, *weights = lax.optimization_barrier(held)
         with jax.named_scope("relay"):
             late = call(relay_kernel, struct((2 * rows + 16, lon), BF), [], far, near, p_c)
-        dfar, dnear, late = lax.optimization_barrier((dfar, dnear, late))
+        dnear, dfar, late = lax.optimization_barrier((dnear, dfar, late))
         r_c = lax.ppermute(late, ("tm", "lat"), swap_pairs(tiles, bands)[0])
     *w_conv, p_conv = weights[:6]
     p_model = weights[6:]

time: 24.1 us -> 24.4 us (1.012)
  waiting for transfers between devices: 0.02 us -> 1.45 us
  starting transfers between devices: 9.06 us -> 8.01 us
    ppermute x1, starting transfers between devices: 2.22 us -> 0.55 us  [exchange_pairs(): r_dnear = lax.ppermute(dnear, axes, diag_near)]
    ppermute x1, waiting for transfers between devices: 0.01 us -> 1.01 us  [exchange_pairs(): r_dfar = lax.ppermute(dfar, axes, diag_far)]
    ppermute x1, starting transfers between devices: 0.51 us -> 1.08 us  [exchange_pairs(): r_dfar = lax.ppermute(dfar, axes, diag_far)]
    ppermute x1, waiting for transfers between devices: 0.01 us -> 0.43 us  [exchange_pairs(): r_far = lax.ppermute(far, axes, next_chip)]
  transfers between devices with their start and end apart: 6 -> 6, of which waited for: 0 -> 2; matrix products, arithmetic and copies ran while one was open for 0% -> 0% of each run, Pallas kernels for 35% -> 35%
where the time goes in v5:
time: 24.4 us; the launch traced here: 24.2 us
  Pallas kernels  13 us (53%)
  starting transfers between devices  8.01 us (33%)
  local copies, waits for them, and re-layouts  1.65 us (7%)
  waiting for transfers between devices  1.45 us (6%)
    pallas_call x6, Pallas kernels, call(): pl.pallas_call(body, out_shape=out_shape, in_specs=[given if n in fetched...  13 us
    ppermute x1, starting transfers between devices, exchange_pairs(): r_bg = lax.ppermute(p_bg, axes, across)  2.97 us
    ppermute x1, starting transfers between devices, shards(): r_c = lax.ppermute(late, ('tm', 'lat'), swap_pairs(tiles, bands)[0])  1.74 us
    unnamed x20, local copies, waits for them, and re-layouts  1.65 us
    ppermute x1, starting transfers between devices, exchange_pairs(): r_near = lax.ppermute(near, axes, on_chip)  1.59 us
    ppermute x1, starting transfers between devices, exchange_pairs(): r_dfar = lax.ppermute(dfar, axes, diag_far)  1.08 us
    ppermute x1, waiting for transfers between devices, exchange_pairs(): r_dfar = lax.ppermute(dfar, axes, diag_far)  1.01 us
    ppermute x1, starting transfers between devices, exchange_pairs(): r_dnear = lax.ppermute(dnear, axes, diag_near)  0.55 us
  transfers between devices with their start and end apart: 6, of which 2 were waited for; matrix products, arithmetic and copies ran while one was open for 0% of the time, Pallas kernels for 35%

profile of v5, /device:TPU:0, one launch (start us, length us, event | category | flops | bytes accessed | tf_op | source)
XLA Modules:
  0.0 24.2 jit_solution(7853121371563291165)
XLA Ops:
  0.0 3.0 %collective-permute-start.2 = (bf16[64,2048]{1,0:T(8,128)(2,1)}, bf16[64,2048]{1,0:T(8,128)(2,1)S(1)}, u32[]{:S(2)}, u32[]{:S(2)}) collective-permute-start(bf16[64,2048]{1,0:T(8,128)(2,1)} %bitcast.4), channel_id=1, source_target_pairs={{0,16},{1,17},{2,18},{3,19},{4,20},{5,21},{6,22},{7,23},{8,24},{9,... | collective-permute-start | bytes 786440 | tf_op jit(solution)/shard_map/ppermute | solution.py:672
  3.0 2.0 %pack.1 = (bf16[32,2048]{1,0:T(8,128)(2,1)}, bf16[32,2048]{1,0:T(8,128)(2,1)}, bf16[32,2048]{1,0:T(8,128)(2,1)}, bf16[8,2048]{1,0:T(8,128)(2,1)}, bf16[8,2048]{1,0:T(8,128)(2,1)}) custom-call(bf16[2,2,16,2048]{3,2,1,0:T(8,128)(2,1)} %bg_in.1, f32[16,1024]{1,0:T(8,128)} %east_in.1, f32[16,1024]{1,0:T(8,128)} %north_in.1, f32[16,1024]{1,0:T(8,128)} %diff_in.1, ...), custom_call_target="tpu_custom_call" | custom-call | tf_op jit(solution)/shard_map/pack/pallas_call | solution.py:621
  5.0 0.1 collective-permute-start
  5.0 1.6 %collective-permute-start.1 = (bf16[32,2048]{1,0:T(8,128)(2,1)}, bf16[32,2048]{1,0:T(8,128)(2,1)S(1)}, u32[]{:S(2)}, u32[]{:S(2)}) collective-permute-start(bf16[32,2048]{1,0:T(8,128)(2,1)} %get-tuple-element.42), channel_id=1, source_target_pairs={{0,1},{1,0},{2,3},{3,2},{4,5},{5,4},{6,7},{7,6},{8,9},{9,8},{10,11... | collective-permute-start | bytes 393224 | tf_op jit(solution)/shard_map/ppermute | solution.py:676
  6.6 0.5 %collective-permute-start.3 = (bf16[8,2048]{1,0:T(8,128)(2,1)}, bf16[8,2048]{1,0:T(8,128)(2,1)S(1)}, u32[]{:S(2)}, u32[]{:S(2)}) collective-permute-start(bf16[8,2048]{1,0:T(8,128)(2,1)} %get-tuple-element.57), channel_id=1, source_target_pairs={{0,17},{1,16},{2,19},{3,18},{4,21},{5,20},{6,23},{7,22},{8,25},{9,... | collective-permute-start | bytes 98312 | tf_op jit(solution)/shard_map/ppermute | solution.py:675
  7.2 1.1 %collective-permute-start.4 = (bf16[8,2048]{1,0:T(8,128)(2,1)}, bf16[8,2048]{1,0:T(8,128)(2,1)S(1)}, u32[]{:S(2)}, u32[]{:S(2)}) collective-permute-start(bf16[8,2048]{1,0:T(8,128)(2,1)} %get-tuple-element.58), channel_id=1, source_target_pairs={{0,16},{1,18},{2,17},{3,20},{4,19},{5,22},{6,21},{7,24},{8,23},{9,... | collective-permute-start | bytes 98312 | tf_op jit(solution)/shard_map/ppermute | solution.py:673
  8.3 0.9 %copy-done.1 = bf16[32,2048]{1,0:T(8,128)(2,1)S(1)} copy-done((bf16[32,2048]{1,0:T(8,128)(2,1)S(1)}, bf16[32,2048]{1,0:T(8,128)(2,1)}, u32[]{:S(2)}) %copy-start.1) | copy-done | bytes 131096
  9.2 0.0 copy-start.2
  9.2 0.0 copy-start.3
  9.2 0.0 copy-start.9
  9.2 0.0 copy-start.6
  9.2 0.0 copy-start.7
  9.2 0.0 copy-start.8
  9.2 0.7 %copy-done.2 = s32[5,8,256]{2,1,0:T(8,128)S(1)} copy-done((s32[5,8,256]{2,1,0:T(8,128)S(1)}, s32[5,8,256]{2,1,0:T(8,128)}, u32[]{:S(2)}) %copy-start.2) | copy-done | bytes 40984
  9.9 0.0 copy-done.3
  10.0 0.0 copy-done.4
  10.0 0.0 copy-done.5
  10.0 0.0 copy-done.9
  10.0 0.0 copy-done.6
  10.0 0.0 copy-done.7
  10.0 0.0 copy-done.8
  10.0 0.8 %weights.1 = (bf16[512,256]{1,0:T(8,128)(2,1)S(1)}, bf16[256,256]{1,0:T(8,128)(2,1)S(1)}, bf16[16,256]{1,0:T(8,128)(2,1)S(1)}, f32[256,128]{1,0:T(8,128)S(1)}, f...) custom-call(bf16[32,90]{1,0:T(8,128)(2,1)S(1)} %copy-done.4, ...), custom_call_target="tpu_custom_call" | custom-call | tf_op jit(solution)/shard_map/weights/pallas_call | solution.py:621
  10.8 0.4 %collective-permute-done.far = bf16[32,2048]{1,0:T(8,128)(2,1)S(1)} collective-permute-done((bf16[32,2048]{1,0:T(8,128)(2,1)}, bf16[32,2048]{1,0:T(8,128)(2,1)S(1)}, u32[]{:S(2)}, u32[]{:S(2)}) %collective-permute-start) | collective-permute-done | bytes 131104 | tf_op jit(solution)/shard_map/ppermute | solution.py:674
  11.2 0.0 collective-permute-done.1.near
  11.2 0.0 collective-permute-done.2.r_bg
  11.3 0.0 collective-permute-done.3.dnear
  11.3 1.0 %collective-permute-done.4.dfar = bf16[8,2048]{1,0:T(8,128)(2,1)S(1)} collective-permute-done((bf16[8,2048]{1,0:T(8,128)(2,1)}, bf16[8,2048]{1,0:T(8,128)(2,1)S(1)}, u32[]{:S(2)}, u32[]{:S(2)}) %collective-permute-start.4) | collective-permute-done | bytes 32800 | tf_op jit(solution)/shard_map/ppermute | solution.py:673
  12.3 1.7 %collective-permute-start.5 = (bf16[48,2048]{1,0:T(8,128)(2,1)S(1)}, bf16[48,2048]{1,0:T(8,128)(2,1)S(1)}, u32[]{:S(2)}, u32[]{:S(2)}) collective-permute-start(bf16[48,2048]{1,0:T(8,128)(2,1)S(1)} %relay.1), channel_id=1, source_target_pairs={{0,16},{1,17},{2,18},{3,19},{4,20},{5,21},{6,22},{7,23},{8,24},{9,... | collective-permute-start | bytes 589832 | tf_op jit(solution)/shard_map/ppermute | solution.py:803
  14.0 0.0 copy-done
  14.0 5.6 %prior.1.rest_0_ = f32[2,2,16,2048]{3,2,1,0:T(8,128)S(1)} custom-call(bf16[64,2048]{1,0:T(8,128)(2,1)S(1)} %bitcast.5, bf16[64,2048]{1,0:T(8,128)(2,1)S(1)} %collective-permute-done.2.r_bg, bf16[32,2048]{1,0:T(8,128)(2,1)S(1)} %collective-permute-done.1.near, bf16[32,2048]{1,0:T(8,128)(2,1)S(1)} %collective-permute-done.far, ...), custom_call_target="tpu_custom_call" | custom-call | flops 100000000 | bytes 60000000 | tf_op jit(solution)/shard_map/prior/pallas_call | solution.py:621
  19.7 0.0 collective-permute-done.5.r_c
  19.7 4.5 %model.1 = f32[2,2,16,2048]{3,2,1,0:T(8,128)} custom-call(bf16[64,2048]{1,0:T(8,128)(2,1)S(1)} %bitcast.6, bf16[32,2048]{1,0:T(8,128)(2,1)S(1)} %own_coefs.1.p_c, bf16[48,2048]{1,0:T(8,128)(2,1)S(1)} %collective-permute-done.5.r_c, bf16[32,2048]{1,0:T(8,128)(2,1)S(1)} %collective-permute-done.1.near, bf16[32,2048]{1,0:T(8,128)(2,1)S(1)} %collective-permute-done.far, ...), custom_call_target="tpu_custom_call" | custom-call | tf_op jit(solution)/shard_map/model/pallas_call | solution.py:621
  (6 shorter events, 0.0 us)
Async XLA Ops:
  0.0 11.2 %collective-permute-start.2 = (bf16[64,2048]{1,0:T(8,128)(2,1)}, bf16[64,2048]{1,0:T(8,128)(2,1)S(1)}, u32[]{:S(2)}, u32[]{:S(2)}) collective-permute-start(bf16[64,2048]{1,0:T(8,128)(2,1)} %bitcast.4), channel_id=1, source_target_pairs={{0,16},{1,17},{2,18},{3,19},{4,20},{5,21},{6,22},{7,23},{8,24},{9,... | collective-permute-start | bytes 786440 | tf_op jit(solution)/shard_map/ppermute | solution.py:672
  5.0 6.3 %collective-permute-start = (bf16[32,2048]{1,0:T(8,128)(2,1)}, bf16[32,2048]{1,0:T(8,128)(2,1)S(1)}, u32[]{:S(2)}, u32[]{:S(2)}) collective-permute-start(bf16[32,2048]{1,0:T(8,128)(2,1)} %get-tuple-element.41), channel_id=1, source_target_pairs={{0,16},{1,2},{2,1},{3,4},{4,3},{5,6},{6,5},{7,8},{8,7},{9,10},{10,... | collective-permute-start | bytes 393224 | tf_op jit(solution)/shard_map/ppermute | solution.py:674
  5.0 6.2 %collective-permute-start.1 = (bf16[32,2048]{1,0:T(8,128)(2,1)}, bf16[32,2048]{1,0:T(8,128)(2,1)S(1)}, u32[]{:S(2)}, u32[]{:S(2)}) collective-permute-start(bf16[32,2048]{1,0:T(8,128)(2,1)} %get-tuple-element.42), channel_id=1, source_target_pairs={{0,1},{1,0},{2,3},{3,2},{4,5},{5,4},{6,7},{7,6},{8,9},{9,8},{10,11... | collective-permute-start | bytes 393224 | tf_op jit(solution)/shard_map/ppermute | solution.py:676
  6.6 4.6 %collective-permute-start.3 = (bf16[8,2048]{1,0:T(8,128)(2,1)}, bf16[8,2048]{1,0:T(8,128)(2,1)S(1)}, u32[]{:S(2)}, u32[]{:S(2)}) collective-permute-start(bf16[8,2048]{1,0:T(8,128)(2,1)} %get-tuple-element.57), channel_id=1, source_target_pairs={{0,17},{1,16},{2,19},{3,18},{4,21},{5,20},{6,23},{7,22},{8,25},{9,... | collective-permute-start | bytes 98312 | tf_op jit(solution)/shard_map/ppermute | solution.py:675
  7.2 5.1 %collective-permute-start.4 = (bf16[8,2048]{1,0:T(8,128)(2,1)}, bf16[8,2048]{1,0:T(8,128)(2,1)S(1)}, u32[]{:S(2)}, u32[]{:S(2)}) collective-permute-start(bf16[8,2048]{1,0:T(8,128)(2,1)} %get-tuple-element.58), channel_id=1, source_target_pairs={{0,16},{1,18},{2,17},{3,20},{4,19},{5,22},{6,21},{7,24},{8,23},{9,... | collective-permute-start | bytes 98312 | tf_op jit(solution)/shard_map/ppermute | solution.py:673
  8.3 0.9 %copy-start.1 = (bf16[32,2048]{1,0:T(8,128)(2,1)S(1)}, bf16[32,2048]{1,0:T(8,128)(2,1)}, u32[]{:S(2)}) copy-start(bf16[32,2048]{1,0:T(8,128)(2,1)} %get-tuple-element.43.source) | copy-start | bytes 393220
  9.2 0.8 %copy-start.2 = (s32[5,8,256]{2,1,0:T(8,128)S(1)}, s32[5,8,256]{2,1,0:T(8,128)}, u32[]{:S(2)}) copy-start(s32[5,8,256]{2,1,0:T(8,128)} %constant.8.clone.refs_7_) | copy-start | bytes 122884
  9.2 0.8 %copy-start.3 = (s32[2,8,256]{2,1,0:T(8,128)S(1)}, s32[2,8,256]{2,1,0:T(8,128)}, u32[]{:S(2)}) copy-start(s32[2,8,256]{2,1,0:T(8,128)} %constant.7.clone.refs_6_) | copy-start | bytes 49156
  9.2 0.8 %copy-start.4 = (bf16[32,90]{1,0:T(8,128)(2,1)S(1)}, bf16[32,90]{1,0:T(8,128)(2,1)}, u32[]{:S(2)}) copy-start(bf16[32,90]{1,0:T(8,128)(2,1)} %refs_0_.1) | copy-start | bytes 17284
  9.2 0.8 %copy-start.5 = (bf16[32,32]{1,0:T(8,128)(2,1)S(1)}, bf16[32,32]{1,0:T(8,128)(2,1)}, u32[]{:S(2)}) copy-start(bf16[32,32]{1,0:T(8,128)(2,1)} %refs_2_.1) | copy-start | bytes 6148
  9.2 0.8 %copy-start.9 = (f32[2]{0:T(128)S(1)}, f32[2]{0:T(128)}, u32[]{:S(2)}) copy-start(f32[2]{0:T(128)} %param.21) | copy-start | bytes 28
  9.2 0.8 %copy-start.6 = (f32[32]{0:T(128)S(1)}, f32[32]{0:T(128)}, u32[]{:S(2)}) copy-start(f32[32]{0:T(128)} %param.17) | copy-start | bytes 388
  9.2 0.8 %copy-start.7 = (f32[32]{0:T(128)S(1)}, f32[32]{0:T(128)}, u32[]{:S(2)}) copy-start(f32[32]{0:T(128)} %param.19) | copy-start | bytes 388
  9.2 0.7 %copy-start.8 = (bf16[2,32]{1,0:T(2,128)(2,1)S(1)}, bf16[2,32]{1,0:T(2,128)(2,1)}, u32[]{:S(2)}) copy-start(bf16[2,32]{1,0:T(2,128)(2,1)} %refs_4_.1) | copy-start | bytes 388
  11.2 2.8 %copy-start = (bf16[2,2,16,2048]{3,2,1,0:T(8,128)(2,1)S(1)}, bf16[2,2,16,2048]{3,2,1,0:T(8,128)(2,1)}, u32[]{:S(2)}) copy-start(bf16[2,2,16,2048]{3,2,1,0:T(8,128)(2,1)} %bg_in.1) | copy-start | bytes 786436
  12.3 7.4 %collective-permute-start.5 = (bf16[48,2048]{1,0:T(8,128)(2,1)S(1)}, bf16[48,2048]{1,0:T(8,128)(2,1)S(1)}, u32[]{:S(2)}, u32[]{:S(2)}) collective-permute-start(bf16[48,2048]{1,0:T(8,128)(2,1)S(1)} %relay.1), channel_id=1, source_target_pairs={{0,16},{1,17},{2,18},{3,19},{4,20},{5,21},{6,22},{7,23},{8,24},{9,... | collective-permute-start | bytes 589832 | tf_op jit(solution)/shard_map/ppermute | solution.py:803
